TPU v7x, 512 devices: a whole 4x8x8 slice. The times are simulated.
512 devices in a mesh: blk: 16 (over x, z_hi), shard: 32 (over y, z_lo, core).
Axes of the slice: x: 4, y: 8, z: 8 (z_hi: 4, z_lo: 2; z = z_hi * 2 + z_lo), core: 2. Of those that a mesh axis runs over, the one named last changes fastest.
Arguments:
- queries: bfloat16 [2048, 1280], P('blk'), may hold values from -56 to 56
- database: bfloat16 [393216, 1280], P(('blk', 'shard')), may hold values from -56 to 56
- pair_tiles: int32 [512, 24, 2], P(('blk', 'shard')), may hold values from 0 to 15, as said below
- pair_lengths: int32 [512, 24, 2], P(('blk', 'shard')), may hold values from 8 to 128
- live_pairs: int32 [512], P(('blk', 'shard')), may hold values from 1 to 24, as said below
Outputs:
- aligned: bfloat16 [2048, 1280], P(('blk', 'shard'))
Inputs may be any that keep to these rules, and one draw needn't show every extreme that they name: `pair_tiles`: entry [e, p, 0] is a query tile in 0 to 15 and entry [e, p, 1] a tile of device e in 0 to 5; in each device's used slots the query tiles never fall. `live_pairs`: some device uses all 24 slots in every draw.
All inputs are finite; a program needn't handle non-finite values.
Results may differ from a plain program's by a relative error of at most 0.0055.
Values may be sent and summed in bfloat16 or wider, within the bound.
No kernel may reach another device: no remote copies, remote signals or barrier semaphores. Data moves between devices by JAX's collectives and lax.ppermute only.
A program may use at most 128 MiB of HBM per device.

v0:
```python
import jax
import jax.numpy as jnp
from jax import lax
from jax.sharding import PartitionSpec as P


def shifted(block, axis, distance):
    devices = range(lax.axis_size(axis))
    route = [((i - distance) % len(devices), i) for i in devices]
    return lax.ppermute(block, axis, route)


def pair_term(panel, key_tile, lengths, scale):
    tile = panel.shape[0]
    scores = (
        lax.dot_general(
            panel, key_tile, (((1,), (1,)), ((), ())), preferred_element_type=jnp.float32
        )
        * scale
    )
    index = jnp.arange(tile)
    valid = (index[:, None] < lengths[0]) & (index[None, :] < lengths[1])
    masked = jnp.where(valid, scores, -1e30)
    row_max = jnp.max(masked, axis=1, keepdims=True)
    row_lse = row_max + jnp.log(jnp.sum(jnp.exp(masked - row_max), axis=1, keepdims=True))
    col_max = jnp.max(masked, axis=0, keepdims=True)
    col_lse = col_max + jnp.log(jnp.sum(jnp.exp(masked - col_max), axis=0, keepdims=True))
    weight = jnp.where(valid, jnp.exp(scores - 0.5 * (row_lse + col_lse)), 0.0).astype(jnp.bfloat16)
    return jnp.dot(weight, key_tile, preferred_element_type=jnp.float32)


def on_device(queries, database, pair_tiles, pair_lengths, live_pairs):
    tile, width = queries.shape
    scale = width ** (-0.5)
    groups = lax.axis_size("blk")
    mine = lax.axis_index("blk")
    kept = database.reshape(-1, tile, width)
    listed = pair_tiles[0]
    lengths = pair_lengths[0]
    live_count = live_pairs[0]
    slots = jnp.arange(listed.shape[0])
    used = slots < live_count

    def term_of(panel, slot_index):
        key_tile = lax.dynamic_index_in_dim(kept, listed[slot_index, 1], 0, keepdims=False)
        return pair_term(panel, key_tile, lengths[slot_index], scale)

    def visit(step, carry):
        panel, partial_sum = carry
        home = (mine - step) % groups
        first = jnp.sum(((listed[:, 0] < home) & used).astype(jnp.int32))
        last = jnp.sum(((listed[:, 0] <= home) & used).astype(jnp.int32))
        partial_sum = lax.fori_loop(
            first, last, lambda slot_index, total: total + term_of(panel, slot_index), partial_sum
        )
        panel = shifted(panel, "blk", 1)
        partial_sum = shifted(partial_sum, "blk", 1)
        return (panel, partial_sum)

    start = jnp.zeros((tile, width), jnp.float32)
    panel, summed = lax.fori_loop(0, groups, visit, (queries, start))
    return lax.psum_scatter(summed, "shard", scatter_dimension=0, tiled=True).astype(jnp.bfloat16)


def solution(mesh):
    in_specs = (
        P("blk", None),
        P(("blk", "shard"), None),
        P(("blk", "shard"), None, None),
        P(("blk", "shard"), None, None),
        P(("blk", "shard")),
    )
    out_specs = P(("blk", "shard"), None)
    return jax.shard_map(
        on_device, mesh=mesh, in_specs=in_specs, out_specs=out_specs, check_vma=False
    )
```

profile of v0, /device:TPU:2, one launch (start us, length us, event | category | flops | bytes accessed | tf_op | source)
XLA Modules:
  0.0 1234.3 jit_solution(5042886559679302419)
XLA Ops:
  1.0 980.5 %while.51 = (s32[]{:T(128)}, bf16[128,1280]{1,0:T(8,128)(2,1)S(1)}, f32[128,1280]{1,0:T(8,128)S(1)}, s32[24,2]{0,1:T(2,128)}, s32[]{:T(128)}, /*index=5*/s32[24,...) while((s32[]{:T(128)}, bf16[128,1280]{1,0:T(8,128)(2,1)S(1)}, ...), condition=%wide.region_9.10_spmd.clone, body=%wide.region_0.9_spmd.clone.sunk | while | flops 84361448 | bytes 8463383 | solution.py:61
  1.1 2.0 fusion.33
  3.1 14.3 %while.52 = (s32[]{:T(128)}, f32[128,1280]{1,0:T(8,128)S(1)}, s32[]{:T(128)}, s32[24,2]{0,1:T(2,128)}, s32[24,2]{0,1:T(2,128)}, /*index=5*/bf16[6,128,1280]{2,1,...) while((s32[]{:T(128)}, f32[128,1280]{1,0:T(8,128)S(1)}, ...), condition=%wide.region_8.8_spmd, body=%wide.region_3.7_spmd.sunk | while | flops 84361224 | bytes 2564593 | solution.py:53
  21.2 31.0 %collective-permute-done.1 = f32[128,1280]{1,0:T(8,128)S(1)} collective-permute-done((f32[128,1280]{1,0:T(8,128)S(1)}, f32[128,1280]{1,0:T(8,128)S(1)}, u32[]{:S(2)}, u32[]{:S(2)}) %collective-permute-start.1) | collective-permute-done | bytes 655392 | tf_op jit(solution)/shard_map/while/body/eval_jaxpr/ppermute | solution.py:10
  52.3 14.6 %collective-permute-done = bf16[128,1280]{1,0:T(8,128)(2,1)S(1)} collective-permute-done((bf16[128,1280]{1,0:T(8,128)(2,1)S(1)}, bf16[128,1280]{1,0:T(8,128)(2,1)S(1)}, u32[]{:S(2)}, u32[]{:S(2)}) %collective-permute-start) | collective-permute-done | bytes 327712 | tf_op jit(solution)/shard_map/while/body/eval_jaxpr/ppermute | solution.py:10
  66.9 2.0 fusion.33
  69.0 27.3 %while.52 = (s32[]{:T(128)}, f32[128,1280]{1,0:T(8,128)S(1)}, s32[]{:T(128)}, s32[24,2]{0,1:T(2,128)}, s32[24,2]{0,1:T(2,128)}, /*index=5*/bf16[6,128,1280]{2,1,...) while((s32[]{:T(128)}, f32[128,1280]{1,0:T(8,128)S(1)}, ...), condition=%wide.region_8.8_spmd, body=%wide.region_3.7_spmd.sunk | while | flops 84361224 | bytes 2564593 | solution.py:53
  98.2 14.2 %collective-permute-start = (bf16[128,1280]{1,0:T(8,128)(2,1)S(1)}, bf16[128,1280]{1,0:T(8,128)(2,1)S(1)}, u32[]{:S(2)}, u32[]{:S(2)}) collective-permute-start(bf16[128,1280]{1,0:T(8,128)(2,1)S(1)} %get-tuple-element.514), channel_id=1, source_target_pairs={{480,0},{0,32},{32,64},{64,96},{96,128},{128,160},{160,192},{192,2... | collective-permute-start | bytes 983048 | tf_op jit(solution)/shard_map/while/body/eval_jaxpr/ppermute | solution.py:10
  112.5 4.3 collective-permute-done.1
  116.8 13.6 %collective-permute-done = bf16[128,1280]{1,0:T(8,128)(2,1)S(1)} collective-permute-done((bf16[128,1280]{1,0:T(8,128)(2,1)S(1)}, bf16[128,1280]{1,0:T(8,128)(2,1)S(1)}, u32[]{:S(2)}, u32[]{:S(2)}) %collective-permute-start) | collective-permute-done | bytes 327712 | tf_op jit(solution)/shard_map/while/body/eval_jaxpr/ppermute | solution.py:10
  130.4 2.0 fusion.33
  132.4 14.3 %while.52 = (s32[]{:T(128)}, f32[128,1280]{1,0:T(8,128)S(1)}, s32[]{:T(128)}, s32[24,2]{0,1:T(2,128)}, s32[24,2]{0,1:T(2,128)}, /*index=5*/bf16[6,128,1280]{2,1,...) while((s32[]{:T(128)}, f32[128,1280]{1,0:T(8,128)S(1)}, ...), condition=%wide.region_8.8_spmd, body=%wide.region_3.7_spmd.sunk | while | flops 84361224 | bytes 2564593 | solution.py:53
  150.6 15.7 %collective-permute-done.1 = f32[128,1280]{1,0:T(8,128)S(1)} collective-permute-done((f32[128,1280]{1,0:T(8,128)S(1)}, f32[128,1280]{1,0:T(8,128)S(1)}, u32[]{:S(2)}, u32[]{:S(2)}) %collective-permute-start.1) | collective-permute-done | bytes 655392 | tf_op jit(solution)/shard_map/while/body/eval_jaxpr/ppermute | solution.py:10
  166.3 15.1 %collective-permute-done = bf16[128,1280]{1,0:T(8,128)(2,1)S(1)} collective-permute-done((bf16[128,1280]{1,0:T(8,128)(2,1)S(1)}, bf16[128,1280]{1,0:T(8,128)(2,1)S(1)}, u32[]{:S(2)}, u32[]{:S(2)}) %collective-permute-start) | collective-permute-done | bytes 327712 | tf_op jit(solution)/shard_map/while/body/eval_jaxpr/ppermute | solution.py:10
  181.5 2.0 fusion.33
  183.5 40.4 %while.52 = (s32[]{:T(128)}, f32[128,1280]{1,0:T(8,128)S(1)}, s32[]{:T(128)}, s32[24,2]{0,1:T(2,128)}, s32[24,2]{0,1:T(2,128)}, /*index=5*/bf16[6,128,1280]{2,1,...) while((s32[]{:T(128)}, f32[128,1280]{1,0:T(8,128)S(1)}, ...), condition=%wide.region_8.8_spmd, body=%wide.region_3.7_spmd.sunk | while | flops 84361224 | bytes 2564593 | solution.py:53
  227.8 15.3 %collective-permute-done.1 = f32[128,1280]{1,0:T(8,128)S(1)} collective-permute-done((f32[128,1280]{1,0:T(8,128)S(1)}, f32[128,1280]{1,0:T(8,128)S(1)}, u32[]{:S(2)}, u32[]{:S(2)}) %collective-permute-start.1) | collective-permute-done | bytes 655392 | tf_op jit(solution)/shard_map/while/body/eval_jaxpr/ppermute | solution.py:10
  243.1 10.4 collective-permute-done
  253.6 2.0 fusion.33
  255.6 27.3 %while.52 = (s32[]{:T(128)}, f32[128,1280]{1,0:T(8,128)S(1)}, s32[]{:T(128)}, s32[24,2]{0,1:T(2,128)}, s32[24,2]{0,1:T(2,128)}, /*index=5*/bf16[6,128,1280]{2,1,...) while((s32[]{:T(128)}, f32[128,1280]{1,0:T(8,128)S(1)}, ...), condition=%wide.region_8.8_spmd, body=%wide.region_3.7_spmd.sunk | while | flops 84361224 | bytes 2564593 | solution.py:53
  286.8 21.4 %collective-permute-done.1 = f32[128,1280]{1,0:T(8,128)S(1)} collective-permute-done((f32[128,1280]{1,0:T(8,128)S(1)}, f32[128,1280]{1,0:T(8,128)S(1)}, u32[]{:S(2)}, u32[]{:S(2)}) %collective-permute-start.1) | collective-permute-done | bytes 655392 | tf_op jit(solution)/shard_map/while/body/eval_jaxpr/ppermute | solution.py:10
  308.3 13.2 %collective-permute-done = bf16[128,1280]{1,0:T(8,128)(2,1)S(1)} collective-permute-done((bf16[128,1280]{1,0:T(8,128)(2,1)S(1)}, bf16[128,1280]{1,0:T(8,128)(2,1)S(1)}, u32[]{:S(2)}, u32[]{:S(2)}) %collective-permute-start) | collective-permute-done | bytes 327712 | tf_op jit(solution)/shard_map/while/body/eval_jaxpr/ppermute | solution.py:10
  321.5 2.0 fusion.33
  323.6 27.3 %while.52 = (s32[]{:T(128)}, f32[128,1280]{1,0:T(8,128)S(1)}, s32[]{:T(128)}, s32[24,2]{0,1:T(2,128)}, s32[24,2]{0,1:T(2,128)}, /*index=5*/bf16[6,128,1280]{2,1,...) while((s32[]{:T(128)}, f32[128,1280]{1,0:T(8,128)S(1)}, ...), condition=%wide.region_8.8_spmd, body=%wide.region_3.7_spmd.sunk | while | flops 84361224 | bytes 2564593 | solution.py:53
  354.8 31.4 %collective-permute-done.1 = f32[128,1280]{1,0:T(8,128)S(1)} collective-permute-done((f32[128,1280]{1,0:T(8,128)S(1)}, f32[128,1280]{1,0:T(8,128)S(1)}, u32[]{:S(2)}, u32[]{:S(2)}) %collective-permute-start.1) | collective-permute-done | bytes 655392 | tf_op jit(solution)/shard_map/while/body/eval_jaxpr/ppermute | solution.py:10
  386.2 7.0 collective-permute-done
  393.3 2.0 fusion.33
  395.3 53.5 %while.52 = (s32[]{:T(128)}, f32[128,1280]{1,0:T(8,128)S(1)}, s32[]{:T(128)}, s32[24,2]{0,1:T(2,128)}, s32[24,2]{0,1:T(2,128)}, /*index=5*/bf16[6,128,1280]{2,1,...) while((s32[]{:T(128)}, f32[128,1280]{1,0:T(8,128)S(1)}, ...), condition=%wide.region_8.8_spmd, body=%wide.region_3.7_spmd.sunk | while | flops 84361224 | bytes 2564593 | solution.py:53
  452.6 19.9 %collective-permute-done.1 = f32[128,1280]{1,0:T(8,128)S(1)} collective-permute-done((f32[128,1280]{1,0:T(8,128)S(1)}, f32[128,1280]{1,0:T(8,128)S(1)}, u32[]{:S(2)}, u32[]{:S(2)}) %collective-permute-start.1) | collective-permute-done | bytes 655392 | tf_op jit(solution)/shard_map/while/body/eval_jaxpr/ppermute | solution.py:10
  472.5 19.6 %collective-permute-done = bf16[128,1280]{1,0:T(8,128)(2,1)S(1)} collective-permute-done((bf16[128,1280]{1,0:T(8,128)(2,1)S(1)}, bf16[128,1280]{1,0:T(8,128)(2,1)S(1)}, u32[]{:S(2)}, u32[]{:S(2)}) %collective-permute-start) | collective-permute-done | bytes 327712 | tf_op jit(solution)/shard_map/while/body/eval_jaxpr/ppermute | solution.py:10
  492.2 2.0 fusion.33
  499.3 12.1 collective-permute-done.1
  511.4 3.5 collective-permute-done
  514.9 2.0 fusion.33
  517.0 27.3 %while.52 = (s32[]{:T(128)}, f32[128,1280]{1,0:T(8,128)S(1)}, s32[]{:T(128)}, s32[24,2]{0,1:T(2,128)}, s32[24,2]{0,1:T(2,128)}, /*index=5*/bf16[6,128,1280]{2,1,...) while((s32[]{:T(128)}, f32[128,1280]{1,0:T(8,128)S(1)}, ...), condition=%wide.region_8.8_spmd, body=%wide.region_3.7_spmd.sunk | while | flops 84361224 | bytes 2564593 | solution.py:53
  548.1 24.4 %collective-permute-done.1 = f32[128,1280]{1,0:T(8,128)S(1)} collective-permute-done((f32[128,1280]{1,0:T(8,128)S(1)}, f32[128,1280]{1,0:T(8,128)S(1)}, u32[]{:S(2)}, u32[]{:S(2)}) %collective-permute-start.1) | collective-permute-done | bytes 655392 | tf_op jit(solution)/shard_map/while/body/eval_jaxpr/ppermute | solution.py:10
  572.6 4.7 collective-permute-done
  577.4 2.0 fusion.33
  579.4 14.3 %while.52 = (s32[]{:T(128)}, f32[128,1280]{1,0:T(8,128)S(1)}, s32[]{:T(128)}, s32[24,2]{0,1:T(2,128)}, s32[24,2]{0,1:T(2,128)}, /*index=5*/bf16[6,128,1280]{2,1,...) while((s32[]{:T(128)}, f32[128,1280]{1,0:T(8,128)S(1)}, ...), condition=%wide.region_8.8_spmd, body=%wide.region_3.7_spmd.sunk | while | flops 84361224 | bytes 2564593 | solution.py:53
  597.5 20.2 %collective-permute-done.1 = f32[128,1280]{1,0:T(8,128)S(1)} collective-permute-done((f32[128,1280]{1,0:T(8,128)S(1)}, f32[128,1280]{1,0:T(8,128)S(1)}, u32[]{:S(2)}, u32[]{:S(2)}) %collective-permute-start.1) | collective-permute-done | bytes 655392 | tf_op jit(solution)/shard_map/while/body/eval_jaxpr/ppermute | solution.py:10
  617.8 3.5 collective-permute-done
  621.3 2.0 fusion.33
  624.5 5.3 collective-permute-start.1
  631.8 38.9 %collective-permute-done.1 = f32[128,1280]{1,0:T(8,128)S(1)} collective-permute-done((f32[128,1280]{1,0:T(8,128)S(1)}, f32[128,1280]{1,0:T(8,128)S(1)}, u32[]{:S(2)}, u32[]{:S(2)}) %collective-permute-start.1) | collective-permute-done | bytes 655392 | tf_op jit(solution)/shard_map/while/body/eval_jaxpr/ppermute | solution.py:10
  670.8 6.2 collective-permute-done
  677.0 2.0 fusion.33
  684.1 32.5 %collective-permute-done.1 = f32[128,1280]{1,0:T(8,128)S(1)} collective-permute-done((f32[128,1280]{1,0:T(8,128)S(1)}, f32[128,1280]{1,0:T(8,128)S(1)}, u32[]{:S(2)}, u32[]{:S(2)}) %collective-permute-start.1) | collective-permute-done | bytes 655392 | tf_op jit(solution)/shard_map/while/body/eval_jaxpr/ppermute | solution.py:10
  716.6 3.6 collective-permute-done
  720.2 2.0 fusion.33
  722.2 14.3 %while.52 = (s32[]{:T(128)}, f32[128,1280]{1,0:T(8,128)S(1)}, s32[]{:T(128)}, s32[24,2]{0,1:T(2,128)}, s32[24,2]{0,1:T(2,128)}, /*index=5*/bf16[6,128,1280]{2,1,...) while((s32[]{:T(128)}, f32[128,1280]{1,0:T(8,128)S(1)}, ...), condition=%wide.region_8.8_spmd, body=%wide.region_3.7_spmd.sunk | while | flops 84361224 | bytes 2564593 | solution.py:53
  740.4 23.1 %collective-permute-done.1 = f32[128,1280]{1,0:T(8,128)S(1)} collective-permute-done((f32[128,1280]{1,0:T(8,128)S(1)}, f32[128,1280]{1,0:T(8,128)S(1)}, u32[]{:S(2)}, u32[]{:S(2)}) %collective-permute-start.1) | collective-permute-done | bytes 655392 | tf_op jit(solution)/shard_map/while/body/eval_jaxpr/ppermute | solution.py:10
  763.5 12.9 %collective-permute-done = bf16[128,1280]{1,0:T(8,128)(2,1)S(1)} collective-permute-done((bf16[128,1280]{1,0:T(8,128)(2,1)S(1)}, bf16[128,1280]{1,0:T(8,128)(2,1)S(1)}, u32[]{:S(2)}, u32[]{:S(2)}) %collective-permute-start) | collective-permute-done | bytes 327712 | tf_op jit(solution)/shard_map/while/body/eval_jaxpr/ppermute | solution.py:10
  776.4 2.0 fusion.33
  778.5 27.3 %while.52 = (s32[]{:T(128)}, f32[128,1280]{1,0:T(8,128)S(1)}, s32[]{:T(128)}, s32[24,2]{0,1:T(2,128)}, s32[24,2]{0,1:T(2,128)}, /*index=5*/bf16[6,128,1280]{2,1,...) while((s32[]{:T(128)}, f32[128,1280]{1,0:T(8,128)S(1)}, ...), condition=%wide.region_8.8_spmd, body=%wide.region_3.7_spmd.sunk | while | flops 84361224 | bytes 2564593 | solution.py:53
  809.7 25.2 %collective-permute-done.1 = f32[128,1280]{1,0:T(8,128)S(1)} collective-permute-done((f32[128,1280]{1,0:T(8,128)S(1)}, f32[128,1280]{1,0:T(8,128)S(1)}, u32[]{:S(2)}, u32[]{:S(2)}) %collective-permute-start.1) | collective-permute-done | bytes 655392 | tf_op jit(solution)/shard_map/while/body/eval_jaxpr/ppermute | solution.py:10
  834.9 7.0 collective-permute-done
  842.0 2.0 fusion.33
  845.2 44.5 %collective-permute-start.1 = (f32[128,1280]{1,0:T(8,128)S(1)}, f32[128,1280]{1,0:T(8,128)S(1)}, u32[]{:S(2)}, u32[]{:S(2)}) collective-permute-start(f32[128,1280]{1,0:T(8,128)S(1)} %get-tuple-element.416), channel_id=1, source_target_pairs={{480,0},{0,32},{32,64},{64,96},{96,128},{128,160},{160,192},{192,2... | collective-permute-start | bytes 1966088 | tf_op jit(solution)/shard_map/while/body/eval_jaxpr/ppermute | solution.py:10
  891.7 6.2 collective-permute-done.1
  897.9 8.0 collective-permute-done
  908.0 40.4 %while.52 = (s32[]{:T(128)}, f32[128,1280]{1,0:T(8,128)S(1)}, s32[]{:T(128)}, s32[24,2]{0,1:T(2,128)}, s32[24,2]{0,1:T(2,128)}, /*index=5*/bf16[6,128,1280]{2,1,...) while((s32[]{:T(128)}, f32[128,1280]{1,0:T(8,128)S(1)}, ...), condition=%wide.region_8.8_spmd, body=%wide.region_3.7_spmd.sunk | while | flops 84361224 | bytes 2564593 | solution.py:53
  952.3 15.6 %collective-permute-done.1 = f32[128,1280]{1,0:T(8,128)S(1)} collective-permute-done((f32[128,1280]{1,0:T(8,128)S(1)}, f32[128,1280]{1,0:T(8,128)S(1)}, u32[]{:S(2)}, u32[]{:S(2)}) %collective-permute-start.1) | collective-permute-done | bytes 655392 | tf_op jit(solution)/shard_map/while/body/eval_jaxpr/ppermute | solution.py:10
  967.9 13.6 %collective-permute-done = bf16[128,1280]{1,0:T(8,128)(2,1)S(1)} collective-permute-done((bf16[128,1280]{1,0:T(8,128)(2,1)S(1)}, bf16[128,1280]{1,0:T(8,128)(2,1)S(1)}, u32[]{:S(2)}, u32[]{:S(2)}) %collective-permute-start) | collective-permute-done | bytes 327712 | tf_op jit(solution)/shard_map/while/body/eval_jaxpr/ppermute | solution.py:10
  981.5 250.3 %all-reduce.2 = bf16[128,1280]{1,0:T(8,128)(2,1)S(1)} all-reduce(f32[128,1280]{1,0:T(8,128)S(1)} %get-tuple-element.242), channel_id=2, replica_groups=mesh['blk'=16,'shard'=32] {'shard'}, use_global_device_ids=true, to_apply=%region_10.11.clone | all-reduce | flops 163840 | bytes 983040
  (310 shorter events, 230.3 us)
Async XLA Ops:
  17.4 34.9 %collective-permute-start.1 = (f32[128,1280]{1,0:T(8,128)S(1)}, f32[128,1280]{1,0:T(8,128)S(1)}, u32[]{:S(2)}, u32[]{:S(2)}) collective-permute-start(f32[128,1280]{1,0:T(8,128)S(1)} %get-tuple-element.416), channel_id=1, source_target_pairs={{480,0},{0,32},{32,64},{64,96},{96,128},{128,160},{160,192},{192,2... | collective-permute-start | bytes 1966088 | tf_op jit(solution)/shard_map/while/body/eval_jaxpr/ppermute | solution.py:10
  19.3 47.6 %collective-permute-start = (bf16[128,1280]{1,0:T(8,128)(2,1)S(1)}, bf16[128,1280]{1,0:T(8,128)(2,1)S(1)}, u32[]{:S(2)}, u32[]{:S(2)}) collective-permute-start(bf16[128,1280]{1,0:T(8,128)(2,1)S(1)} %get-tuple-element.514), channel_id=1, source_target_pairs={{480,0},{0,32},{32,64},{64,96},{96,128},{128,160},{160,192},{192,2... | collective-permute-start | bytes 983048 | tf_op jit(solution)/shard_map/while/body/eval_jaxpr/ppermute | solution.py:10
  96.3 20.4 %collective-permute-start.1 = (f32[128,1280]{1,0:T(8,128)S(1)}, f32[128,1280]{1,0:T(8,128)S(1)}, u32[]{:S(2)}, u32[]{:S(2)}) collective-permute-start(f32[128,1280]{1,0:T(8,128)S(1)} %get-tuple-element.416), channel_id=1, source_target_pairs={{480,0},{0,32},{32,64},{64,96},{96,128},{128,160},{160,192},{192,2... | collective-permute-start | bytes 1966088 | tf_op jit(solution)/shard_map/while/body/eval_jaxpr/ppermute | solution.py:10
  98.2 32.1 %collective-permute-start = (bf16[128,1280]{1,0:T(8,128)(2,1)S(1)}, bf16[128,1280]{1,0:T(8,128)(2,1)S(1)}, u32[]{:S(2)}, u32[]{:S(2)}) collective-permute-start(bf16[128,1280]{1,0:T(8,128)(2,1)S(1)} %get-tuple-element.514), channel_id=1, source_target_pairs={{480,0},{0,32},{32,64},{64,96},{96,128},{128,160},{160,192},{192,2... | collective-permute-start | bytes 983048 | tf_op jit(solution)/shard_map/while/body/eval_jaxpr/ppermute | solution.py:10
  146.7 19.6 %collective-permute-start.1 = (f32[128,1280]{1,0:T(8,128)S(1)}, f32[128,1280]{1,0:T(8,128)S(1)}, u32[]{:S(2)}, u32[]{:S(2)}) collective-permute-start(f32[128,1280]{1,0:T(8,128)S(1)} %get-tuple-element.416), channel_id=1, source_target_pairs={{480,0},{0,32},{32,64},{64,96},{96,128},{128,160},{160,192},{192,2... | collective-permute-start | bytes 1966088 | tf_op jit(solution)/shard_map/while/body/eval_jaxpr/ppermute | solution.py:10
  148.6 32.8 %collective-permute-start = (bf16[128,1280]{1,0:T(8,128)(2,1)S(1)}, bf16[128,1280]{1,0:T(8,128)(2,1)S(1)}, u32[]{:S(2)}, u32[]{:S(2)}) collective-permute-start(bf16[128,1280]{1,0:T(8,128)(2,1)S(1)} %get-tuple-element.514), channel_id=1, source_target_pairs={{480,0},{0,32},{32,64},{64,96},{96,128},{128,160},{160,192},{192,2... | collective-permute-start | bytes 983048 | tf_op jit(solution)/shard_map/while/body/eval_jaxpr/ppermute | solution.py:10
  223.9 19.1 %collective-permute-start.1 = (f32[128,1280]{1,0:T(8,128)S(1)}, f32[128,1280]{1,0:T(8,128)S(1)}, u32[]{:S(2)}, u32[]{:S(2)}) collective-permute-start(f32[128,1280]{1,0:T(8,128)S(1)} %get-tuple-element.416), channel_id=1, source_target_pairs={{480,0},{0,32},{32,64},{64,96},{96,128},{128,160},{160,192},{192,2... | collective-permute-start | bytes 1966088 | tf_op jit(solution)/shard_map/while/body/eval_jaxpr/ppermute | solution.py:10
  225.8 27.7 %collective-permute-start = (bf16[128,1280]{1,0:T(8,128)(2,1)S(1)}, bf16[128,1280]{1,0:T(8,128)(2,1)S(1)}, u32[]{:S(2)}, u32[]{:S(2)}) collective-permute-start(bf16[128,1280]{1,0:T(8,128)(2,1)S(1)} %get-tuple-element.514), channel_id=1, source_target_pairs={{480,0},{0,32},{32,64},{64,96},{96,128},{128,160},{160,192},{192,2... | collective-permute-start | bytes 983048 | tf_op jit(solution)/shard_map/while/body/eval_jaxpr/ppermute | solution.py:10
  282.9 25.3 %collective-permute-start.1 = (f32[128,1280]{1,0:T(8,128)S(1)}, f32[128,1280]{1,0:T(8,128)S(1)}, u32[]{:S(2)}, u32[]{:S(2)}) collective-permute-start(f32[128,1280]{1,0:T(8,128)S(1)} %get-tuple-element.416), channel_id=1, source_target_pairs={{480,0},{0,32},{32,64},{64,96},{96,128},{128,160},{160,192},{192,2... | collective-permute-start | bytes 1966088 | tf_op jit(solution)/shard_map/while/body/eval_jaxpr/ppermute | solution.py:10
  284.9 36.6 %collective-permute-start = (bf16[128,1280]{1,0:T(8,128)(2,1)S(1)}, bf16[128,1280]{1,0:T(8,128)(2,1)S(1)}, u32[]{:S(2)}, u32[]{:S(2)}) collective-permute-start(bf16[128,1280]{1,0:T(8,128)(2,1)S(1)} %get-tuple-element.514), channel_id=1, source_target_pairs={{480,0},{0,32},{32,64},{64,96},{96,128},{128,160},{160,192},{192,2... | collective-permute-start | bytes 983048 | tf_op jit(solution)/shard_map/while/body/eval_jaxpr/ppermute | solution.py:10
  350.9 35.3 %collective-permute-start.1 = (f32[128,1280]{1,0:T(8,128)S(1)}, f32[128,1280]{1,0:T(8,128)S(1)}, u32[]{:S(2)}, u32[]{:S(2)}) collective-permute-start(f32[128,1280]{1,0:T(8,128)S(1)} %get-tuple-element.416), channel_id=1, source_target_pairs={{480,0},{0,32},{32,64},{64,96},{96,128},{128,160},{160,192},{192,2... | collective-permute-start | bytes 1966088 | tf_op jit(solution)/shard_map/while/body/eval_jaxpr/ppermute | solution.py:10
  352.8 40.4 %collective-permute-start = (bf16[128,1280]{1,0:T(8,128)(2,1)S(1)}, bf16[128,1280]{1,0:T(8,128)(2,1)S(1)}, u32[]{:S(2)}, u32[]{:S(2)}) collective-permute-start(bf16[128,1280]{1,0:T(8,128)(2,1)S(1)} %get-tuple-element.514), channel_id=1, source_target_pairs={{480,0},{0,32},{32,64},{64,96},{96,128},{128,160},{160,192},{192,2... | collective-permute-start | bytes 983048 | tf_op jit(solution)/shard_map/while/body/eval_jaxpr/ppermute | solution.py:10
  448.7 23.8 %collective-permute-start.1 = (f32[128,1280]{1,0:T(8,128)S(1)}, f32[128,1280]{1,0:T(8,128)S(1)}, u32[]{:S(2)}, u32[]{:S(2)}) collective-permute-start(f32[128,1280]{1,0:T(8,128)S(1)} %get-tuple-element.416), channel_id=1, source_target_pairs={{480,0},{0,32},{32,64},{64,96},{96,128},{128,160},{160,192},{192,2... | collective-permute-start | bytes 1966088 | tf_op jit(solution)/shard_map/while/body/eval_jaxpr/ppermute | solution.py:10
  450.7 41.5 %collective-permute-start = (bf16[128,1280]{1,0:T(8,128)(2,1)S(1)}, bf16[128,1280]{1,0:T(8,128)(2,1)S(1)}, u32[]{:S(2)}, u32[]{:S(2)}) collective-permute-start(bf16[128,1280]{1,0:T(8,128)(2,1)S(1)} %get-tuple-element.514), channel_id=1, source_target_pairs={{480,0},{0,32},{32,64},{64,96},{96,128},{128,160},{160,192},{192,2... | collective-permute-start | bytes 983048 | tf_op jit(solution)/shard_map/while/body/eval_jaxpr/ppermute | solution.py:10
  495.4 15.9 %collective-permute-start.1 = (f32[128,1280]{1,0:T(8,128)S(1)}, f32[128,1280]{1,0:T(8,128)S(1)}, u32[]{:S(2)}, u32[]{:S(2)}) collective-permute-start(f32[128,1280]{1,0:T(8,128)S(1)} %get-tuple-element.416), channel_id=1, source_target_pairs={{480,0},{0,32},{32,64},{64,96},{96,128},{128,160},{160,192},{192,2... | collective-permute-start | bytes 1966088 | tf_op jit(solution)/shard_map/while/body/eval_jaxpr/ppermute | solution.py:10
  497.4 17.5 %collective-permute-start = (bf16[128,1280]{1,0:T(8,128)(2,1)S(1)}, bf16[128,1280]{1,0:T(8,128)(2,1)S(1)}, u32[]{:S(2)}, u32[]{:S(2)}) collective-permute-start(bf16[128,1280]{1,0:T(8,128)(2,1)S(1)} %get-tuple-element.514), channel_id=1, source_target_pairs={{480,0},{0,32},{32,64},{64,96},{96,128},{128,160},{160,192},{192,2... | collective-permute-start | bytes 983048 | tf_op jit(solution)/shard_map/while/body/eval_jaxpr/ppermute | solution.py:10
  544.3 28.3 %collective-permute-start.1 = (f32[128,1280]{1,0:T(8,128)S(1)}, f32[128,1280]{1,0:T(8,128)S(1)}, u32[]{:S(2)}, u32[]{:S(2)}) collective-permute-start(f32[128,1280]{1,0:T(8,128)S(1)} %get-tuple-element.416), channel_id=1, source_target_pairs={{480,0},{0,32},{32,64},{64,96},{96,128},{128,160},{160,192},{192,2... | collective-permute-start | bytes 1966088 | tf_op jit(solution)/shard_map/while/body/eval_jaxpr/ppermute | solution.py:10
  546.2 31.1 %collective-permute-start = (bf16[128,1280]{1,0:T(8,128)(2,1)S(1)}, bf16[128,1280]{1,0:T(8,128)(2,1)S(1)}, u32[]{:S(2)}, u32[]{:S(2)}) collective-permute-start(bf16[128,1280]{1,0:T(8,128)(2,1)S(1)} %get-tuple-element.514), channel_id=1, source_target_pairs={{480,0},{0,32},{32,64},{64,96},{96,128},{128,160},{160,192},{192,2... | collective-permute-start | bytes 983048 | tf_op jit(solution)/shard_map/while/body/eval_jaxpr/ppermute | solution.py:10
  593.7 24.1 %collective-permute-start.1 = (f32[128,1280]{1,0:T(8,128)S(1)}, f32[128,1280]{1,0:T(8,128)S(1)}, u32[]{:S(2)}, u32[]{:S(2)}) collective-permute-start(f32[128,1280]{1,0:T(8,128)S(1)} %get-tuple-element.416), channel_id=1, source_target_pairs={{480,0},{0,32},{32,64},{64,96},{96,128},{128,160},{160,192},{192,2... | collective-permute-start | bytes 1966088 | tf_op jit(solution)/shard_map/while/body/eval_jaxpr/ppermute | solution.py:10
  595.6 25.7 %collective-permute-start = (bf16[128,1280]{1,0:T(8,128)(2,1)S(1)}, bf16[128,1280]{1,0:T(8,128)(2,1)S(1)}, u32[]{:S(2)}, u32[]{:S(2)}) collective-permute-start(bf16[128,1280]{1,0:T(8,128)(2,1)S(1)} %get-tuple-element.514), channel_id=1, source_target_pairs={{480,0},{0,32},{32,64},{64,96},{96,128},{128,160},{160,192},{192,2... | collective-permute-start | bytes 983048 | tf_op jit(solution)/shard_map/while/body/eval_jaxpr/ppermute | solution.py:10
  624.5 46.2 %collective-permute-start.1 = (f32[128,1280]{1,0:T(8,128)S(1)}, f32[128,1280]{1,0:T(8,128)S(1)}, u32[]{:S(2)}, u32[]{:S(2)}) collective-permute-start(f32[128,1280]{1,0:T(8,128)S(1)} %get-tuple-element.416), channel_id=1, source_target_pairs={{480,0},{0,32},{32,64},{64,96},{96,128},{128,160},{160,192},{192,2... | collective-permute-start | bytes 1966088 | tf_op jit(solution)/shard_map/while/body/eval_jaxpr/ppermute | solution.py:10
  629.9 47.1 %collective-permute-start = (bf16[128,1280]{1,0:T(8,128)(2,1)S(1)}, bf16[128,1280]{1,0:T(8,128)(2,1)S(1)}, u32[]{:S(2)}, u32[]{:S(2)}) collective-permute-start(bf16[128,1280]{1,0:T(8,128)(2,1)S(1)} %get-tuple-element.514), channel_id=1, source_target_pairs={{480,0},{0,32},{32,64},{64,96},{96,128},{128,160},{160,192},{192,2... | collective-permute-start | bytes 983048 | tf_op jit(solution)/shard_map/while/body/eval_jaxpr/ppermute | solution.py:10
  680.3 36.3 %collective-permute-start.1 = (f32[128,1280]{1,0:T(8,128)S(1)}, f32[128,1280]{1,0:T(8,128)S(1)}, u32[]{:S(2)}, u32[]{:S(2)}) collective-permute-start(f32[128,1280]{1,0:T(8,128)S(1)} %get-tuple-element.416), channel_id=1, source_target_pairs={{480,0},{0,32},{32,64},{64,96},{96,128},{128,160},{160,192},{192,2... | collective-permute-start | bytes 1966088 | tf_op jit(solution)/shard_map/while/body/eval_jaxpr/ppermute | solution.py:10
  682.2 38.0 %collective-permute-start = (bf16[128,1280]{1,0:T(8,128)(2,1)S(1)}, bf16[128,1280]{1,0:T(8,128)(2,1)S(1)}, u32[]{:S(2)}, u32[]{:S(2)}) collective-permute-start(bf16[128,1280]{1,0:T(8,128)(2,1)S(1)} %get-tuple-element.514), channel_id=1, source_target_pairs={{480,0},{0,32},{32,64},{64,96},{96,128},{128,160},{160,192},{192,2... | collective-permute-start | bytes 983048 | tf_op jit(solution)/shard_map/while/body/eval_jaxpr/ppermute | solution.py:10
  736.5 26.9 %collective-permute-start.1 = (f32[128,1280]{1,0:T(8,128)S(1)}, f32[128,1280]{1,0:T(8,128)S(1)}, u32[]{:S(2)}, u32[]{:S(2)}) collective-permute-start(f32[128,1280]{1,0:T(8,128)S(1)} %get-tuple-element.416), channel_id=1, source_target_pairs={{480,0},{0,32},{32,64},{64,96},{96,128},{128,160},{160,192},{192,2... | collective-permute-start | bytes 1966088 | tf_op jit(solution)/shard_map/while/body/eval_jaxpr/ppermute | solution.py:10
  738.4 38.0 %collective-permute-start = (bf16[128,1280]{1,0:T(8,128)(2,1)S(1)}, bf16[128,1280]{1,0:T(8,128)(2,1)S(1)}, u32[]{:S(2)}, u32[]{:S(2)}) collective-permute-start(bf16[128,1280]{1,0:T(8,128)(2,1)S(1)} %get-tuple-element.514), channel_id=1, source_target_pairs={{480,0},{0,32},{32,64},{64,96},{96,128},{128,160},{160,192},{192,2... | collective-permute-start | bytes 983048 | tf_op jit(solution)/shard_map/while/body/eval_jaxpr/ppermute | solution.py:10
  805.8 29.1 %collective-permute-start.1 = (f32[128,1280]{1,0:T(8,128)S(1)}, f32[128,1280]{1,0:T(8,128)S(1)}, u32[]{:S(2)}, u32[]{:S(2)}) collective-permute-start(f32[128,1280]{1,0:T(8,128)S(1)} %get-tuple-element.416), channel_id=1, source_target_pairs={{480,0},{0,32},{32,64},{64,96},{96,128},{128,160},{160,192},{192,2... | collective-permute-start | bytes 1966088 | tf_op jit(solution)/shard_map/while/body/eval_jaxpr/ppermute | solution.py:10
  807.7 34.2 %collective-permute-start = (bf16[128,1280]{1,0:T(8,128)(2,1)S(1)}, bf16[128,1280]{1,0:T(8,128)(2,1)S(1)}, u32[]{:S(2)}, u32[]{:S(2)}) collective-permute-start(bf16[128,1280]{1,0:T(8,128)(2,1)S(1)} %get-tuple-element.514), channel_id=1, source_target_pairs={{480,0},{0,32},{32,64},{64,96},{96,128},{128,160},{160,192},{192,2... | collective-permute-start | bytes 983048 | tf_op jit(solution)/shard_map/while/body/eval_jaxpr/ppermute | solution.py:10
  845.2 52.7 %collective-permute-start.1 = (f32[128,1280]{1,0:T(8,128)S(1)}, f32[128,1280]{1,0:T(8,128)S(1)}, u32[]{:S(2)}, u32[]{:S(2)}) collective-permute-start(f32[128,1280]{1,0:T(8,128)S(1)} %get-tuple-element.416), channel_id=1, source_target_pairs={{480,0},{0,32},{32,64},{64,96},{96,128},{128,160},{160,192},{192,2... | collective-permute-start | bytes 1966088 | tf_op jit(solution)/shard_map/while/body/eval_jaxpr/ppermute | solution.py:10
  889.7 16.2 %collective-permute-start = (bf16[128,1280]{1,0:T(8,128)(2,1)S(1)}, bf16[128,1280]{1,0:T(8,128)(2,1)S(1)}, u32[]{:S(2)}, u32[]{:S(2)}) collective-permute-start(bf16[128,1280]{1,0:T(8,128)(2,1)S(1)} %get-tuple-element.514), channel_id=1, source_target_pairs={{480,0},{0,32},{32,64},{64,96},{96,128},{128,160},{160,192},{192,2... | collective-permute-start | bytes 983048 | tf_op jit(solution)/shard_map/while/body/eval_jaxpr/ppermute | solution.py:10
  948.4 19.5 %collective-permute-start.1 = (f32[128,1280]{1,0:T(8,128)S(1)}, f32[128,1280]{1,0:T(8,128)S(1)}, u32[]{:S(2)}, u32[]{:S(2)}) collective-permute-start(f32[128,1280]{1,0:T(8,128)S(1)} %get-tuple-element.416), channel_id=1, source_target_pairs={{480,0},{0,32},{32,64},{64,96},{96,128},{128,160},{160,192},{192,2... | collective-permute-start | bytes 1966088 | tf_op jit(solution)/shard_map/while/body/eval_jaxpr/ppermute | solution.py:10
  950.3 31.2 %collective-permute-start = (bf16[128,1280]{1,0:T(8,128)(2,1)S(1)}, bf16[128,1280]{1,0:T(8,128)(2,1)S(1)}, u32[]{:S(2)}, u32[]{:S(2)}) collective-permute-start(bf16[128,1280]{1,0:T(8,128)(2,1)S(1)} %get-tuple-element.514), channel_id=1, source_target_pairs={{480,0},{0,32},{32,64},{64,96},{96,128},{128,160},{160,192},{192,2... | collective-permute-start | bytes 983048 | tf_op jit(solution)/shard_map/while/body/eval_jaxpr/ppermute | solution.py:10
where the time goes:
time: 1240 us; the launch traced here: 1230 us
  waiting for transfers between devices  494 us (40%)
  blocking collectives  250 us (20%)
  loops' own time  169 us (14%)
  starting transfers between devices  120 us (10%)
  other arithmetic  71.6 us (6%)
  local copies, waits for them, and re-layouts  66.2 us (5%)
  matrix products  62.6 us (5%)
    ppermute x32, waiting for transfers between devices, shifted(): return lax.ppermute(block, axis, route)  494 us
    unnamed x1, blocking collectives  250 us
    another operation x16, loops' own time, visit(): lax.fori_loop(first, last, lambda slot_index, total: total + term_of(pane...  169 us
    ppermute x32, starting transfers between devices, shifted(): return lax.ppermute(block, axis, route)  120 us
    dot_general x24, matrix products, pair_term(): return jnp.dot(weight, key_tile, preferred_element_type=jnp.float32)  32.5 us
    reduce_sum x16, other arithmetic, visit(): last = jnp.sum(((listed[:, 0] <= home) & used).astype(jnp.int32))  32.5 us
    dynamic_slice x24, local copies, waits for them, and re-layouts, term_of(): listed[slot_index, 1]  31 us
    dot_general x24, matrix products, pair_term(): lax.dot_general(panel, key_tile, (((1,), (1,)), ((), ())), preferred_elem...  30 us
  transfers between devices with their start and end apart: 32, of which 32 were waited for; matrix products, arithmetic and copies ran while one was open for 0% of the time, Pallas kernels for 0%

commit v1 on v0

v1 whole, which is shorter than its diff:
```python
import functools

import jax
import jax.numpy as jnp
from jax import lax
from jax.experimental import pallas as pl
from jax.experimental.pallas import tpu as pltpu
from jax.sharding import Mesh
from jax.sharding import PartitionSpec as P

TILE = 128
BLK = ("x", "zh")
SHARD = ("y", "zl", "c")
GROUP_TILES = 2
UNROLL = 4


def pair_weight(scores, rows, cols, row_count, col_count):
    valid = (rows < row_count) & (cols < col_count)
    masked = jnp.where(valid, scores, -1e30)
    row_max = jnp.max(masked, axis=1, keepdims=True)
    row_lse = row_max + jnp.log(jnp.sum(jnp.exp(masked - row_max), axis=1, keepdims=True))
    col_max = jnp.max(masked, axis=0, keepdims=True)
    col_lse = col_max + jnp.log(jnp.sum(jnp.exp(masked - col_max), axis=0, keepdims=True))
    weight = jnp.where(valid, jnp.exp(scores - 0.5 * (row_lse + col_lse)), 0.0)
    return weight.astype(jnp.bfloat16)


def align_kernel(
    scale, tiles, slots, meta, q_ref, own_ref, other_ref, out_ref, scores, weights, listed, seen
):
    step = pl.program_id(0)
    width = tiles * TILE
    stride = meta.shape[0] // 2
    core = meta[4 * slots + 1]

    @pl.when(step == 0)
    def _():
        seen[0] = 0
        seen[1] = 0

    across = (((1,), (1,)), ((), ()))
    query = q_ref[...]
    for side, ref in enumerate((own_ref, other_ref)):
        scores[:, side * width : (side + 1) * width] = (
            lax.dot_general(query, ref[...], across, preferred_element_type=jnp.float32) * scale
        )
    weights[...] = jnp.zeros_like(weights)

    count = jnp.int32(0)
    for side in range(2):
        base = side * stride
        live = meta[base + 4 * slots]

        def here(slot, base=base, live=live):
            at = base + 2 * jnp.minimum(slot, slots - 1)
            return (slot < live) & ((meta[at] >> 2) == step)

        def take(carry, base=base, side=side):
            slot, count = carry
            query_tile = meta[base + 2 * slot]
            mine = (query_tile & 1) == core

            @pl.when(mine)
            def _():
                listed[0, count] = (query_tile & 3) >> 1
                listed[1, count] = meta[base + 2 * slot + 1] + side * tiles
                listed[2, count] = meta[base + 2 * slots + 2 * slot]
                listed[3, count] = meta[base + 2 * slots + 2 * slot + 1]

            return slot + 1, count + mine.astype(jnp.int32)

        slot, count = lax.while_loop(lambda carry: here(carry[0]), take, (seen[side], count))
        seen[side] = slot
    for extra in range(UNROLL - 1):
        listed[0, count + extra] = 0
        listed[1, count + extra] = 0
        listed[2, count + extra] = 0
        listed[3, count + extra] = 0

    place = lax.broadcasted_iota(jnp.int32, (TILE, TILE), 0)
    rows = ((place & 63) >> 2) * 8 + (place >> 6) * 4 + (place & 3)
    cols = lax.broadcasted_iota(jnp.int32, (TILE, TILE), 1)

    def batch(index, carry):
        made = []
        for k in range(UNROLL):
            slot = index * UNROLL + k
            at_row = pl.ds(pl.multiple_of(listed[0, slot] * TILE, TILE), TILE)
            at_col = pl.ds(pl.multiple_of(listed[1, slot] * TILE, TILE), TILE)
            weight = pair_weight(scores[at_row, at_col], rows, cols, listed[2, slot], listed[3, slot])
            made.append((at_row, at_col, weight))
        for at_row, at_col, weight in made:
            weights[at_row, at_col] += weight.astype(jnp.float32)
        return carry

    lax.fori_loop(0, (count + UNROLL - 1) // UNROLL, batch, 0)

    weight = weights[...].astype(jnp.bfloat16)
    out_ref[...] = (
        jnp.dot(weight[:, :width], own_ref[...], preferred_element_type=jnp.float32)
        + jnp.dot(weight[:, width:], other_ref[...], preferred_element_type=jnp.float32)
    ).astype(out_ref.dtype)


def align(meta, queries, own, other, slots):
    rows, width = queries.shape
    block = GROUP_TILES * TILE
    tiles = own.shape[0] // TILE
    columns = 2 * own.shape[0]
    whole = pl.BlockSpec(own.shape, lambda i, meta: (0, 0))
    return pl.pallas_call(
        functools.partial(align_kernel, width ** (-0.5), tiles, slots),
        grid_spec=pltpu.PrefetchScalarGridSpec(
            num_scalar_prefetch=1,
            grid=(rows // block,),
            in_specs=[pl.BlockSpec((block, width), lambda i, meta: (i, 0)), whole, whole],
            out_specs=pl.BlockSpec((block, width), lambda i, meta: (i, 0)),
            scratch_shapes=[
                pltpu.VMEM((block, columns), jnp.float32),
                pltpu.VMEM((block, columns), jnp.float32),
                pltpu.SMEM((4, 2 * slots + UNROLL), jnp.int32),
                pltpu.SMEM((2,), jnp.int32),
            ],
        ),
        out_shape=jax.ShapeDtypeStruct((rows, width), jnp.bfloat16),
        compiler_params=pltpu.CompilerParams(
            dimension_semantics=("arbitrary",), vmem_limit_bytes=40 * 1024 * 1024
        ),
        cost_estimate=pl.CostEstimate(
            flops=4 * rows * columns * width, bytes_accessed=12 * 1024 * 1024, transcendentals=0
        ),
        name="align",
    )(meta, queries, own, other)


def sibling(value):
    return lax.ppermute(value, "c", [(0, 1), (1, 0)])


def on_device(queries, database, pair_tiles, pair_lengths, live_pairs):
    tile, width = queries.shape
    slots = pair_tiles.shape[1]
    core = lax.axis_index("c")
    groups = lax.axis_size("x")
    deep = lax.axis_size("zh")

    used = 4 * slots + 2
    own_meta = jnp.concatenate(
        [pair_tiles.reshape(-1), pair_lengths.reshape(-1), live_pairs, core[None].astype(jnp.int32)]
    )
    own_meta = jnp.pad(own_meta, (0, 128 - used))
    other_meta = sibling(own_meta)
    meta = jnp.concatenate([own_meta, other_meta])
    other = sibling(database)

    halves = queries.reshape(tile // 8, 2, 4, width).swapaxes(0, 1).reshape(2, tile // 2, width)
    half = lax.dynamic_index_in_dim(halves, core, 0, keepdims=False)

    column = lax.all_to_all(
        jnp.broadcast_to(half[None], (deep, tile // 2, width)), "zh", 0, 0, tiled=True
    ).reshape(deep // 2, 2, tile // 2, width)
    kept = lax.dynamic_index_in_dim(column, core, 1, keepdims=False)
    given = lax.dynamic_index_in_dim(column, 1 - core, 1, keepdims=False)
    taken = sibling(given)
    panel = jnp.where(
        core == 0, jnp.stack([kept, taken], 1), jnp.stack([taken, kept], 1)
    ).reshape(deep // 2 * tile, width)

    rows = panel.shape[0]
    panels = lax.all_to_all(
        jnp.broadcast_to(panel[None], (groups, rows, width)), "x", 0, 0, tiled=True
    ).reshape(groups * rows, width)

    terms = align(meta, panels, database, other, slots)

    parts = lax.all_to_all(terms.reshape(groups, rows, width), "x", 0, 0, tiled=True)
    summed = jnp.sum(parts.astype(jnp.float32), axis=0).astype(jnp.bfloat16)
    summed = summed.reshape(deep // 2, 2, tile // 2, width)
    kept = lax.dynamic_index_in_dim(summed, core, 1, keepdims=False)
    given = lax.dynamic_index_in_dim(summed, 1 - core, 1, keepdims=False)
    taken = sibling(given)
    column = jnp.where(core == 0, jnp.stack([kept, taken], 1), jnp.stack([taken, kept], 1))
    rest = ("zh", "y", "zl")
    pieces = lax.all_to_all(column.reshape(-1, 4, width), rest, 0, 0, tiled=True)
    return jnp.sum(pieces.astype(jnp.float32), axis=0).astype(jnp.bfloat16)


def solution(mesh):
    fine = Mesh(mesh.devices.reshape(4, 4, 8, 2, 2), BLK + SHARD)
    both = BLK + SHARD
    in_specs = (P(BLK, None), P(both, None), P(both, None, None), P(both, None, None), P(both))
    return jax.shard_map(
        on_device, mesh=fine, in_specs=in_specs, out_specs=P(both, None), check_vma=False
    )
```

time: 1240 us -> 161 us (0.13)
  the two profiles are of different devices: /device:TPU:2 before, /device:TPU:1 now
where the time goes in v1:
time: 161 us
  blocking collectives  64.4 us (40%)
  waiting for transfers between devices  42.2 us (26%)
  starting transfers between devices  29.6 us (18%)
  Pallas kernels  17 us (11%)
  local copies, waits for them, and re-layouts  4.87 us (3%)
  other arithmetic  1.9 us (1%)
    all_to_all x1, blocking collectives, on_device(): lax.all_to_all(column.reshape(-1, 4, width), rest, 0, 0, tiled=True)  32.5 us
    all_to_all x1, blocking collectives, on_device(): lax.all_to_all(terms.reshape(groups, rows, width), 'x', 0, 0, tiled=True)  31.9 us
    all_to_all x1, waiting for transfers between devices, on_device(): lax.all_to_all(jnp.broadcast_to(panel[None], (groups, rows, width)), 'x',...  26.6 us
    pallas_call x1, Pallas kernels, align(): pl.pallas_call(functools.partial(align_kernel, width ** (-0.5), tiles, sl...  17 us
    ppermute x4, starting transfers between devices, sibling(): return lax.ppermute(value, 'c', [(0, 1), (1, 0)])  14.6 us
    all_to_all x1, waiting for transfers between devices, on_device(): lax.all_to_all(jnp.broadcast_to(half[None], (deep, tile // 2, width)), 'z...  13.6 us
    all_to_all x1, starting transfers between devices, on_device(): lax.all_to_all(jnp.broadcast_to(half[None], (deep, tile // 2, width)), 'z...  10.8 us
    all_to_all x1, starting transfers between devices, on_device(): lax.all_to_all(jnp.broadcast_to(panel[None], (groups, rows, width)), 'x',...  4.14 us
  transfers between devices with their start and end apart: 6, of which 4 were waited for; matrix products, arithmetic and copies ran while one was open for 1% of the time, Pallas kernels for 0%

profile of v1, /device:TPU:1, one launch (start us, length us, event | category | flops | bytes accessed | tf_op | source)
XLA Modules:
  0.0 160.8 jit_solution(4808924954291260004)
XLA Ops:
  0.0 1.1 reshape.42
  1.1 0.3 copy.13
  1.3 0.3 constant_dynamic-slice_fusion.2
  1.7 0.9 broadcast_in_dim.18
  2.6 10.8 %all-to-all-start = ((bf16[4,64,1280]{2,1,0:T(8,128)(2,1)}), bf16[4,64,1280]{2,1,0:T(8,128)(2,1)S(1)}, u32[]{:S(2)}, u32[]{:S(2)}) async-start(bf16[4,64,1280]{2,1,0:T(8,128)(2,1)} %broadcast_in_dim.18), calls=%async_computation | async-start | bytes 1310720 | tf_op jit(solution)/shard_map/all_to_all | solution.py:160
  13.4 13.6 %all-to-all-done = bf16[4,64,1280]{2,1,0:T(8,128)(2,1)S(1)} async-done(((bf16[4,64,1280]{2,1,0:T(8,128)(2,1)}), bf16[4,64,1280]{2,1,0:T(8,128)(2,1)S(1)}, u32[]{:S(2)}, u32[]{:S(2)}) %all-to-all-start) | async-done | bytes 655392 | tf_op jit(solution)/shard_map/all_to_all | solution.py:160
  27.1 4.6 %collective-permute-start.1 = (bf16[2,64,1280]{2,1,0:T(8,128)(2,1)S(1)}, bf16[2,64,1280]{2,1,0:T(8,128)(2,1)S(1)}, u32[]{:S(2)}, u32[]{:S(2)}) collective-permute-start(bf16[2,64,1280]{2,1,0:T(8,128)(2,1)S(1)} %get-tuple-element.8), channel_id=1, source_target_pairs={{0,1},{1,0},{2,3},{3,2},{4,5},{5,4},{6,7},{7,6},{8,9},{9,8},{10,11... | collective-permute-start | bytes 983048 | tf_op jit(solution)/shard_map/ppermute | solution.py:138
  31.7 1.9 %collective-permute-start.2 = (bf16[768,1280]{1,0:T(8,128)(2,1)}, bf16[768,1280]{1,0:T(8,128)(2,1)}, u32[]{:S(2)}, u32[]{:S(2)}) collective-permute-start(bf16[768,1280]{1,0:T(8,128)(2,1)} %own_ref.1), channel_id=1, source_target_pairs={{0,1},{1,0},{2,3},{3,2},{4,5},{5,4},{6,7},{7,6},{8,9},{9,8},{10,11... | collective-permute-start | bytes 5898248 | tf_op jit(solution)/shard_map/ppermute | solution.py:138
  33.6 0.0 collective-permute-done.1
  33.6 0.1 maximum_select_fusion
  33.7 1.7 %broadcast_in_dim.19 = bf16[4,256,1280]{2,1,0:T(8,128)(2,1)} broadcast(bf16[256,1280]{1,0:T(8,128)(2,1)S(1)} %bitcast.23), dimensions={1,2} | broadcast | bytes 3276800 | tf_op jit(solution)/shard_map/broadcast_in_dim | solution.py:172
  35.4 0.0 copy-start
  35.4 0.0 copy-start.1
  35.4 4.1 %all-to-all-start.1 = ((bf16[4,256,1280]{2,1,0:T(8,128)(2,1)}), bf16[4,256,1280]{2,1,0:T(8,128)(2,1)S(1)}, u32[]{:S(2)}, u32[]{:S(2)}) async-start(bf16[4,256,1280]{2,1,0:T(8,128)(2,1)} %broadcast_in_dim.19), calls=%async_computation.1 | async-start | bytes 5242880 | tf_op jit(solution)/shard_map/all_to_all | solution.py:171
  40.2 0.0 copy-done
  40.2 0.1 copy.11
  40.3 0.1 reshape.40
  40.4 0.0 copy-done.1
  40.4 0.1 copy.12
  40.5 0.1 reshape.41
  40.6 0.1 pad_add_fusion.1
  40.7 2.7 %collective-permute-start = (s32[128]{0:T(128)S(1)}, s32[128]{0:T(128)S(1)}, u32[]{:S(2)}, u32[]{:S(2)}) collective-permute-start(s32[128]{0:T(128)S(1)} %pad.4), channel_id=1, source_target_pairs={{0,1},{1,0},{2,3},{3,2},{4,5},{5,4},{6,7},{7,6},{8,9},{9,8},{10,11... | collective-permute-start | bytes 1544 | tf_op jit(solution)/shard_map/ppermute | solution.py:138
  43.3 0.8 collective-permute-done
  44.2 0.0 collective-permute-done.2.other_ref
  44.2 26.6 %all-to-all-done.1 = bf16[4,256,1280]{2,1,0:T(8,128)(2,1)S(1)} async-done(((bf16[4,256,1280]{2,1,0:T(8,128)(2,1)}), bf16[4,256,1280]{2,1,0:T(8,128)(2,1)S(1)}, u32[]{:S(2)}, u32[]{:S(2)}) %all-to-all-start.1) | async-done | bytes 2621472 | tf_op jit(solution)/shard_map/all_to_all | solution.py:171
  70.8 17.0 %align.1 = bf16[1024,1280]{1,0:T(8,128)(2,1)S(1)} custom-call(s32[256]{0:T(256)S(1)} %pad_add_fusion.meta, bf16[1024,1280]{1,0:T(8,128)(2,1)S(1)} %bitcast.20, bf16[768,1280]{1,0:T(8,128)(2,1)} %own_ref.1, bf16[768,1280]{1,0:T(8,128)(2,1)} %collective-permute-done.2.other_ref), custom_call_target="tpu_custom_call" | custom-call | flops 8053063680 | bytes 12582912 | tf_op jit(solution)/shard_map/align/pallas_call | solution.py:112
  87.8 31.9 %all_to_all.20 = bf16[4,256,1280]{2,1,0:T(8,128)(2,1)S(1)} all-to-all(bf16[4,256,1280]{2,1,0:T(8,128)(2,1)S(1)} %bitcast.21), channel_id=1, replica_groups=mesh['x'=4,'zh'=4,'y'=8,'zl'=2,'c'=2] {'x'}, dimensions={0} | all-to-all | bytes 5242880 | tf_op jit(solution)/shard_map/all_to_all | solution.py:177
  119.7 0.8 reduce_sum.24
  120.5 0.1 constant_dynamic-slice_fusion
  120.6 5.4 %collective-permute-start.3 = (bf16[2,64,1280]{2,1,0:T(8,128)(2,1)S(1)}, bf16[2,64,1280]{2,1,0:T(8,128)(2,1)S(1)}, u32[]{:S(2)}, u32[]{:S(2)}) collective-permute-start(bf16[2,64,1280]{2,1,0:T(8,128)(2,1)S(1)} %get-tuple-element.6), channel_id=1, source_target_pairs={{0,1},{1,0},{2,3},{3,2},{4,5},{5,4},{6,7},{7,6},{8,9},{9,8},{10,11... | collective-permute-start | bytes 983048 | tf_op jit(solution)/shard_map/ppermute | solution.py:138
  126.0 1.2 collective-permute-done.3
  127.2 0.1 maximum_select_fusion.1
  127.3 0.2 select_n.40
  127.4 32.5 %all_to_all.21 = bf16[64,4,1280]{2,1,0:T(4,128)(2,1)S(1)} all-to-all(bf16[64,4,1280]{2,1,0:T(4,128)(2,1)S(1)} %select_n.40), channel_id=1, replica_groups=mesh['x'=4,'zh'=4,'y'=8,'zl'=2,'c'=2] {'zh','y','zl'}, dimensions={0} | all-to-all | bytes 1310720 | tf_op jit(solution)/shard_map/all_to_all | solution.py:185
  159.9 0.9 reduce_sum.25
  (4 shorter events, 0.1 us)
Async XLA Ops:
  2.6 24.4 %all-to-all-start = ((bf16[4,64,1280]{2,1,0:T(8,128)(2,1)}), bf16[4,64,1280]{2,1,0:T(8,128)(2,1)S(1)}, u32[]{:S(2)}, u32[]{:S(2)}) async-start(bf16[4,64,1280]{2,1,0:T(8,128)(2,1)} %broadcast_in_dim.18), calls=%async_computation | async-start | bytes 1310720 | tf_op jit(solution)/shard_map/all_to_all | solution.py:160
  27.1 6.5 %collective-permute-start.1 = (bf16[2,64,1280]{2,1,0:T(8,128)(2,1)S(1)}, bf16[2,64,1280]{2,1,0:T(8,128)(2,1)S(1)}, u32[]{:S(2)}, u32[]{:S(2)}) collective-permute-start(bf16[2,64,1280]{2,1,0:T(8,128)(2,1)S(1)} %get-tuple-element.8), channel_id=1, source_target_pairs={{0,1},{1,0},{2,3},{3,2},{4,5},{5,4},{6,7},{7,6},{8,9},{9,8},{10,11... | collective-permute-start | bytes 983048 | tf_op jit(solution)/shard_map/ppermute | solution.py:138
  31.7 12.5 %collective-permute-start.2 = (bf16[768,1280]{1,0:T(8,128)(2,1)}, bf16[768,1280]{1,0:T(8,128)(2,1)}, u32[]{:S(2)}, u32[]{:S(2)}) collective-permute-start(bf16[768,1280]{1,0:T(8,128)(2,1)} %own_ref.1), channel_id=1, source_target_pairs={{0,1},{1,0},{2,3},{3,2},{4,5},{5,4},{6,7},{7,6},{8,9},{9,8},{10,11... | collective-permute-start | bytes 5898248 | tf_op jit(solution)/shard_map/ppermute | solution.py:138
  35.4 4.8 %copy-start = (s32[1,24,2]{1,2,0:T(2,128)S(1)}, s32[1,24,2]{1,2,0:T(2,128)}, u32[]{:S(2)}) copy-start(s32[1,24,2]{1,2,0:T(2,128)} %param.7) | copy-start | bytes 580
  35.4 5.0 %copy-start.1 = (s32[1,24,2]{1,2,0:T(2,128)S(1)}, s32[1,24,2]{1,2,0:T(2,128)}, u32[]{:S(2)}) copy-start(s32[1,24,2]{1,2,0:T(2,128)} %param.8) | copy-start | bytes 580
  35.4 35.4 %all-to-all-start.1 = ((bf16[4,256,1280]{2,1,0:T(8,128)(2,1)}), bf16[4,256,1280]{2,1,0:T(8,128)(2,1)S(1)}, u32[]{:S(2)}, u32[]{:S(2)}) async-start(bf16[4,256,1280]{2,1,0:T(8,128)(2,1)} %broadcast_in_dim.19), calls=%async_computation.1 | async-start | bytes 5242880 | tf_op jit(solution)/shard_map/all_to_all | solution.py:171
  40.7 3.5 %collective-permute-start = (s32[128]{0:T(128)S(1)}, s32[128]{0:T(128)S(1)}, u32[]{:S(2)}, u32[]{:S(2)}) collective-permute-start(s32[128]{0:T(128)S(1)} %pad.4), channel_id=1, source_target_pairs={{0,1},{1,0},{2,3},{3,2},{4,5},{5,4},{6,7},{7,6},{8,9},{9,8},{10,11... | collective-permute-start | bytes 1544 | tf_op jit(solution)/shard_map/ppermute | solution.py:138
  120.6 6.6 %collective-permute-start.3 = (bf16[2,64,1280]{2,1,0:T(8,128)(2,1)S(1)}, bf16[2,64,1280]{2,1,0:T(8,128)(2,1)S(1)}, u32[]{:S(2)}, u32[]{:S(2)}) collective-permute-start(bf16[2,64,1280]{2,1,0:T(8,128)(2,1)S(1)} %get-tuple-element.6), channel_id=1, source_target_pairs={{0,1},{1,0},{2,3},{3,2},{4,5},{5,4},{6,7},{7,6},{8,9},{9,8},{10,11... | collective-permute-start | bytes 983048 | tf_op jit(solution)/shard_map/ppermute | solution.py:138

commit v2 on v1

v2 whole, which is shorter than its diff:
```python
import functools

import jax
import jax.numpy as jnp
from jax import lax
from jax.experimental import pallas as pl
from jax.experimental.pallas import tpu as pltpu
from jax.sharding import Mesh
from jax.sharding import PartitionSpec as P

TILE = 128
BLK = ("x", "zh")
SHARD = ("y", "zl", "c")
HALF = 2
CHUNK = 256
UNROLL = 4


def pair_weight(scores, rows, cols, row_count, col_count):
    valid = (rows < row_count) & (cols < col_count)
    masked = jnp.where(valid, scores, -1e30)
    row_max = jnp.max(masked, axis=1, keepdims=True)
    row_lse = row_max + jnp.log(jnp.sum(jnp.exp(masked - row_max), axis=1, keepdims=True))
    col_max = jnp.max(masked, axis=0, keepdims=True)
    col_lse = col_max + jnp.log(jnp.sum(jnp.exp(masked - col_max), axis=0, keepdims=True))
    weight = jnp.where(valid, jnp.exp(scores - 0.5 * (row_lse + col_lse)), 0.0)
    return weight.astype(jnp.bfloat16)


def align_kernel(
    scale, tiles, slots, meta, group, q_ref, own_ref, other_ref, out_ref,
    base_rows, scores, weights, listed, arrived,
):
    stride = meta.shape[0] // 2
    core = meta[4 * slots + 1]
    deep = meta[4 * slots + 2]
    width = tiles * TILE
    chunks = 2 * width // CHUNK

    def copy(index):
        source = own_ref if index < chunks // 2 else other_ref
        first = (index % (chunks // 2)) * CHUNK
        return pltpu.make_async_copy(
            source.at[pl.ds(first, CHUNK)],
            base_rows.at[pl.ds(index * CHUNK, CHUNK)],
            arrived.at[index],
        )

    for index in range(chunks):
        copy(index).start()
    weights[...] = jnp.zeros_like(weights)

    count = jnp.int32(0)
    for side in range(2):
        base = side * stride

        def look(slot, count, base=base, side=side):
            query_tile = meta[base + 2 * slot]
            near = (query_tile & 3) ^ deep
            mine = ((query_tile >> 2) == group[0]) & ((near >> 1) == core)

            @pl.when(mine)
            def _():
                listed[0, count] = near & 1
                listed[1, count] = meta[base + 2 * slot + 1] + side * tiles
                listed[2, count] = meta[base + 2 * slots + 2 * slot]
                listed[3, count] = meta[base + 2 * slots + 2 * slot + 1]

            return count + mine.astype(jnp.int32)

        count = lax.fori_loop(0, meta[base + 4 * slots], look, count)
    for extra in range(UNROLL - 1):
        for field in range(4):
            listed[field, count + extra] = 0

    across = (((1,), (1,)), ((), ()))
    query = q_ref[...]
    for index in range(chunks):
        copy(index).wait()
        span = pl.ds(index * CHUNK, CHUNK)
        scores[:, span] = (
            lax.dot_general(
                query, base_rows[span, :], across, preferred_element_type=jnp.float32
            )
            * scale
        )

    rows = lax.broadcasted_iota(jnp.int32, (TILE, TILE), 0)
    cols = lax.broadcasted_iota(jnp.int32, (TILE, TILE), 1)

    def batch(index, carry):
        made = []
        for k in range(UNROLL):
            slot = index * UNROLL + k
            at_row = pl.ds(pl.multiple_of(listed[0, slot] * TILE, TILE), TILE)
            at_col = pl.ds(pl.multiple_of(listed[1, slot] * TILE, TILE), TILE)
            weight = pair_weight(scores[at_row, at_col], rows, cols, listed[2, slot], listed[3, slot])
            made.append((at_row, at_col, weight))
        for at_row, at_col, weight in made:
            weights[at_row, at_col] += weight.astype(jnp.float32)
        return carry

    lax.fori_loop(0, (count + UNROLL - 1) // UNROLL, batch, 0)

    both = HALF * TILE
    place = lax.broadcasted_iota(jnp.int32, (both, both), 0)
    row = lax.broadcasted_iota(jnp.int32, (both, both), 1)
    wanted = (place & ~127) + ((place & 63) >> 2) * 8 + ((place >> 6) & 1) * 4 + (place & 3)
    sort = (row == wanted).astype(jnp.bfloat16)
    weight = jnp.dot(
        sort, weights[...].astype(jnp.bfloat16), preferred_element_type=jnp.float32
    ).astype(jnp.bfloat16)
    out_ref[...] = jnp.dot(
        weight, base_rows[...], preferred_element_type=jnp.float32
    ).astype(out_ref.dtype)


def align(meta, group, queries, own, other, slots):
    rows, width = queries.shape
    tiles = own.shape[0] // TILE
    columns = 2 * own.shape[0]
    whole = pl.BlockSpec(memory_space=pl.ANY)
    block = pl.BlockSpec((rows, width), lambda i, meta, group: (0, 0))
    return pl.pallas_call(
        functools.partial(align_kernel, width ** (-0.5), tiles, slots),
        grid_spec=pltpu.PrefetchScalarGridSpec(
            num_scalar_prefetch=2,
            grid=(1,),
            in_specs=[block, whole, whole],
            out_specs=block,
            scratch_shapes=[
                pltpu.VMEM((columns, width), jnp.bfloat16),
                pltpu.VMEM((rows, columns), jnp.float32),
                pltpu.VMEM((rows, columns), jnp.float32),
                pltpu.SMEM((4, 2 * slots + UNROLL), jnp.int32),
                pltpu.SemaphoreType.DMA((columns // CHUNK,)),
            ],
        ),
        out_shape=jax.ShapeDtypeStruct((rows, width), jnp.bfloat16),
        compiler_params=pltpu.CompilerParams(vmem_limit_bytes=24 * 1024 * 1024),
        cost_estimate=pl.CostEstimate(
            flops=4 * rows * columns * width, bytes_accessed=6 * 1024 * 1024, transcendentals=0
        ),
        name="align",
    )(meta, group, queries, own, other)


def sibling(value):
    return lax.ppermute(value, "c", [(0, 1), (1, 0)])


def turned(value, distance):
    groups = lax.axis_size("x")
    return lax.ppermute(value, "x", [(i, (i + distance) % groups) for i in range(groups)])


def on_device(queries, database, pair_tiles, pair_lengths, live_pairs):
    tile, width = queries.shape
    slots = pair_tiles.shape[1]
    core = lax.axis_index("c").astype(jnp.int32)
    deep = lax.axis_index("zh").astype(jnp.int32)
    here = lax.axis_index("x").astype(jnp.int32)
    groups = lax.axis_size("x")
    places = lax.axis_size("zh")

    near = [(2 * z + c, 2 * (z ^ (1 + c)) + c) for z in range(places) for c in range(2)]
    far = [(2 * z + 1, 2 * (z ^ 3) + 1) for z in range(places)]
    first = lax.ppermute(queries, ("zh", "c"), near)
    second = lax.ppermute(queries, ("zh", "c"), far)
    panel = jnp.concatenate(
        [jnp.where(core == 0, queries, first), jnp.where(core == 0, first, second)]
    )

    other = sibling(database)
    own_meta = jnp.concatenate(
        [pair_tiles.reshape(-1), pair_lengths.reshape(-1), live_pairs, core[None], deep[None]]
    )
    own_meta = jnp.pad(own_meta, (0, 128 - own_meta.shape[0]))
    meta = jnp.concatenate([own_meta, sibling(own_meta)])

    def terms_of(rows, distance):
        group = lax.rem(here - distance + groups, groups)
        return align(meta, group[None], rows, database, other, slots)

    distances = (1, 3, 2)
    panels = [turned(panel, d) for d in distances]
    parts = [terms_of(panel, 0)]
    for distance, rows in zip(distances, panels, strict=True):
        parts.append(turned(terms_of(rows, distance), -distance))

    parts = [part.reshape(HALF, 2, tile // 2, width) for part in parts]

    def half(which):
        return sum(
            lax.dynamic_index_in_dim(part, which, 1, keepdims=False).astype(jnp.float32)
            for part in parts
        ).astype(jnp.bfloat16)

    taken = sibling(half(1 - core))
    kept = half(core)
    same = (deep >> 1) == core
    column = jnp.stack([jnp.where(same, kept, taken), jnp.where(same, taken, kept)])
    column = jnp.where((deep & 1) == 0, column, column[:, ::-1])

    pieces = lax.all_to_all(column.reshape(-1, 4, width), ("zh", "y", "zl"), 0, 0, tiled=True)
    return jnp.sum(pieces.astype(jnp.float32), axis=0).astype(jnp.bfloat16)


def solution(mesh):
    fine = Mesh(mesh.devices.reshape(4, 4, 8, 2, 2), BLK + SHARD)
    both = BLK + SHARD
    in_specs = (P(BLK, None), P(both, None), P(both, None, None), P(both, None, None), P(both))
    return jax.shard_map(
        on_device, mesh=fine, in_specs=in_specs, out_specs=P(both, None), check_vma=False
    )
```

time: 161 us -> 145 us (0.901)
  blocking collectives: 64.4 us -> 25.9 us
  Pallas kernels: 17 us -> 34.3 us
  starting transfers between devices: 29.6 us -> 39.1 us
  local copies, waits for them, and re-layouts: 4.87 us -> 0.62 us
  waiting for transfers between devices: 42.2 us -> 38.4 us
  other arithmetic: 1.9 us -> 3.94 us
    all_to_all x2 -> x0, waiting for transfers between devices: 40.2 us -> none  [the longest x1 26.6 us: on_device(): lax.all_to_all(jnp.broadcast_to(panel[None], (groups, rows, width)), 'x',...]
    all_to_all x2 -> x1, blocking collectives: 64.4 us -> 25.9 us  [on_device(): lax.all_to_all(column.reshape(-1, 4, width), ('zh', 'y', 'zl'), 0, 0, til...]
    ppermute x0 -> x8, waiting for transfers between devices: none -> 35.7 us  [the longest x6 24.3 us: turned(): lax.ppermute(value, 'x', [(i, (i + distance) % groups) for i in range(gro...]
    ppermute x0 -> x8, starting transfers between devices: none -> 26.5 us  [the longest x6 19.3 us: turned(): lax.ppermute(value, 'x', [(i, (i + distance) % groups) for i in range(gro...]
    pallas_call x1 -> x4, Pallas kernels: 17 us -> 34.3 us  [align(): pl.pallas_call(functools.partial(align_kernel, width ** (-0.5), tiles, sl...]
    all_to_all x2 -> x0, starting transfers between devices: 15 us -> none  [the longest x1 10.8 us: on_device(): lax.all_to_all(jnp.broadcast_to(half[None], (deep, tile // 2, width)), 'z...]
    broadcast_in_dim x2 -> x0, local copies, waits for them, and re-layouts: 2.58 us -> none  [the longest x1 1.69 us: on_device(): jnp.broadcast_to(panel[None], (groups, rows, width))]
    ppermute x4 -> x3, starting transfers between devices: 14.6 us -> 12.6 us  [sibling(): return lax.ppermute(value, 'c', [(0, 1), (1, 0)])]
  transfers between devices with their start and end apart: 6 -> 11, of which waited for: 4 -> 5; matrix products, arithmetic and copies ran while one was open for 1% -> 0% of each run, Pallas kernels for 0% -> 24%
where the time goes in v2:
time: 145 us; the launch traced here: 143 us
  starting transfers between devices  39.1 us (27%)
  waiting for transfers between devices  38.4 us (26%)
  Pallas kernels  34.3 us (24%)
  blocking collectives  25.9 us (18%)
  other arithmetic  3.94 us (3%)
    pallas_call x4, Pallas kernels, align(): pl.pallas_call(functools.partial(align_kernel, width ** (-0.5), tiles, sl...  34.3 us
    all_to_all x1, blocking collectives, on_device(): lax.all_to_all(column.reshape(-1, 4, width), ('zh', 'y', 'zl'), 0, 0, til...  25.9 us
    ppermute x6, waiting for transfers between devices, turned(): lax.ppermute(value, 'x', [(i, (i + distance) % groups) for i in range(gro...  24.3 us
    ppermute x6, starting transfers between devices, turned(): lax.ppermute(value, 'x', [(i, (i + distance) % groups) for i in range(gro...  19.3 us
    ppermute x3, starting transfers between devices, sibling(): return lax.ppermute(value, 'c', [(0, 1), (1, 0)])  12.6 us
    ppermute x1, waiting for transfers between devices, on_device(): first = lax.ppermute(queries, ('zh', 'c'), near)  11.4 us
    ppermute x1, starting transfers between devices, on_device(): first = lax.ppermute(queries, ('zh', 'c'), near)  5.26 us
  transfers between devices with their start and end apart: 11, of which 5 were waited for; matrix products, arithmetic and copies ran while one was open for 0% of the time, Pallas kernels for 24%

profile of v2, /device:TPU:1, one launch (start us, length us, event | category | flops | bytes accessed | tf_op | source)
XLA Modules:
  0.0 143.2 jit_solution(6139121525330569276)
XLA Ops:
  0.0 8.8 %collective-permute-start.3 = (bf16[768,1280]{1,0:T(8,128)(2,1)}, bf16[768,1280]{1,0:T(8,128)(2,1)}, u32[]{:S(2)}, u32[]{:S(2)}) collective-permute-start(bf16[768,1280]{1,0:T(8,128)(2,1)} %own_ref.7), channel_id=1, source_target_pairs={{0,1},{1,0},{2,3},{3,2},{4,5},{5,4},{6,7},{7,6},{8,9},{9,8},{10,11... | collective-permute-start | bytes 5898248 | tf_op jit(solution)/shard_map/ppermute | solution.py:149
  8.8 5.3 %collective-permute-start.1 = (bf16[128,1280]{1,0:T(8,128)(2,1)}, bf16[128,1280]{1,0:T(8,128)(2,1)S(1)}, u32[]{:S(2)}, u32[]{:S(2)}) collective-permute-start(bf16[128,1280]{1,0:T(8,128)(2,1)} %param.5), channel_id=1, source_target_pairs={{0,32},{1,65},{32,0},{33,97},{64,96},{65,1},{96,64},{97,33},{2,34}... | collective-permute-start | bytes 983048 | tf_op jit(solution)/shard_map/ppermute | solution.py:168
  14.1 1.9 %collective-permute-start.2 = (bf16[128,1280]{1,0:T(8,128)(2,1)}, bf16[128,1280]{1,0:T(8,128)(2,1)S(1)}, u32[]{:S(2)}, u32[]{:S(2)}) collective-permute-start(bf16[128,1280]{1,0:T(8,128)(2,1)} %param.5), channel_id=1, source_target_pairs={{1,97},{33,65},{65,33},{97,1},{3,99},{35,67},{67,35},{99,3},{5,101... | collective-permute-start | bytes 983048 | tf_op jit(solution)/shard_map/ppermute | solution.py:169
  16.0 0.0 copy-start.1
  16.0 0.0 copy-start.2
  16.0 0.0 copy-start
  16.0 11.4 %collective-permute-done.1 = bf16[128,1280]{1,0:T(8,128)(2,1)S(1)} collective-permute-done((bf16[128,1280]{1,0:T(8,128)(2,1)}, bf16[128,1280]{1,0:T(8,128)(2,1)S(1)}, u32[]{:S(2)}, u32[]{:S(2)}) %collective-permute-start.1) | collective-permute-done | bytes 327712 | tf_op jit(solution)/shard_map/ppermute | solution.py:168
  27.4 0.0 collective-permute-done.2
  27.4 0.1 broadcast_select_fusion.1
  27.5 5.5 %collective-permute-start.4 = (bf16[256,1280]{1,0:T(8,128)(2,1)S(1)}, bf16[256,1280]{1,0:T(8,128)(2,1)}, u32[]{:S(2)}, u32[]{:S(2)}) collective-permute-start(bf16[256,1280]{1,0:T(8,128)(2,1)S(1)} %pad_maximum_fusion.q_ref), channel_id=1, source_target_pairs={{0,128},{128,256},{256,384},{384,0},{1,129},{129,257},{257,385},{3... | collective-permute-start | bytes 1966088 | tf_op jit(solution)/shard_map/ppermute | solution.py:154
  33.1 3.2 %collective-permute-start.6 = (bf16[256,1280]{1,0:T(8,128)(2,1)S(1)}, bf16[256,1280]{1,0:T(8,128)(2,1)}, u32[]{:S(2)}, u32[]{:S(2)}) collective-permute-start(bf16[256,1280]{1,0:T(8,128)(2,1)S(1)} %pad_maximum_fusion.q_ref), channel_id=1, source_target_pairs={{0,384},{128,0},{256,128},{384,256},{1,385},{129,1},{257,129},{385... | collective-permute-start | bytes 1966088 | tf_op jit(solution)/shard_map/ppermute | solution.py:154
  36.2 3.6 %collective-permute-start.8 = (bf16[256,1280]{1,0:T(8,128)(2,1)S(1)}, bf16[256,1280]{1,0:T(8,128)(2,1)S(1)}, u32[]{:S(2)}, u32[]{:S(2)}) collective-permute-start(bf16[256,1280]{1,0:T(8,128)(2,1)S(1)} %pad_maximum_fusion.q_ref), channel_id=1, source_target_pairs={{0,256},{128,384},{256,0},{384,128},{1,257},{129,385},{257,1},{385... | collective-permute-start | bytes 1966088 | tf_op jit(solution)/shard_map/ppermute | solution.py:154
  40.5 0.0 copy-done.1
  40.5 0.1 copy.12
  40.6 0.1 reshape.37
  40.7 0.0 copy-done.2
  40.7 0.1 copy.13
  40.8 0.1 reshape.38
  40.9 0.1 concatenate.9
  41.0 1.9 %collective-permute-start = (s32[128]{0:T(128)S(1)}, s32[128]{0:T(128)S(1)}, u32[]{:S(2)}, u32[]{:S(2)}) collective-permute-start(s32[128]{0:T(128)S(1)} %pad.4), channel_id=1, source_target_pairs={{0,1},{1,0},{2,3},{3,2},{4,5},{5,4},{6,7},{7,6},{8,9},{9,8},{10,11... | collective-permute-start | bytes 1544 | tf_op jit(solution)/shard_map/ppermute | solution.py:149
  43.0 1.1 collective-permute-done
  44.0 18.4 %collective-permute-done.4.q_ref = bf16[256,1280]{1,0:T(8,128)(2,1)} collective-permute-done((bf16[256,1280]{1,0:T(8,128)(2,1)S(1)}, bf16[256,1280]{1,0:T(8,128)(2,1)}, u32[]{:S(2)}, u32[]{:S(2)}) %collective-permute-start.4) | collective-permute-done | bytes 655392 | tf_op jit(solution)/shard_map/ppermute | solution.py:154
  62.5 0.0 collective-permute-done.3.other_ref
  62.5 0.0 copy-done
  62.5 9.2 %align.5 = bf16[256,1280]{1,0:T(8,128)(2,1)} custom-call(s32[256]{0:T(256)S(1)} %pad_add_fusion.meta, s32[1]{0:T(128)} %bitcast.4.group, bf16[256,1280]{1,0:T(8,128)(2,1)} %collective-permute-done.4.q_ref, bf16[768,1280]{1,0:T(8,128)(2,1)S(1)} %copy-done, bf16[768,1280]{1,0:T(8,128)(2,1)} %collective-permute-done.3.other_ref), custom_call_target="tpu_custom_call" | custom-call | flops 2013265920 | bytes 6291456 | tf_op jit(solution)/shard_map/align/pallas_call | solution.py:124
  71.7 1.9 %collective-permute-start.5 = (bf16[256,1280]{1,0:T(8,128)(2,1)}, bf16[256,1280]{1,0:T(8,128)(2,1)}, u32[]{:S(2)}, u32[]{:S(2)}) collective-permute-start(bf16[256,1280]{1,0:T(8,128)(2,1)} %align.5), channel_id=1, source_target_pairs={{0,384},{128,0},{256,128},{384,256},{1,385},{129,1},{257,129},{385... | collective-permute-start | bytes 1966088 | tf_op jit(solution)/shard_map/ppermute | solution.py:154
  73.6 0.0 collective-permute-done.6.q_ref
  73.6 9.2 %align.6 = bf16[256,1280]{1,0:T(8,128)(2,1)} custom-call(s32[256]{0:T(256)S(1)} %pad_add_fusion.meta, s32[1]{0:T(128)} %bitcast.6.group, bf16[256,1280]{1,0:T(8,128)(2,1)} %collective-permute-done.6.q_ref, bf16[768,1280]{1,0:T(8,128)(2,1)S(1)} %copy-done, bf16[768,1280]{1,0:T(8,128)(2,1)} %collective-permute-done.3.other_ref), custom_call_target="tpu_custom_call" | custom-call | flops 2013265920 | bytes 6291456 | tf_op jit(solution)/shard_map/align/pallas_call | solution.py:124
  82.8 3.1 %collective-permute-start.7 = (bf16[256,1280]{1,0:T(8,128)(2,1)}, bf16[256,1280]{1,0:T(8,128)(2,1)}, u32[]{:S(2)}, u32[]{:S(2)}) collective-permute-start(bf16[256,1280]{1,0:T(8,128)(2,1)} %align.6), channel_id=1, source_target_pairs={{0,128},{128,256},{256,384},{384,0},{1,129},{129,257},{257,385},{3... | collective-permute-start | bytes 1966088 | tf_op jit(solution)/shard_map/ppermute | solution.py:154
  86.0 0.0 collective-permute-done.8.q_ref
  86.0 8.2 %align.7 = bf16[256,1280]{1,0:T(8,128)(2,1)} custom-call(s32[256]{0:T(256)S(1)} %pad_add_fusion.meta, s32[1]{0:T(128)} %bitcast.8.group, bf16[256,1280]{1,0:T(8,128)(2,1)S(1)} %collective-permute-done.8.q_ref, bf16[768,1280]{1,0:T(8,128)(2,1)S(1)} %copy-done, bf16[768,1280]{1,0:T(8,128)(2,1)} %collective-permute-done.3.other_ref), custom_call_target="tpu_custom_call" | custom-call | flops 2013265920 | bytes 6291456 | tf_op jit(solution)/shard_map/align/pallas_call | solution.py:124
  94.2 1.9 %collective-permute-start.9 = (bf16[256,1280]{1,0:T(8,128)(2,1)}, bf16[256,1280]{1,0:T(8,128)(2,1)}, u32[]{:S(2)}, u32[]{:S(2)}) collective-permute-start(bf16[256,1280]{1,0:T(8,128)(2,1)} %align.7), channel_id=1, source_target_pairs={{0,256},{128,384},{256,0},{384,128},{1,257},{129,385},{257,1},{385... | collective-permute-start | bytes 1966088 | tf_op jit(solution)/shard_map/ppermute | solution.py:154
  96.1 7.8 %align.4 = bf16[256,1280]{1,0:T(8,128)(2,1)S(1)} custom-call(s32[256]{0:T(256)S(1)} %pad_add_fusion.meta, s32[1]{0:T(128)} %bitcast.2.group, bf16[256,1280]{1,0:T(8,128)(2,1)S(1)} %pad_maximum_fusion.q_ref, bf16[768,1280]{1,0:T(8,128)(2,1)S(1)} %copy-done, bf16[768,1280]{1,0:T(8,128)(2,1)} %collective-permute-done.3.other_ref), custom_call_target="tpu_custom_call" | custom-call | flops 2013265920 | bytes 6291456 | tf_op jit(solution)/shard_map/align/pallas_call | solution.py:124
  103.9 0.0 collective-permute-done.5
  103.9 5.9 %collective-permute-done.7 = bf16[256,1280]{1,0:T(8,128)(2,1)} collective-permute-done((bf16[256,1280]{1,0:T(8,128)(2,1)}, bf16[256,1280]{1,0:T(8,128)(2,1)}, u32[]{:S(2)}, u32[]{:S(2)}) %collective-permute-start.7) | collective-permute-done | bytes 655392 | tf_op jit(solution)/shard_map/ppermute | solution.py:154
  109.8 0.0 collective-permute-done.9
  109.8 1.3 fusion.1
  111.1 1.9 %collective-permute-start.10 = (bf16[2,64,1280]{2,1,0:T(8,128)(2,1)S(1)}, bf16[2,64,1280]{2,1,0:T(8,128)(2,1)S(1)}, u32[]{:S(2)}, u32[]{:S(2)}) collective-permute-start(bf16[2,64,1280]{2,1,0:T(8,128)(2,1)S(1)} %fusion.1), channel_id=1, source_target_pairs={{0,1},{1,0},{2,3},{3,2},{4,5},{5,4},{6,7},{7,6},{8,9},{9,8},{10,11... | collective-permute-start | bytes 983048 | tf_op jit(solution)/shard_map/ppermute | solution.py:149
  113.0 1.6 %collective-permute-done.10 = bf16[2,64,1280]{2,1,0:T(8,128)(2,1)S(1)} collective-permute-done((bf16[2,64,1280]{2,1,0:T(8,128)(2,1)S(1)}, bf16[2,64,1280]{2,1,0:T(8,128)(2,1)S(1)}, u32[]{:S(2)}, u32[]{:S(2)}) %collective-permute-start.10) | collective-permute-done | bytes 327712 | tf_op jit(solution)/shard_map/ppermute | solution.py:149
  114.6 1.4 select_bitcast_fusion.1
  116.1 0.1 pad_maximum_fusion.1
  116.1 0.1 reverse_select_fusion
  116.2 0.2 reshape.43
  116.4 25.9 %all_to_all.5 = bf16[64,4,1280]{2,1,0:T(4,128)(2,1)S(1)} all-to-all(bf16[64,4,1280]{2,1,0:T(4,128)(2,1)S(1)} %reshape.43), channel_id=1, replica_groups=mesh['x'=4,'zh'=4,'y'=8,'zl'=2,'c'=2] {'zh','y','zl'}, dimensions={0} | all-to-all | bytes 1310720 | tf_op jit(solution)/shard_map/all_to_all | solution.py:205
  142.3 0.9 reduce_sum.12
  (4 shorter events, 0.1 us)
Async XLA Ops:
  0.0 62.5 %collective-permute-start.3 = (bf16[768,1280]{1,0:T(8,128)(2,1)}, bf16[768,1280]{1,0:T(8,128)(2,1)}, u32[]{:S(2)}, u32[]{:S(2)}) collective-permute-start(bf16[768,1280]{1,0:T(8,128)(2,1)} %own_ref.7), channel_id=1, source_target_pairs={{0,1},{1,0},{2,3},{3,2},{4,5},{5,4},{6,7},{7,6},{8,9},{9,8},{10,11... | collective-permute-start | bytes 5898248 | tf_op jit(solution)/shard_map/ppermute | solution.py:149
  8.8 18.6 %collective-permute-start.1 = (bf16[128,1280]{1,0:T(8,128)(2,1)}, bf16[128,1280]{1,0:T(8,128)(2,1)S(1)}, u32[]{:S(2)}, u32[]{:S(2)}) collective-permute-start(bf16[128,1280]{1,0:T(8,128)(2,1)} %param.5), channel_id=1, source_target_pairs={{0,32},{1,65},{32,0},{33,97},{64,96},{65,1},{96,64},{97,33},{2,34}... | collective-permute-start | bytes 983048 | tf_op jit(solution)/shard_map/ppermute | solution.py:168
  14.1 13.3 %collective-permute-start.2 = (bf16[128,1280]{1,0:T(8,128)(2,1)}, bf16[128,1280]{1,0:T(8,128)(2,1)S(1)}, u32[]{:S(2)}, u32[]{:S(2)}) collective-permute-start(bf16[128,1280]{1,0:T(8,128)(2,1)} %param.5), channel_id=1, source_target_pairs={{1,97},{33,65},{65,33},{97,1},{3,99},{35,67},{67,35},{99,3},{5,101... | collective-permute-start | bytes 983048 | tf_op jit(solution)/shard_map/ppermute | solution.py:169
  16.0 24.5 %copy-start.1 = (s32[1,24,2]{1,2,0:T(2,128)S(1)}, s32[1,24,2]{1,2,0:T(2,128)}, u32[]{:S(2)}) copy-start(s32[1,24,2]{1,2,0:T(2,128)} %param.7) | copy-start | bytes 580
  16.0 24.7 %copy-start.2 = (s32[1,24,2]{1,2,0:T(2,128)S(1)}, s32[1,24,2]{1,2,0:T(2,128)}, u32[]{:S(2)}) copy-start(s32[1,24,2]{1,2,0:T(2,128)} %param.8) | copy-start | bytes 580
  16.0 46.4 %copy-start = (bf16[768,1280]{1,0:T(8,128)(2,1)S(1)}, bf16[768,1280]{1,0:T(8,128)(2,1)}, u32[]{:S(2)}) copy-start(bf16[768,1280]{1,0:T(8,128)(2,1)} %own_ref.7) | copy-start | bytes 5898244
  27.5 35.0 %collective-permute-start.4 = (bf16[256,1280]{1,0:T(8,128)(2,1)S(1)}, bf16[256,1280]{1,0:T(8,128)(2,1)}, u32[]{:S(2)}, u32[]{:S(2)}) collective-permute-start(bf16[256,1280]{1,0:T(8,128)(2,1)S(1)} %pad_maximum_fusion.q_ref), channel_id=1, source_target_pairs={{0,128},{128,256},{256,384},{384,0},{1,129},{129,257},{257,385},{3... | collective-permute-start | bytes 1966088 | tf_op jit(solution)/shard_map/ppermute | solution.py:154
  33.1 40.6 %collective-permute-start.6 = (bf16[256,1280]{1,0:T(8,128)(2,1)S(1)}, bf16[256,1280]{1,0:T(8,128)(2,1)}, u32[]{:S(2)}, u32[]{:S(2)}) collective-permute-start(bf16[256,1280]{1,0:T(8,128)(2,1)S(1)} %pad_maximum_fusion.q_ref), channel_id=1, source_target_pairs={{0,384},{128,0},{256,128},{384,256},{1,385},{129,1},{257,129},{385... | collective-permute-start | bytes 1966088 | tf_op jit(solution)/shard_map/ppermute | solution.py:154
  36.2 49.7 %collective-permute-start.8 = (bf16[256,1280]{1,0:T(8,128)(2,1)S(1)}, bf16[256,1280]{1,0:T(8,128)(2,1)S(1)}, u32[]{:S(2)}, u32[]{:S(2)}) collective-permute-start(bf16[256,1280]{1,0:T(8,128)(2,1)S(1)} %pad_maximum_fusion.q_ref), channel_id=1, source_target_pairs={{0,256},{128,384},{256,0},{384,128},{1,257},{129,385},{257,1},{385... | collective-permute-start | bytes 1966088 | tf_op jit(solution)/shard_map/ppermute | solution.py:154
  41.0 3.0 %collective-permute-start = (s32[128]{0:T(128)S(1)}, s32[128]{0:T(128)S(1)}, u32[]{:S(2)}, u32[]{:S(2)}) collective-permute-start(s32[128]{0:T(128)S(1)} %pad.4), channel_id=1, source_target_pairs={{0,1},{1,0},{2,3},{3,2},{4,5},{5,4},{6,7},{7,6},{8,9},{9,8},{10,11... | collective-permute-start | bytes 1544 | tf_op jit(solution)/shard_map/ppermute | solution.py:149
  71.7 32.2 %collective-permute-start.5 = (bf16[256,1280]{1,0:T(8,128)(2,1)}, bf16[256,1280]{1,0:T(8,128)(2,1)}, u32[]{:S(2)}, u32[]{:S(2)}) collective-permute-start(bf16[256,1280]{1,0:T(8,128)(2,1)} %align.5), channel_id=1, source_target_pairs={{0,384},{128,0},{256,128},{384,256},{1,385},{129,1},{257,129},{385... | collective-permute-start | bytes 1966088 | tf_op jit(solution)/shard_map/ppermute | solution.py:154
  82.8 26.9 %collective-permute-start.7 = (bf16[256,1280]{1,0:T(8,128)(2,1)}, bf16[256,1280]{1,0:T(8,128)(2,1)}, u32[]{:S(2)}, u32[]{:S(2)}) collective-permute-start(bf16[256,1280]{1,0:T(8,128)(2,1)} %align.6), channel_id=1, source_target_pairs={{0,128},{128,256},{256,384},{384,0},{1,129},{129,257},{257,385},{3... | collective-permute-start | bytes 1966088 | tf_op jit(solution)/shard_map/ppermute | solution.py:154
  94.2 15.6 %collective-permute-start.9 = (bf16[256,1280]{1,0:T(8,128)(2,1)}, bf16[256,1280]{1,0:T(8,128)(2,1)}, u32[]{:S(2)}, u32[]{:S(2)}) collective-permute-start(bf16[256,1280]{1,0:T(8,128)(2,1)} %align.7), channel_id=1, source_target_pairs={{0,256},{128,384},{256,0},{384,128},{1,257},{129,385},{257,1},{385... | collective-permute-start | bytes 1966088 | tf_op jit(solution)/shard_map/ppermute | solution.py:154
  111.1 3.5 %collective-permute-start.10 = (bf16[2,64,1280]{2,1,0:T(8,128)(2,1)S(1)}, bf16[2,64,1280]{2,1,0:T(8,128)(2,1)S(1)}, u32[]{:S(2)}, u32[]{:S(2)}) collective-permute-start(bf16[2,64,1280]{2,1,0:T(8,128)(2,1)S(1)} %fusion.1), channel_id=1, source_target_pairs={{0,1},{1,0},{2,3},{3,2},{4,5},{5,4},{6,7},{7,6},{8,9},{9,8},{10,11... | collective-permute-start | bytes 983048 | tf_op jit(solution)/shard_map/ppermute | solution.py:149

commit v3 on v2

--- a/solution.py
+++ b/solution.py
@@ -28,8 +28,8 @@
 
 
 def align_kernel(
-    scale, tiles, slots, meta, group, q_ref, own_ref, other_ref, out_ref,
-    base_rows, scores, weights, listed, arrived,
+    scale, tiles, slots, meta, group, q_ref, own_ref, other_ref, kept_ref, given_ref,
+    scores, weights, listed,
 ):
     stride = meta.shape[0] // 2
     core = meta[4 * slots + 1]
@@ -37,17 +37,6 @@
     width = tiles * TILE
     chunks = 2 * width // CHUNK
 
-    def copy(index):
-        source = own_ref if index < chunks // 2 else other_ref
-        first = (index % (chunks // 2)) * CHUNK
-        return pltpu.make_async_copy(
-            source.at[pl.ds(first, CHUNK)],
-            base_rows.at[pl.ds(index * CHUNK, CHUNK)],
-            arrived.at[index],
-        )
-
-    for index in range(chunks):
-        copy(index).start()
     weights[...] = jnp.zeros_like(weights)
 
     count = jnp.int32(0)
@@ -76,11 +65,12 @@
     across = (((1,), (1,)), ((), ()))
     query = q_ref[...]
     for index in range(chunks):
-        copy(index).wait()
-        span = pl.ds(index * CHUNK, CHUNK)
+        span = slice(index * CHUNK, (index + 1) * CHUNK)
+        source = own_ref if index < chunks // 2 else other_ref
+        at = (index % (chunks // 2)) * CHUNK
         scores[:, span] = (
             lax.dot_general(
-                query, base_rows[span, :], across, preferred_element_type=jnp.float32
+                query, source[at : at + CHUNK, :], across, preferred_element_type=jnp.float32
             )
             * scale
         )
@@ -105,38 +95,37 @@
     both = HALF * TILE
     place = lax.broadcasted_iota(jnp.int32, (both, both), 0)
     row = lax.broadcasted_iota(jnp.int32, (both, both), 1)
-    wanted = (place & ~127) + ((place & 63) >> 2) * 8 + ((place >> 6) & 1) * 4 + (place & 3)
+    goes_to = (place >> 7) ^ core
+    tile = ((place >> 6) & 1) ^ (deep & 1)
+    wanted = tile * TILE + ((place & 63) >> 2) * 8 + goes_to * 4 + (place & 3)
     sort = (row == wanted).astype(jnp.bfloat16)
     weight = jnp.dot(
         sort, weights[...].astype(jnp.bfloat16), preferred_element_type=jnp.float32
     ).astype(jnp.bfloat16)
-    out_ref[...] = jnp.dot(
-        weight, base_rows[...], preferred_element_type=jnp.float32
-    ).astype(out_ref.dtype)
+    for half, ref in enumerate((kept_ref, given_ref)):
+        part = weight[half * TILE : (half + 1) * TILE]
+        ref[...] = (
+            jnp.dot(part[:, :width], own_ref[...], preferred_element_type=jnp.float32)
+            + jnp.dot(part[:, width:], other_ref[...], preferred_element_type=jnp.float32)
+        ).astype(ref.dtype)
 
 
 def align(meta, group, queries, own, other, slots):
     rows, width = queries.shape
     tiles = own.shape[0] // TILE
     columns = 2 * own.shape[0]
-    whole = pl.BlockSpec(memory_space=pl.ANY)
-    block = pl.BlockSpec((rows, width), lambda i, meta, group: (0, 0))
+    vmem = pl.BlockSpec(memory_space=pltpu.VMEM)
+    smem = pl.BlockSpec(memory_space=pltpu.SMEM)
     return pl.pallas_call(
         functools.partial(align_kernel, width ** (-0.5), tiles, slots),
-        grid_spec=pltpu.PrefetchScalarGridSpec(
-            num_scalar_prefetch=2,
-            grid=(1,),
-            in_specs=[block, whole, whole],
-            out_specs=block,
-            scratch_shapes=[
-                pltpu.VMEM((columns, width), jnp.bfloat16),
-                pltpu.VMEM((rows, columns), jnp.float32),
-                pltpu.VMEM((rows, columns), jnp.float32),
-                pltpu.SMEM((4, 2 * slots + UNROLL), jnp.int32),
-                pltpu.SemaphoreType.DMA((columns // CHUNK,)),
-            ],
-        ),
-        out_shape=jax.ShapeDtypeStruct((rows, width), jnp.bfloat16),
+        in_specs=[smem, smem, vmem, vmem, vmem],
+        out_specs=[vmem, vmem],
+        scratch_shapes=[
+            pltpu.VMEM((rows, columns), jnp.float32),
+            pltpu.VMEM((rows, columns), jnp.float32),
+            pltpu.SMEM((4, 2 * slots + UNROLL), jnp.int32),
+        ],
+        out_shape=[jax.ShapeDtypeStruct((rows // 2, width), jnp.bfloat16)] * 2,
         compiler_params=pltpu.CompilerParams(vmem_limit_bytes=24 * 1024 * 1024),
         cost_estimate=pl.CostEstimate(
             flops=4 * rows * columns * width, bytes_accessed=6 * 1024 * 1024, transcendentals=0
@@ -145,13 +134,48 @@
     )(meta, group, queries, own, other)
 
 
+def combine_kernel(same, *refs):
+    parts, out_ref = refs[:-1], refs[-1]
+    rows = parts[0].shape[0]
+    count = len(parts) // 2
+
+    def total(some):
+        return sum(ref[...].astype(jnp.float32) for ref in some).astype(out_ref.dtype)
+
+    kept_at = pl.multiple_of(jnp.where(same[0] == 1, 0, rows), rows)
+    taken_at = pl.multiple_of(jnp.where(same[0] == 1, rows, 0), rows)
+    out_ref[pl.ds(kept_at, rows), :] = total(parts[:count])
+    out_ref[pl.ds(taken_at, rows), :] = total(parts[count:])
+
+
+def combine(same, parts):
+    rows, width = parts[0].shape
+    vmem = pl.BlockSpec(memory_space=pltpu.VMEM)
+    return pl.pallas_call(
+        combine_kernel,
+        in_specs=[pl.BlockSpec(memory_space=pltpu.SMEM)] + [vmem] * len(parts),
+        out_specs=vmem,
+        out_shape=jax.ShapeDtypeStruct((2 * rows, width), jnp.bfloat16),
+        compiler_params=pltpu.CompilerParams(vmem_limit_bytes=24 * 1024 * 1024),
+        cost_estimate=pl.CostEstimate(
+            flops=len(parts) * rows * width, bytes_accessed=0, transcendentals=0
+        ),
+        name="combine",
+    )(same, *parts)
+
+
 def sibling(value):
     return lax.ppermute(value, "c", [(0, 1), (1, 0)])
 
 
-def turned(value, distance):
+def turned(value, distance, crossed):
     groups = lax.axis_size("x")
-    return lax.ppermute(value, "x", [(i, (i + distance) % groups) for i in range(groups)])
+    route = [
+        (2 * i + c, 2 * ((i + distance) % groups) + (c ^ crossed))
+        for i in range(groups)
+        for c in range(2)
+    ]
+    return lax.ppermute(value, ("x", "c"), route)
 
 
 def on_device(queries, database, pair_tiles, pair_lengths, live_pairs):
@@ -171,11 +195,12 @@
         [jnp.where(core == 0, queries, first), jnp.where(core == 0, first, second)]
     )
 
-    other = sibling(database)
     own_meta = jnp.concatenate(
         [pair_tiles.reshape(-1), pair_lengths.reshape(-1), live_pairs, core[None], deep[None]]
     )
     own_meta = jnp.pad(own_meta, (0, 128 - own_meta.shape[0]))
+    panel, database, own_meta = lax.optimization_barrier((panel, database, own_meta))
+    other = sibling(database)
     meta = jnp.concatenate([own_meta, sibling(own_meta)])
 
     def terms_of(rows, distance):
@@ -183,25 +208,17 @@
         return align(meta, group[None], rows, database, other, slots)
 
     distances = (1, 3, 2)
-    panels = [turned(panel, d) for d in distances]
-    parts = [terms_of(panel, 0)]
+    panels = [turned(panel, d, 0) for d in distances]
+    kept, given = terms_of(panel, 0)
+    kept, panels[0] = lax.optimization_barrier((kept, panels[0]))
+    own_parts, other_parts = [kept], [sibling(given)]
     for distance, rows in zip(distances, panels, strict=True):
-        parts.append(turned(terms_of(rows, distance), -distance))
-
-    parts = [part.reshape(HALF, 2, tile // 2, width) for part in parts]
-
-    def half(which):
-        return sum(
-            lax.dynamic_index_in_dim(part, which, 1, keepdims=False).astype(jnp.float32)
-            for part in parts
-        ).astype(jnp.bfloat16)
-
-    taken = sibling(half(1 - core))
-    kept = half(core)
-    same = (deep >> 1) == core
-    column = jnp.stack([jnp.where(same, kept, taken), jnp.where(same, taken, kept)])
-    column = jnp.where((deep & 1) == 0, column, column[:, ::-1])
-
+        kept, given = terms_of(rows, distance)
+        own_parts.append(turned(kept, -distance, 0))
+        other_parts.append(turned(given, -distance, 1))
+
+    same = ((deep >> 1) == core).astype(jnp.int32)
+    column = combine(same[None], own_parts + other_parts)
     pieces = lax.all_to_all(column.reshape(-1, 4, width), ("zh", "y", "zl"), 0, 0, tiled=True)
     return jnp.sum(pieces.astype(jnp.float32), axis=0).astype(jnp.bfloat16)
 

time: 145 us -> 140 us (0.966)
  starting transfers between devices: 39.1 us -> 53.5 us
  waiting for transfers between devices: 38.4 us -> 24.3 us
  Pallas kernels: 34.3 us -> 23.3 us
  blocking collectives: 25.9 us -> 34.6 us
  other arithmetic: 3.94 us -> 1 us
    pallas_call x4, Pallas kernels: 34.3 us -> 23 us  [align(): pl.pallas_call(functools.partial(align_kernel, width ** (-0.5), tiles, sl...]
    ppermute x6 -> x9, starting transfers between devices: 19.3 us -> 30.5 us  [turned(): return lax.ppermute(value, ('x', 'c'), route)]
    ppermute x6 -> x9, waiting for transfers between devices: 24.3 us -> 15.4 us  [turned(): return lax.ppermute(value, ('x', 'c'), route)]
    all_to_all x1, blocking collectives: 25.9 us -> 34.6 us  [on_device(): lax.all_to_all(column.reshape(-1, 4, width), ('zh', 'y', 'zl'), 0, 0, til...]
    ppermute x1, waiting for transfers between devices: 11.4 us -> 4.62 us  [on_device(): first = lax.ppermute(queries, ('zh', 'c'), near)]
    ppermute x1, starting transfers between devices: 5.26 us -> 11.5 us  [on_device(): first = lax.ppermute(queries, ('zh', 'c'), near)]
    ppermute x1, waiting for transfers between devices: 0.01 us -> 3.54 us  [on_device(): second = lax.ppermute(queries, ('zh', 'c'), far)]
    ppermute x3, starting transfers between devices: 12.6 us -> 9.64 us  [sibling(): return lax.ppermute(value, 'c', [(0, 1), (1, 0)])]
  transfers between devices with their start and end apart: 11 -> 14, of which waited for: 5 -> 7; matrix products, arithmetic and copies ran while one was open for 0% -> 1% of each run, Pallas kernels for 24% -> 16%
where the time goes in v3:
time: 140 us
  starting transfers between devices  53.5 us (38%)
  blocking collectives  34.6 us (25%)
  waiting for transfers between devices  24.3 us (17%)
  Pallas kernels  23.3 us (17%)
  local copies, waits for them, and re-layouts  1.99 us (1%)
    all_to_all x1, blocking collectives, on_device(): lax.all_to_all(column.reshape(-1, 4, width), ('zh', 'y', 'zl'), 0, 0, til...  34.6 us
    ppermute x9, starting transfers between devices, turned(): return lax.ppermute(value, ('x', 'c'), route)  30.5 us
    pallas_call x4, Pallas kernels, align(): pl.pallas_call(functools.partial(align_kernel, width ** (-0.5), tiles, sl...  23 us
    ppermute x9, waiting for transfers between devices, turned(): return lax.ppermute(value, ('x', 'c'), route)  15.4 us
    ppermute x1, starting transfers between devices, on_device(): first = lax.ppermute(queries, ('zh', 'c'), near)  11.5 us
    ppermute x3, starting transfers between devices, sibling(): return lax.ppermute(value, 'c', [(0, 1), (1, 0)])  9.64 us
    ppermute x1, waiting for transfers between devices, on_device(): first = lax.ppermute(queries, ('zh', 'c'), near)  4.62 us
    ppermute x1, waiting for transfers between devices, on_device(): second = lax.ppermute(queries, ('zh', 'c'), far)  3.54 us
  transfers between devices with their start and end apart: 14, of which 7 were waited for; matrix products, arithmetic and copies ran while one was open for 1% of the time, Pallas kernels for 16%

profile of v3, /device:TPU:1, one launch (start us, length us, event | category | flops | bytes accessed | tf_op | source)
XLA Modules:
  0.0 139.6 jit_solution(13427194617856618941)
XLA Ops:
  0.0 11.5 %collective-permute-start = (bf16[128,1280]{1,0:T(8,128)(2,1)}, bf16[128,1280]{1,0:T(8,128)(2,1)S(1)}, u32[]{:S(2)}, u32[]{:S(2)}) collective-permute-start(bf16[128,1280]{1,0:T(8,128)(2,1)} %param.5), channel_id=1, source_target_pairs={{0,32},{1,65},{32,0},{33,97},{64,96},{65,1},{96,64},{97,33},{2,34}... | collective-permute-start | bytes 983048 | tf_op jit(solution)/shard_map/ppermute | solution.py:192
  11.5 1.9 %collective-permute-start.1 = (bf16[128,1280]{1,0:T(8,128)(2,1)}, bf16[128,1280]{1,0:T(8,128)(2,1)S(1)}, u32[]{:S(2)}, u32[]{:S(2)}) collective-permute-start(bf16[128,1280]{1,0:T(8,128)(2,1)} %param.5), channel_id=1, source_target_pairs={{1,97},{33,65},{65,33},{97,1},{3,99},{35,67},{67,35},{99,3},{5,101... | collective-permute-start | bytes 983048 | tf_op jit(solution)/shard_map/ppermute | solution.py:193
  14.1 0.8 copy.8
  14.8 0.1 reshape.9
  14.9 0.8 copy.9
  15.7 0.1 reshape.10
  15.8 0.1 concatenate.10
  15.9 0.0 copy-start
  15.9 4.6 %collective-permute-done = bf16[128,1280]{1,0:T(8,128)(2,1)S(1)} collective-permute-done((bf16[128,1280]{1,0:T(8,128)(2,1)}, bf16[128,1280]{1,0:T(8,128)(2,1)S(1)}, u32[]{:S(2)}, u32[]{:S(2)}) %collective-permute-start) | collective-permute-done | bytes 327712 | tf_op jit(solution)/shard_map/ppermute | solution.py:192
  20.5 3.5 %collective-permute-done.1 = bf16[128,1280]{1,0:T(8,128)(2,1)S(1)} collective-permute-done((bf16[128,1280]{1,0:T(8,128)(2,1)}, bf16[128,1280]{1,0:T(8,128)(2,1)S(1)}, u32[]{:S(2)}, u32[]{:S(2)}) %collective-permute-start.1) | collective-permute-done | bytes 327712 | tf_op jit(solution)/shard_map/ppermute | solution.py:193
  24.0 0.1 broadcast_select_fusion.1
  24.1 0.0 copy-done
  24.2 4.1 %collective-permute-start.3 = (bf16[768,1280]{1,0:T(8,128)(2,1)S(1)}, bf16[768,1280]{1,0:T(8,128)(2,1)}, u32[]{:S(2)}, u32[]{:S(2)}) collective-permute-start(bf16[768,1280]{1,0:T(8,128)(2,1)S(1)} %copy-done), channel_id=1, source_target_pairs={{0,1},{1,0},{2,3},{3,2},{4,5},{5,4},{6,7},{7,6},{8,9},{9,8},{10,11... | collective-permute-start | bytes 5898248 | tf_op jit(solution)/shard_map/ppermute | solution.py:168
  28.3 4.1 %collective-permute-start.4 = (bf16[256,1280]{1,0:T(8,128)(2,1)S(1)}, bf16[256,1280]{1,0:T(8,128)(2,1)}, u32[]{:S(2)}, u32[]{:S(2)}) collective-permute-start(bf16[256,1280]{1,0:T(8,128)(2,1)S(1)} %pad_maximum_fusion.q_ref), channel_id=1, source_target_pairs={{0,128},{1,129},{128,256},{129,257},{256,384},{257,385},{384,0},{3... | collective-permute-start | bytes 1966088 | tf_op jit(solution)/shard_map/ppermute | solution.py:178
  32.4 4.4 %collective-permute-start.8 = (bf16[256,1280]{1,0:T(8,128)(2,1)S(1)}, bf16[256,1280]{1,0:T(8,128)(2,1)}, u32[]{:S(2)}, u32[]{:S(2)}) collective-permute-start(bf16[256,1280]{1,0:T(8,128)(2,1)S(1)} %pad_maximum_fusion.q_ref), channel_id=1, source_target_pairs={{0,256},{1,257},{128,384},{129,385},{256,0},{257,1},{384,128},{385... | collective-permute-start | bytes 1966088 | tf_op jit(solution)/shard_map/ppermute | solution.py:178
  36.8 3.1 %collective-permute-start.6 = (bf16[256,1280]{1,0:T(8,128)(2,1)S(1)}, bf16[256,1280]{1,0:T(8,128)(2,1)S(1)}, u32[]{:S(2)}, u32[]{:S(2)}) collective-permute-start(bf16[256,1280]{1,0:T(8,128)(2,1)S(1)} %pad_maximum_fusion.q_ref), channel_id=1, source_target_pairs={{0,384},{1,385},{128,0},{129,1},{256,128},{257,129},{384,256},{385... | collective-permute-start | bytes 1966088 | tf_op jit(solution)/shard_map/ppermute | solution.py:178
  39.9 3.2 %collective-permute-start.2 = (s32[128]{0:T(128)S(1)}, s32[128]{0:T(128)S(1)}, u32[]{:S(2)}, u32[]{:S(2)}) collective-permute-start(s32[128]{0:T(128)S(1)} %pad.4), channel_id=1, source_target_pairs={{0,1},{1,0},{2,3},{3,2},{4,5},{5,4},{6,7},{7,6},{8,9},{9,8},{10,11... | collective-permute-start | bytes 1544 | tf_op jit(solution)/shard_map/ppermute | solution.py:168
  43.1 0.8 collective-permute-done.2
  43.9 0.0 collective-permute-done.3.other_ref
  43.9 5.9 %align.4 = (bf16[128,1280]{1,0:T(8,128)(2,1)S(1)}, bf16[128,1280]{1,0:T(8,128)(2,1)}) custom-call(s32[256]{0:T(256)S(1)} %constant_dynamic-update-slice_fusion.meta, s32[1]{0:T(128)} %bitcast.3.group, bf16[256,1280]{1,0:T(8,128)(2,1)S(1)} %pad_maximum_fusion.q_ref, bf16[768,1280]{1,0:T(8,128)(2,1)S(1)} %copy-done, ...), custom_call_target="tpu_custom_call" | custom-call | flops 2013265920 | bytes 6291456 | tf_op jit(solution)/shard_map/align/pallas_call | solution.py:119
  49.8 0.0 collective-permute-done.4.q_ref
  49.8 0.0 copy-start.1
  49.8 5.8 %align.5 = (bf16[128,1280]{1,0:T(8,128)(2,1)S(1)}, bf16[128,1280]{1,0:T(8,128)(2,1)S(1)}) custom-call(s32[256]{0:T(256)S(1)} %constant_dynamic-update-slice_fusion.meta, s32[1]{0:T(128)} %bitcast.4.group, bf16[256,1280]{1,0:T(8,128)(2,1)} %collective-permute-done.4.q_ref, bf16[768,1280]{1,0:T(8,128)(2,1)S(1)} %copy-done, ...), custom_call_target="tpu_custom_call" | custom-call | flops 2013265920 | bytes 6291456 | tf_op jit(solution)/shard_map/align/pallas_call | solution.py:119
  55.6 1.9 %collective-permute-start.5 = (bf16[128,1280]{1,0:T(8,128)(2,1)S(1)}, bf16[128,1280]{1,0:T(8,128)(2,1)S(1)}, u32[]{:S(2)}, u32[]{:S(2)}) collective-permute-start(bf16[128,1280]{1,0:T(8,128)(2,1)S(1)} %get-tuple-element.24), channel_id=1, source_target_pairs={{0,384},{1,385},{128,0},{129,1},{256,128},{257,129},{384,256},{385... | collective-permute-start | bytes 983048 | tf_op jit(solution)/shard_map/ppermute | solution.py:178
  57.6 4.4 %collective-permute-start.11 = (bf16[128,1280]{1,0:T(8,128)(2,1)S(1)}, bf16[128,1280]{1,0:T(8,128)(2,1)S(1)}, u32[]{:S(2)}, u32[]{:S(2)}) collective-permute-start(bf16[128,1280]{1,0:T(8,128)(2,1)S(1)} %get-tuple-element.28), channel_id=1, source_target_pairs={{0,385},{1,384},{128,1},{129,0},{256,129},{257,128},{384,257},{385... | collective-permute-start | bytes 983048 | tf_op jit(solution)/shard_map/ppermute | solution.py:178
  61.9 1.4 %collective-permute-done.8.q_ref = bf16[256,1280]{1,0:T(8,128)(2,1)} collective-permute-done((bf16[256,1280]{1,0:T(8,128)(2,1)S(1)}, bf16[256,1280]{1,0:T(8,128)(2,1)}, u32[]{:S(2)}, u32[]{:S(2)}) %collective-permute-start.8) | collective-permute-done | bytes 655392 | tf_op jit(solution)/shard_map/ppermute | solution.py:178
  63.3 0.0 copy-done.1
  63.3 6.1 %align.7 = (bf16[128,1280]{1,0:T(8,128)(2,1)}, bf16[128,1280]{1,0:T(8,128)(2,1)}) custom-call(s32[256]{0:T(256)S(1)} %constant_dynamic-update-slice_fusion.meta, s32[1]{0:T(128)} %bitcast.6.group, bf16[256,1280]{1,0:T(8,128)(2,1)} %collective-permute-done.8.q_ref, bf16[768,1280]{1,0:T(8,128)(2,1)S(1)} %copy-done.1, ...), custom_call_target="tpu_custom_call" | custom-call | flops 2013265920 | bytes 6291456 | tf_op jit(solution)/shard_map/align/pallas_call | solution.py:119
  69.4 2.4 %collective-permute-start.9 = (bf16[128,1280]{1,0:T(8,128)(2,1)}, bf16[128,1280]{1,0:T(8,128)(2,1)S(1)}, u32[]{:S(2)}, u32[]{:S(2)}) collective-permute-start(bf16[128,1280]{1,0:T(8,128)(2,1)} %get-tuple-element.26), channel_id=1, source_target_pairs={{0,256},{1,257},{128,384},{129,385},{256,0},{257,1},{384,128},{385... | collective-permute-start | bytes 983048 | tf_op jit(solution)/shard_map/ppermute | solution.py:178
  71.9 6.2 %collective-permute-start.13 = (bf16[128,1280]{1,0:T(8,128)(2,1)}, bf16[128,1280]{1,0:T(8,128)(2,1)S(1)}, u32[]{:S(2)}, u32[]{:S(2)}) collective-permute-start(bf16[128,1280]{1,0:T(8,128)(2,1)} %get-tuple-element.30), channel_id=1, source_target_pairs={{0,257},{1,256},{128,385},{129,384},{256,1},{257,0},{384,129},{385... | collective-permute-start | bytes 983048 | tf_op jit(solution)/shard_map/ppermute | solution.py:178
  78.0 0.0 collective-permute-done.6.q_ref
  78.0 5.2 %align.6 = (bf16[128,1280]{1,0:T(8,128)(2,1)S(1)}, bf16[128,1280]{1,0:T(8,128)(2,1)S(1)}) custom-call(s32[256]{0:T(256)S(1)} %constant_dynamic-update-slice_fusion.meta, s32[1]{0:T(128)} %bitcast.5.group, bf16[256,1280]{1,0:T(8,128)(2,1)S(1)} %collective-permute-done.6.q_ref, bf16[768,1280]{1,0:T(8,128)(2,1)S(1)} %copy-done.1, ...), custom_call_target="tpu_custom_call" | custom-call | flops 2013265920 | bytes 6291456 | tf_op jit(solution)/shard_map/align/pallas_call | solution.py:119
  83.2 1.9 %collective-permute-start.7 = (bf16[128,1280]{1,0:T(8,128)(2,1)S(1)}, bf16[128,1280]{1,0:T(8,128)(2,1)S(1)}, u32[]{:S(2)}, u32[]{:S(2)}) collective-permute-start(bf16[128,1280]{1,0:T(8,128)(2,1)S(1)} %get-tuple-element.25), channel_id=1, source_target_pairs={{0,128},{1,129},{128,256},{129,257},{256,384},{257,385},{384,0},{3... | collective-permute-start | bytes 983048 | tf_op jit(solution)/shard_map/ppermute | solution.py:178
  85.2 0.0 collective-permute-done.5.refs_1_
  85.2 2.2 %collective-permute-start.12 = (bf16[128,1280]{1,0:T(8,128)(2,1)S(1)}, bf16[128,1280]{1,0:T(8,128)(2,1)S(1)}, u32[]{:S(2)}, u32[]{:S(2)}) collective-permute-start(bf16[128,1280]{1,0:T(8,128)(2,1)S(1)} %get-tuple-element.29), channel_id=1, source_target_pairs={{0,129},{1,128},{128,257},{129,256},{256,385},{257,384},{384,1},{3... | collective-permute-start | bytes 983048 | tf_op jit(solution)/shard_map/ppermute | solution.py:178
  87.4 0.0 collective-permute-done.11.refs_5_
  87.4 2.3 %collective-permute-start.10 = (bf16[128,1280]{1,0:T(8,128)(2,1)}, bf16[128,1280]{1,0:T(8,128)(2,1)S(1)}, u32[]{:S(2)}, u32[]{:S(2)}) collective-permute-start(bf16[128,1280]{1,0:T(8,128)(2,1)} %get-tuple-element.27), channel_id=1, source_target_pairs={{0,1},{1,0},{2,3},{3,2},{4,5},{5,4},{6,7},{7,6},{8,9},{9,8},{10,11... | collective-permute-start | bytes 983048 | tf_op jit(solution)/shard_map/ppermute | solution.py:168
  89.7 0.0 collective-permute-done.9.refs_3_
  89.7 2.0 %collective-permute-done.13.refs_7_ = bf16[128,1280]{1,0:T(8,128)(2,1)S(1)} collective-permute-done((bf16[128,1280]{1,0:T(8,128)(2,1)}, bf16[128,1280]{1,0:T(8,128)(2,1)S(1)}, u32[]{:S(2)}, u32[]{:S(2)}) %collective-permute-start.13) | collective-permute-done | bytes 327712 | tf_op jit(solution)/shard_map/ppermute | solution.py:178
  91.7 5.6 %collective-permute-done.7.refs_2_ = bf16[128,1280]{1,0:T(8,128)(2,1)S(1)} collective-permute-done((bf16[128,1280]{1,0:T(8,128)(2,1)S(1)}, bf16[128,1280]{1,0:T(8,128)(2,1)S(1)}, u32[]{:S(2)}, u32[]{:S(2)}) %collective-permute-start.7) | collective-permute-done | bytes 327712 | tf_op jit(solution)/shard_map/ppermute | solution.py:178
  97.2 6.4 %collective-permute-done.12.refs_6_ = bf16[128,1280]{1,0:T(8,128)(2,1)S(1)} collective-permute-done((bf16[128,1280]{1,0:T(8,128)(2,1)S(1)}, bf16[128,1280]{1,0:T(8,128)(2,1)S(1)}, u32[]{:S(2)}, u32[]{:S(2)}) %collective-permute-start.12) | collective-permute-done | bytes 327712 | tf_op jit(solution)/shard_map/ppermute | solution.py:178
  103.6 0.0 collective-permute-done.10.refs_4_
  103.6 0.3 combine.1
  103.9 0.2 reshape.11
  104.1 34.6 %all_to_all.5 = bf16[64,4,1280]{2,1,0:T(4,128)(2,1)S(1)} all-to-all(bf16[64,4,1280]{2,1,0:T(4,128)(2,1)S(1)} %reshape.11), channel_id=1, replica_groups=mesh['x'=4,'zh'=4,'y'=8,'zl'=2,'c'=2] {'zh','y','zl'}, dimensions={0} | all-to-all | bytes 1310720 | tf_op jit(solution)/shard_map/all_to_all | solution.py:222
  138.7 0.9 reduce_sum.12
  (5 shorter events, 0.1 us)
Async XLA Ops:
  0.0 20.5 %collective-permute-start = (bf16[128,1280]{1,0:T(8,128)(2,1)}, bf16[128,1280]{1,0:T(8,128)(2,1)S(1)}, u32[]{:S(2)}, u32[]{:S(2)}) collective-permute-start(bf16[128,1280]{1,0:T(8,128)(2,1)} %param.5), channel_id=1, source_target_pairs={{0,32},{1,65},{32,0},{33,97},{64,96},{65,1},{96,64},{97,33},{2,34}... | collective-permute-start | bytes 983048 | tf_op jit(solution)/shard_map/ppermute | solution.py:192
  11.5 12.6 %collective-permute-start.1 = (bf16[128,1280]{1,0:T(8,128)(2,1)}, bf16[128,1280]{1,0:T(8,128)(2,1)S(1)}, u32[]{:S(2)}, u32[]{:S(2)}) collective-permute-start(bf16[128,1280]{1,0:T(8,128)(2,1)} %param.5), channel_id=1, source_target_pairs={{1,97},{33,65},{65,33},{97,1},{3,99},{35,67},{67,35},{99,3},{5,101... | collective-permute-start | bytes 983048 | tf_op jit(solution)/shard_map/ppermute | solution.py:193
  15.9 8.3 %copy-start = (bf16[768,1280]{1,0:T(8,128)(2,1)S(1)}, bf16[768,1280]{1,0:T(8,128)(2,1)}, u32[]{:S(2)}) copy-start(bf16[768,1280]{1,0:T(8,128)(2,1)} %own_ref.3) | copy-start | bytes 5898244
  24.2 19.8 %collective-permute-start.3 = (bf16[768,1280]{1,0:T(8,128)(2,1)S(1)}, bf16[768,1280]{1,0:T(8,128)(2,1)}, u32[]{:S(2)}, u32[]{:S(2)}) collective-permute-start(bf16[768,1280]{1,0:T(8,128)(2,1)S(1)} %copy-done), channel_id=1, source_target_pairs={{0,1},{1,0},{2,3},{3,2},{4,5},{5,4},{6,7},{7,6},{8,9},{9,8},{10,11... | collective-permute-start | bytes 5898248 | tf_op jit(solution)/shard_map/ppermute | solution.py:168
  28.3 21.5 %collective-permute-start.4 = (bf16[256,1280]{1,0:T(8,128)(2,1)S(1)}, bf16[256,1280]{1,0:T(8,128)(2,1)}, u32[]{:S(2)}, u32[]{:S(2)}) collective-permute-start(bf16[256,1280]{1,0:T(8,128)(2,1)S(1)} %pad_maximum_fusion.q_ref), channel_id=1, source_target_pairs={{0,128},{1,129},{128,256},{129,257},{256,384},{257,385},{384,0},{3... | collective-permute-start | bytes 1966088 | tf_op jit(solution)/shard_map/ppermute | solution.py:178
  32.4 30.9 %collective-permute-start.8 = (bf16[256,1280]{1,0:T(8,128)(2,1)S(1)}, bf16[256,1280]{1,0:T(8,128)(2,1)}, u32[]{:S(2)}, u32[]{:S(2)}) collective-permute-start(bf16[256,1280]{1,0:T(8,128)(2,1)S(1)} %pad_maximum_fusion.q_ref), channel_id=1, source_target_pairs={{0,256},{1,257},{128,384},{129,385},{256,0},{257,1},{384,128},{385... | collective-permute-start | bytes 1966088 | tf_op jit(solution)/shard_map/ppermute | solution.py:178
  36.8 41.2 %collective-permute-start.6 = (bf16[256,1280]{1,0:T(8,128)(2,1)S(1)}, bf16[256,1280]{1,0:T(8,128)(2,1)S(1)}, u32[]{:S(2)}, u32[]{:S(2)}) collective-permute-start(bf16[256,1280]{1,0:T(8,128)(2,1)S(1)} %pad_maximum_fusion.q_ref), channel_id=1, source_target_pairs={{0,384},{1,385},{128,0},{129,1},{256,128},{257,129},{384,256},{385... | collective-permute-start | bytes 1966088 | tf_op jit(solution)/shard_map/ppermute | solution.py:178
  39.9 4.1 %collective-permute-start.2 = (s32[128]{0:T(128)S(1)}, s32[128]{0:T(128)S(1)}, u32[]{:S(2)}, u32[]{:S(2)}) collective-permute-start(s32[128]{0:T(128)S(1)} %pad.4), channel_id=1, source_target_pairs={{0,1},{1,0},{2,3},{3,2},{4,5},{5,4},{6,7},{7,6},{8,9},{9,8},{10,11... | collective-permute-start | bytes 1544 | tf_op jit(solution)/shard_map/ppermute | solution.py:168
  49.8 13.5 %copy-start.1 = (bf16[768,1280]{1,0:T(8,128)(2,1)S(1)}, bf16[768,1280]{1,0:T(8,128)(2,1)}, u32[]{:S(2)}) copy-start(bf16[768,1280]{1,0:T(8,128)(2,1)} %own_ref.3) | copy-start | bytes 5898244
  55.6 29.5 %collective-permute-start.5 = (bf16[128,1280]{1,0:T(8,128)(2,1)S(1)}, bf16[128,1280]{1,0:T(8,128)(2,1)S(1)}, u32[]{:S(2)}, u32[]{:S(2)}) collective-permute-start(bf16[128,1280]{1,0:T(8,128)(2,1)S(1)} %get-tuple-element.24), channel_id=1, source_target_pairs={{0,384},{1,385},{128,0},{129,1},{256,128},{257,129},{384,256},{385... | collective-permute-start | bytes 983048 | tf_op jit(solution)/shard_map/ppermute | solution.py:178
  57.6 29.8 %collective-permute-start.11 = (bf16[128,1280]{1,0:T(8,128)(2,1)S(1)}, bf16[128,1280]{1,0:T(8,128)(2,1)S(1)}, u32[]{:S(2)}, u32[]{:S(2)}) collective-permute-start(bf16[128,1280]{1,0:T(8,128)(2,1)S(1)} %get-tuple-element.28), channel_id=1, source_target_pairs={{0,385},{1,384},{128,1},{129,0},{256,129},{257,128},{384,257},{385... | collective-permute-start | bytes 983048 | tf_op jit(solution)/shard_map/ppermute | solution.py:178
  69.4 20.2 %collective-permute-start.9 = (bf16[128,1280]{1,0:T(8,128)(2,1)}, bf16[128,1280]{1,0:T(8,128)(2,1)S(1)}, u32[]{:S(2)}, u32[]{:S(2)}) collective-permute-start(bf16[128,1280]{1,0:T(8,128)(2,1)} %get-tuple-element.26), channel_id=1, source_target_pairs={{0,256},{1,257},{128,384},{129,385},{256,0},{257,1},{384,128},{385... | collective-permute-start | bytes 983048 | tf_op jit(solution)/shard_map/ppermute | solution.py:178
  71.9 19.8 %collective-permute-start.13 = (bf16[128,1280]{1,0:T(8,128)(2,1)}, bf16[128,1280]{1,0:T(8,128)(2,1)S(1)}, u32[]{:S(2)}, u32[]{:S(2)}) collective-permute-start(bf16[128,1280]{1,0:T(8,128)(2,1)} %get-tuple-element.30), channel_id=1, source_target_pairs={{0,257},{1,256},{128,385},{129,384},{256,1},{257,0},{384,129},{385... | collective-permute-start | bytes 983048 | tf_op jit(solution)/shard_map/ppermute | solution.py:178
  83.2 14.0 %collective-permute-start.7 = (bf16[128,1280]{1,0:T(8,128)(2,1)S(1)}, bf16[128,1280]{1,0:T(8,128)(2,1)S(1)}, u32[]{:S(2)}, u32[]{:S(2)}) collective-permute-start(bf16[128,1280]{1,0:T(8,128)(2,1)S(1)} %get-tuple-element.25), channel_id=1, source_target_pairs={{0,128},{1,129},{128,256},{129,257},{256,384},{257,385},{384,0},{3... | collective-permute-start | bytes 983048 | tf_op jit(solution)/shard_map/ppermute | solution.py:178
  85.2 18.4 %collective-permute-start.12 = (bf16[128,1280]{1,0:T(8,128)(2,1)S(1)}, bf16[128,1280]{1,0:T(8,128)(2,1)S(1)}, u32[]{:S(2)}, u32[]{:S(2)}) collective-permute-start(bf16[128,1280]{1,0:T(8,128)(2,1)S(1)} %get-tuple-element.29), channel_id=1, source_target_pairs={{0,129},{1,128},{128,257},{129,256},{256,385},{257,384},{384,1},{3... | collective-permute-start | bytes 983048 | tf_op jit(solution)/shard_map/ppermute | solution.py:178
  87.4 16.2 %collective-permute-start.10 = (bf16[128,1280]{1,0:T(8,128)(2,1)}, bf16[128,1280]{1,0:T(8,128)(2,1)S(1)}, u32[]{:S(2)}, u32[]{:S(2)}) collective-permute-start(bf16[128,1280]{1,0:T(8,128)(2,1)} %get-tuple-element.27), channel_id=1, source_target_pairs={{0,1},{1,0},{2,3},{3,2},{4,5},{5,4},{6,7},{7,6},{8,9},{9,8},{10,11... | collective-permute-start | bytes 983048 | tf_op jit(solution)/shard_map/ppermute | solution.py:168

commit v4 on v3

v4 whole, which is shorter than its diff:
```python
import functools
import math

import jax
import jax.numpy as jnp
from jax import lax
from jax.experimental import pallas as pl
from jax.experimental.pallas import tpu as pltpu
from jax.sharding import Mesh
from jax.sharding import PartitionSpec as P

TILE = 128
BLK = ("x", "zh")
SHARD = ("yq", "yp", "zl", "c")
HALF = 2
CHUNK = 256
UNROLL = 4
LIST = 64


def pair_weight(scores, rows, cols, row_count, col_count):
    valid = (rows < row_count) & (cols < col_count)
    masked = jnp.where(valid, scores, -1e30)
    row_max = jnp.max(masked, axis=1, keepdims=True)
    row_lse = row_max + jnp.log(jnp.sum(jnp.exp(masked - row_max), axis=1, keepdims=True))
    col_max = jnp.max(masked, axis=0, keepdims=True)
    col_lse = col_max + jnp.log(jnp.sum(jnp.exp(masked - col_max), axis=0, keepdims=True))
    weight = jnp.where(valid, jnp.exp(scores - 0.5 * (row_lse + col_lse)), 0.0)
    return weight.astype(jnp.bfloat16)


def plan_kernel(tiles, slots, meta, lists):
    stride = meta.shape[0] // 2
    core, deep, here = (meta[4 * slots + 1 + k] for k in range(3))
    groups = lists.shape[0] // LIST
    for group in range(groups):
        lists[group * LIST] = 0
    for side in range(2):
        base = side * stride

        def look(slot, carry, base=base, side=side):
            query_tile = meta[base + 2 * slot]
            near = (query_tile & 3) ^ deep

            @pl.when((near >> 1) == core)
            def _():
                at = (query_tile >> 2) * LIST
                count = lists[at] + 1
                lists[at] = count
                lists[at + count] = (
                    (near & 1)
                    + 2 * (meta[base + 2 * slot + 1] + side * tiles)
                    + 256 * meta[base + 2 * slots + 2 * slot]
                    + 65536 * meta[base + 2 * slots + 2 * slot + 1]
                )

            return carry

        lax.fori_loop(0, meta[base + 4 * slots], look, 0)
    for group in range(groups):
        count = lists[group * LIST]
        for extra in range(1, UNROLL):
            lists[group * LIST + count + extra] = 0
    lists[groups * LIST - 3] = core
    lists[groups * LIST - 2] = deep
    lists[groups * LIST - 1] = here


def plan(meta, tiles, slots, groups):
    smem = pl.BlockSpec(memory_space=pltpu.SMEM)
    return pl.pallas_call(
        functools.partial(plan_kernel, tiles, slots),
        in_specs=[smem],
        out_specs=smem,
        out_shape=jax.ShapeDtypeStruct((groups * LIST,), jnp.int32),
        name="plan",
    )(meta)


def align_kernel(scale, distance, lists, q_ref, own_ref, other_ref, *refs):
    out_ref, scores, weights = refs[-3:]
    groups = lists.shape[0] // LIST
    core, deep, here = (lists[groups * LIST - 3 + k] for k in range(3))
    group = (here - distance) & (groups - 1)
    width = own_ref.shape[0]
    weights[...] = jnp.zeros_like(weights)

    across = (((1,), (1,)), ((), ()))
    query = q_ref[...]
    for side, ref in enumerate((own_ref, other_ref)):
        for first in range(0, width, CHUNK):
            scores[:, side * width + first : side * width + first + CHUNK] = (
                lax.dot_general(
                    query, ref[first : first + CHUNK, :], across, preferred_element_type=jnp.float32
                )
                * scale
            )

    rows = lax.broadcasted_iota(jnp.int32, (TILE, TILE), 0)
    cols = lax.broadcasted_iota(jnp.int32, (TILE, TILE), 1)
    start = group * LIST

    def batch(index, carry):
        made = []
        for k in range(UNROLL):
            slot = lists[start + 1 + index * UNROLL + k]
            at_row = pl.ds(pl.multiple_of((slot & 1) * TILE, TILE), TILE)
            at_col = pl.ds(pl.multiple_of(((slot >> 1) & 127) * TILE, TILE), TILE)
            weight = pair_weight(
                scores[at_row, at_col], rows, cols, (slot >> 8) & 255, slot >> 16
            )
            made.append((at_row, at_col, weight))
        for at_row, at_col, weight in made:
            weights[at_row, at_col] += weight.astype(jnp.float32)
        return carry

    lax.fori_loop(0, (lists[start] + UNROLL - 1) // UNROLL, batch, 0)

    both = HALF * TILE
    place = lax.broadcasted_iota(jnp.int32, (both, both), 0)
    row = lax.broadcasted_iota(jnp.int32, (both, both), 1)
    tile = ((place >> 4) & 1) ^ (deep & 1)
    wanted = tile * TILE + ((place >> 2) & 3) * 32 + (place >> 5) * 4 + (place & 3)
    sort = (row == wanted).astype(jnp.bfloat16)
    weight = jnp.dot(
        sort, weights[...].astype(jnp.bfloat16), preferred_element_type=jnp.float32
    ).astype(jnp.bfloat16)
    out_ref[pl.ds(pl.multiple_of(group * both, both), both), :] = (
        jnp.dot(weight[:, :width], own_ref[...], preferred_element_type=jnp.float32)
        + jnp.dot(weight[:, width:], other_ref[...], preferred_element_type=jnp.float32)
    ).astype(out_ref.dtype)


def align(lists, distance, queries, own, other, sofar):
    rows, width = queries.shape
    groups = lists.shape[0] // LIST
    columns = 2 * own.shape[0]
    vmem = pl.BlockSpec(memory_space=pltpu.VMEM)
    return pl.pallas_call(
        functools.partial(align_kernel, width ** (-0.5), distance),
        in_specs=[pl.BlockSpec(memory_space=pltpu.SMEM)] + [vmem] * (3 + len(sofar)),
        out_specs=vmem,
        scratch_shapes=[
            pltpu.VMEM((rows, columns), jnp.float32),
            pltpu.VMEM((rows, columns), jnp.float32),
        ],
        out_shape=jax.ShapeDtypeStruct((groups * rows, width), jnp.bfloat16),
        input_output_aliases={4: 0} if sofar else {},
        compiler_params=pltpu.CompilerParams(vmem_limit_bytes=24 * 1024 * 1024),
        cost_estimate=pl.CostEstimate(
            flops=4 * rows * columns * width, bytes_accessed=6 * 1024 * 1024, transcendentals=0
        ),
        name="align",
    )(lists, queries, own, other, *sofar)


def combine_kernel(cores, lists, parts_ref, out_ref):
    peers, rows, _ = parts_ref.shape
    deep = lists[lists.shape[0] - 2]
    for core in range(cores):
        total = sum(
            parts_ref[peer].astype(jnp.float32) for peer in range(core, peers, cores)
        ).astype(out_ref.dtype)
        out_ref[pl.ds(pl.multiple_of((core ^ (deep >> 1)) * rows, rows), rows), :] = total


def combine(lists, parts, cores):
    peers, rows, width = parts.shape
    vmem = pl.BlockSpec(memory_space=pltpu.VMEM)
    return pl.pallas_call(
        functools.partial(combine_kernel, cores),
        in_specs=[pl.BlockSpec(memory_space=pltpu.SMEM), vmem],
        out_specs=vmem,
        out_shape=jax.ShapeDtypeStruct((cores * rows, width), jnp.bfloat16),
        compiler_params=pltpu.CompilerParams(vmem_limit_bytes=24 * 1024 * 1024),
        cost_estimate=pl.CostEstimate(
            flops=peers * rows * width, bytes_accessed=0, transcendentals=0
        ),
        name="combine",
    )(lists, parts)


def sibling(value):
    return lax.ppermute(value, "c", [(0, 1), (1, 0)])


def turned(value, distance):
    groups = lax.axis_size("x")
    return lax.ppermute(value, "x", [(i, (i + distance) % groups) for i in range(groups)])


def on_device(queries, database, pair_tiles, pair_lengths, live_pairs):
    tile, width = queries.shape
    slots = pair_tiles.shape[1]
    core = lax.axis_index("c").astype(jnp.int32)
    deep = lax.axis_index("zh").astype(jnp.int32)
    here = lax.axis_index("x").astype(jnp.int32)
    groups = lax.axis_size("x")
    places = lax.axis_size("zh")

    near = [(2 * z + c, 2 * (z ^ (1 + c)) + c) for z in range(places) for c in range(2)]
    far = [(2 * z + 1, 2 * (z ^ 3) + 1) for z in range(places)]
    first = lax.ppermute(queries, ("zh", "c"), near)
    second = lax.ppermute(queries, ("zh", "c"), far)
    panel = jnp.concatenate(
        [jnp.where(core == 0, queries, first), jnp.where(core == 0, first, second)]
    )

    own_meta = jnp.concatenate(
        [pair_tiles.reshape(-1), pair_lengths.reshape(-1), live_pairs]
        + [axis[None] for axis in (core, deep, here)]
    )
    own_meta = jnp.pad(own_meta, (0, 128 - own_meta.shape[0]))
    lists = plan(
        jnp.concatenate([own_meta, sibling(own_meta)]), database.shape[0] // tile, slots, groups
    )
    panel, database = lax.optimization_barrier((panel, database))
    other = sibling(database)

    distances = (1, 3, 2)
    panels = [turned(panel, d) for d in distances]
    terms = align(lists, 0, panel, database, other, [])
    for distance, rows in zip(distances, panels, strict=True):
        terms = align(lists, distance, rows, database, other, [terms])

    near_axes = ("x", "yp", "zl", "c")
    peers = math.prod(lax.axis_size(axis) for axis in near_axes)
    parts = lax.all_to_all(terms.reshape(peers, -1, width), near_axes, 0, 0, tiled=True)
    column = combine(lists, parts, lax.axis_size("c"))
    pieces = lax.all_to_all(column.reshape(-1, 4, width), ("zh", "yq"), 0, 0, tiled=True)
    return jnp.sum(pieces.astype(jnp.float32), axis=0).astype(jnp.bfloat16)


def solution(mesh):
    fine = Mesh(mesh.devices.reshape(4, 4, 4, 2, 2, 2), BLK + SHARD)
    both = BLK + SHARD
    in_specs = (P(BLK, None), P(both, None), P(both, None, None), P(both, None, None), P(both))
    return jax.shard_map(
        on_device, mesh=fine, in_specs=in_specs, out_specs=P(both, None), check_vma=False
    )
```

time: 140 us -> 142 us (1.014)
  blocking collectives: 34.6 us -> 70 us
  starting transfers between devices: 53.5 us -> 31.5 us
  waiting for transfers between devices: 24.3 us -> 12.7 us
    all_to_all x1 -> x2, blocking collectives: 34.6 us -> 70 us  [the longest x1 46.3 us: on_device(): lax.all_to_all(terms.reshape(peers, -1, width), near_axes, 0, 0, tiled=True)]
    ppermute x9 -> x3, starting transfers between devices: 30.5 us -> 11.2 us  [turned(): lax.ppermute(value, 'x', [(i, (i + distance) % groups) for i in range(gro...]
    ppermute x9 -> x3, waiting for transfers between devices: 15.4 us -> 2.07 us  [turned(): lax.ppermute(value, 'x', [(i, (i + distance) % groups) for i in range(gro...]
    ppermute x3 -> x2, starting transfers between devices: 9.64 us -> 6.8 us  [sibling(): return lax.ppermute(value, 'c', [(0, 1), (1, 0)])]
    ppermute x1, waiting for transfers between devices: 4.62 us -> 7.07 us  [on_device(): first = lax.ppermute(queries, ('zh', 'c'), near)]
    pallas_call x5 -> x6, Pallas kernels: 23.3 us -> 22.8 us  [the longest x4 20.1 us: align(): pl.pallas_call(functools.partial(align_kernel, width ** (-0.5), distance)...]
  transfers between devices with their start and end apart: 14 -> 7, of which waited for: 7 -> 3; matrix products, arithmetic and copies ran while one was open for 1% -> 1% of each run, Pallas kernels for 16% -> 12%
where the time goes in v4:
time: 142 us; the launch traced here: 141 us
  blocking collectives  70 us (49%)
  starting transfers between devices  31.5 us (22%)
  Pallas kernels  22.8 us (16%)
  waiting for transfers between devices  12.7 us (9%)
  other arithmetic  2.2 us (2%)
    all_to_all x1, blocking collectives, on_device(): lax.all_to_all(terms.reshape(peers, -1, width), near_axes, 0, 0, tiled=True)  46.3 us
    all_to_all x1, blocking collectives, on_device(): lax.all_to_all(column.reshape(-1, 4, width), ('zh', 'yq'), 0, 0, tiled=True)  23.7 us
    pallas_call x4, Pallas kernels, align(): pl.pallas_call(functools.partial(align_kernel, width ** (-0.5), distance)...  20.1 us
    ppermute x1, starting transfers between devices, on_device(): first = lax.ppermute(queries, ('zh', 'c'), near)  11.6 us
    ppermute x3, starting transfers between devices, turned(): lax.ppermute(value, 'x', [(i, (i + distance) % groups) for i in range(gro...  11.2 us
    ppermute x1, waiting for transfers between devices, on_device(): first = lax.ppermute(queries, ('zh', 'c'), near)  7.07 us
    ppermute x2, starting transfers between devices, sibling(): return lax.ppermute(value, 'c', [(0, 1), (1, 0)])  6.8 us
    ppermute x1, waiting for transfers between devices, on_device(): second = lax.ppermute(queries, ('zh', 'c'), far)  3.55 us
  transfers between devices with their start and end apart: 7, of which 3 were waited for; matrix products, arithmetic and copies ran while one was open for 1% of the time, Pallas kernels for 12%

profile of v4, /device:TPU:1, one launch (start us, length us, event | category | flops | bytes accessed | tf_op | source)
XLA Modules:
  0.0 141.3 jit_solution(4006594113776993849)
XLA Ops:
  0.0 0.0 copy-start
  0.0 0.0 copy-start.2
  0.0 0.0 copy-start.3
  0.0 11.6 %collective-permute-start.1 = (bf16[128,1280]{1,0:T(8,128)(2,1)}, bf16[128,1280]{1,0:T(8,128)(2,1)S(1)}, u32[]{:S(2)}, u32[]{:S(2)}) collective-permute-start(bf16[128,1280]{1,0:T(8,128)(2,1)} %param.5), channel_id=1, source_target_pairs={{0,32},{1,65},{32,0},{33,97},{64,96},{65,1},{96,64},{97,33},{2,34}... | collective-permute-start | bytes 983048 | tf_op jit(solution)/shard_map/ppermute | solution.py:203
  11.6 1.9 %collective-permute-start.2 = (bf16[128,1280]{1,0:T(8,128)(2,1)}, bf16[128,1280]{1,0:T(8,128)(2,1)S(1)}, u32[]{:S(2)}, u32[]{:S(2)}) collective-permute-start(bf16[128,1280]{1,0:T(8,128)(2,1)} %param.5), channel_id=1, source_target_pairs={{1,97},{33,65},{65,33},{97,1},{3,99},{35,67},{67,35},{99,3},{5,101... | collective-permute-start | bytes 983048 | tf_op jit(solution)/shard_map/ppermute | solution.py:204
  13.6 7.1 %collective-permute-done.1 = bf16[128,1280]{1,0:T(8,128)(2,1)S(1)} collective-permute-done((bf16[128,1280]{1,0:T(8,128)(2,1)}, bf16[128,1280]{1,0:T(8,128)(2,1)S(1)}, u32[]{:S(2)}, u32[]{:S(2)}) %collective-permute-start.1) | collective-permute-done | bytes 327712 | tf_op jit(solution)/shard_map/ppermute | solution.py:203
  20.6 3.5 %collective-permute-done.2 = bf16[128,1280]{1,0:T(8,128)(2,1)S(1)} collective-permute-done((bf16[128,1280]{1,0:T(8,128)(2,1)}, bf16[128,1280]{1,0:T(8,128)(2,1)S(1)}, u32[]{:S(2)}, u32[]{:S(2)}) %collective-permute-start.2) | collective-permute-done | bytes 327712 | tf_op jit(solution)/shard_map/ppermute | solution.py:204
  24.2 0.1 broadcast_select_fusion.1
  24.2 0.9 pad_maximum_fusion.q_ref
  25.1 0.0 copy-done
  25.1 4.1 %collective-permute-start.4 = (bf16[768,1280]{1,0:T(8,128)(2,1)S(1)}, bf16[768,1280]{1,0:T(8,128)(2,1)}, u32[]{:S(2)}, u32[]{:S(2)}) collective-permute-start(bf16[768,1280]{1,0:T(8,128)(2,1)S(1)} %copy-done), channel_id=1, source_target_pairs={{0,1},{1,0},{2,3},{3,2},{4,5},{5,4},{6,7},{7,6},{8,9},{9,8},{10,11... | collective-permute-start | bytes 5898248 | tf_op jit(solution)/shard_map/ppermute | solution.py:184
  29.3 4.1 %collective-permute-start.6 = (bf16[256,1280]{1,0:T(8,128)(2,1)}, bf16[256,1280]{1,0:T(8,128)(2,1)S(1)}, u32[]{:S(2)}, u32[]{:S(2)}) collective-permute-start(bf16[256,1280]{1,0:T(8,128)(2,1)} %pad_maximum_fusion.q_ref), channel_id=1, source_target_pairs={{0,128},{128,256},{256,384},{384,0},{1,129},{129,257},{257,385},{3... | collective-permute-start | bytes 1966088 | tf_op jit(solution)/shard_map/ppermute | solution.py:189
  33.4 3.2 %collective-permute-start.5 = (bf16[256,1280]{1,0:T(8,128)(2,1)}, bf16[256,1280]{1,0:T(8,128)(2,1)S(1)}, u32[]{:S(2)}, u32[]{:S(2)}) collective-permute-start(bf16[256,1280]{1,0:T(8,128)(2,1)} %pad_maximum_fusion.q_ref), channel_id=1, source_target_pairs={{0,384},{128,0},{256,128},{384,256},{1,385},{129,1},{257,129},{385... | collective-permute-start | bytes 1966088 | tf_op jit(solution)/shard_map/ppermute | solution.py:189
  36.6 0.0 copy-done.2
  36.6 0.1 copy.11
  36.7 0.1 reshape.12
  36.8 0.0 copy-done.3
  36.8 0.1 copy.12
  36.9 0.1 reshape.13
  37.6 0.1 concatenate.9
  37.7 2.7 %collective-permute-start = (s32[128]{0:T(128)S(1)}, s32[128]{0:T(128)S(1)}, u32[]{:S(2)}, u32[]{:S(2)}) collective-permute-start(s32[128]{0:T(128)S(1)} %pad.4), channel_id=1, source_target_pairs={{0,1},{1,0},{2,3},{3,2},{4,5},{5,4},{6,7},{7,6},{8,9},{9,8},{10,11... | collective-permute-start | bytes 1544 | tf_op jit(solution)/shard_map/ppermute | solution.py:184
  40.4 3.9 %collective-permute-start.3 = (bf16[256,1280]{1,0:T(8,128)(2,1)}, bf16[256,1280]{1,0:T(8,128)(2,1)}, u32[]{:S(2)}, u32[]{:S(2)}) collective-permute-start(bf16[256,1280]{1,0:T(8,128)(2,1)} %pad_maximum_fusion.q_ref), channel_id=1, source_target_pairs={{0,256},{128,384},{256,0},{384,128},{1,257},{129,385},{257,1},{385... | collective-permute-start | bytes 1966088 | tf_op jit(solution)/shard_map/ppermute | solution.py:189
  44.3 0.0 collective-permute-done
  44.3 0.6 pad_add_fusion.meta
  44.9 1.8 %plan.1.lists = s32[256]{0:T(256)} custom-call(s32[256]{0:T(256)} %pad_add_fusion.meta), custom_call_target="tpu_custom_call" | custom-call | tf_op jit(solution)/shard_map/plan/pallas_call | solution.py:71
  46.7 0.0 collective-permute-done.4.other_ref
  46.7 0.0 copy-start.1
  46.7 0.7 copy-done.1
  47.4 5.1 %align.4.refs_0_ = bf16[1024,1280]{1,0:T(8,128)(2,1)S(1)} custom-call(s32[256]{0:T(256)S(1)} %copy-done.1, bf16[256,1280]{1,0:T(8,128)(2,1)} %pad_maximum_fusion.q_ref, bf16[768,1280]{1,0:T(8,128)(2,1)S(1)} %copy-done, bf16[768,1280]{1,0:T(8,128)(2,1)} %collective-permute-done.4.other_ref), custom_call_target="tpu_custom_call" | custom-call | flops 2013265920 | bytes 6291456 | tf_op jit(solution)/shard_map/align/pallas_call | solution.py:139
  52.5 0.0 collective-permute-done.6.q_ref
  52.6 4.9 %align.5.refs_0_ = bf16[1024,1280]{1,0:T(8,128)(2,1)S(1)} custom-call(s32[256]{0:T(256)S(1)} %copy-done.1, bf16[256,1280]{1,0:T(8,128)(2,1)S(1)} %collective-permute-done.6.q_ref, bf16[768,1280]{1,0:T(8,128)(2,1)S(1)} %copy-done, bf16[768,1280]{1,0:T(8,128)(2,1)} %collective-permute-done.4.other_ref, ...), custom_call_target="tpu_custom_call", output_to_operand_aliasing={{}: (4, {})} | custom-call | flops 2013265920 | bytes 6291456 | tf_op jit(solution)/shard_map/align/pallas_call | solution.py:139
  57.5 0.0 collective-permute-done.5.q_ref
  57.5 4.9 %align.6.refs_0_ = bf16[1024,1280]{1,0:T(8,128)(2,1)S(1)} custom-call(s32[256]{0:T(256)S(1)} %copy-done.1, bf16[256,1280]{1,0:T(8,128)(2,1)S(1)} %collective-permute-done.5.q_ref, bf16[768,1280]{1,0:T(8,128)(2,1)S(1)} %copy-done, bf16[768,1280]{1,0:T(8,128)(2,1)} %collective-permute-done.4.other_ref, ...), custom_call_target="tpu_custom_call", output_to_operand_aliasing={{}: (4, {})} | custom-call | flops 2013265920 | bytes 6291456 | tf_op jit(solution)/shard_map/align/pallas_call | solution.py:139
  62.4 2.1 %collective-permute-done.3.q_ref = bf16[256,1280]{1,0:T(8,128)(2,1)} collective-permute-done((bf16[256,1280]{1,0:T(8,128)(2,1)}, bf16[256,1280]{1,0:T(8,128)(2,1)}, u32[]{:S(2)}, u32[]{:S(2)}) %collective-permute-start.3) | collective-permute-done | bytes 655392 | tf_op jit(solution)/shard_map/ppermute | solution.py:189
  64.5 5.1 %align.7 = bf16[1024,1280]{1,0:T(8,128)(2,1)S(1)} custom-call(s32[256]{0:T(256)S(1)} %copy-done.1, bf16[256,1280]{1,0:T(8,128)(2,1)} %collective-permute-done.3.q_ref, bf16[768,1280]{1,0:T(8,128)(2,1)S(1)} %copy-done, bf16[768,1280]{1,0:T(8,128)(2,1)} %collective-permute-done.4.other_ref, ...), custom_call_target="tpu_custom_call", output_to_operand_aliasing={{}: (4, {})} | custom-call | flops 2013265920 | bytes 6291456 | tf_op jit(solution)/shard_map/align/pallas_call | solution.py:139
  69.6 46.3 %all_to_all.10.parts_ref = bf16[32,32,1280]{2,1,0:T(8,128)(2,1)S(1)} all-to-all(bf16[32,32,1280]{2,1,0:T(8,128)(2,1)S(1)} %bitcast.4), channel_id=1, replica_groups=mesh['x'=4,'zh'=4,'yq'=4,'yp'=2,'zl'=2,'c'=2] {'x','yp','zl','c'}, dimensions={0} | all-to-all | bytes 5242880 | tf_op jit(solution)/shard_map/all_to_all | solution.py:228
  116.0 0.9 combine.1
  116.9 23.7 %all_to_all.11 = bf16[16,4,1280]{2,1,0:T(4,128)(2,1)S(1)} all-to-all(bf16[16,4,1280]{2,1,0:T(4,128)(2,1)S(1)} %reshape.15), channel_id=1, replica_groups=mesh['x'=4,'zh'=4,'yq'=4,'yp'=2,'zl'=2,'c'=2] {'zh','yq'}, dimensions={0} | all-to-all | bytes 327680 | tf_op jit(solution)/shard_map/all_to_all | solution.py:230
  140.6 0.7 reduce_sum.12
  (2 shorter events, 0.1 us)
Async XLA Ops:
  0.0 25.1 %copy-start = (bf16[768,1280]{1,0:T(8,128)(2,1)S(1)}, bf16[768,1280]{1,0:T(8,128)(2,1)}, u32[]{:S(2)}) copy-start(bf16[768,1280]{1,0:T(8,128)(2,1)} %own_ref.3) | copy-start | bytes 5898244
  0.0 36.6 %copy-start.2 = (s32[1,24,2]{1,2,0:T(2,128)S(1)}, s32[1,24,2]{1,2,0:T(2,128)}, u32[]{:S(2)}) copy-start(s32[1,24,2]{1,2,0:T(2,128)} %param.7) | copy-start | bytes 580
  0.0 36.8 %copy-start.3 = (s32[1,24,2]{1,2,0:T(2,128)S(1)}, s32[1,24,2]{1,2,0:T(2,128)}, u32[]{:S(2)}) copy-start(s32[1,24,2]{1,2,0:T(2,128)} %param.8) | copy-start | bytes 580
  0.0 20.6 %collective-permute-start.1 = (bf16[128,1280]{1,0:T(8,128)(2,1)}, bf16[128,1280]{1,0:T(8,128)(2,1)S(1)}, u32[]{:S(2)}, u32[]{:S(2)}) collective-permute-start(bf16[128,1280]{1,0:T(8,128)(2,1)} %param.5), channel_id=1, source_target_pairs={{0,32},{1,65},{32,0},{33,97},{64,96},{65,1},{96,64},{97,33},{2,34}... | collective-permute-start | bytes 983048 | tf_op jit(solution)/shard_map/ppermute | solution.py:203
  11.6 12.6 %collective-permute-start.2 = (bf16[128,1280]{1,0:T(8,128)(2,1)}, bf16[128,1280]{1,0:T(8,128)(2,1)S(1)}, u32[]{:S(2)}, u32[]{:S(2)}) collective-permute-start(bf16[128,1280]{1,0:T(8,128)(2,1)} %param.5), channel_id=1, source_target_pairs={{1,97},{33,65},{65,33},{97,1},{3,99},{35,67},{67,35},{99,3},{5,101... | collective-permute-start | bytes 983048 | tf_op jit(solution)/shard_map/ppermute | solution.py:204
  25.1 21.6 %collective-permute-start.4 = (bf16[768,1280]{1,0:T(8,128)(2,1)S(1)}, bf16[768,1280]{1,0:T(8,128)(2,1)}, u32[]{:S(2)}, u32[]{:S(2)}) collective-permute-start(bf16[768,1280]{1,0:T(8,128)(2,1)S(1)} %copy-done), channel_id=1, source_target_pairs={{0,1},{1,0},{2,3},{3,2},{4,5},{5,4},{6,7},{7,6},{8,9},{9,8},{10,11... | collective-permute-start | bytes 5898248 | tf_op jit(solution)/shard_map/ppermute | solution.py:184
  29.3 23.3 %collective-permute-start.6 = (bf16[256,1280]{1,0:T(8,128)(2,1)}, bf16[256,1280]{1,0:T(8,128)(2,1)S(1)}, u32[]{:S(2)}, u32[]{:S(2)}) collective-permute-start(bf16[256,1280]{1,0:T(8,128)(2,1)} %pad_maximum_fusion.q_ref), channel_id=1, source_target_pairs={{0,128},{128,256},{256,384},{384,0},{1,129},{129,257},{257,385},{3... | collective-permute-start | bytes 1966088 | tf_op jit(solution)/shard_map/ppermute | solution.py:189
  33.4 24.1 %collective-permute-start.5 = (bf16[256,1280]{1,0:T(8,128)(2,1)}, bf16[256,1280]{1,0:T(8,128)(2,1)S(1)}, u32[]{:S(2)}, u32[]{:S(2)}) collective-permute-start(bf16[256,1280]{1,0:T(8,128)(2,1)} %pad_maximum_fusion.q_ref), channel_id=1, source_target_pairs={{0,384},{128,0},{256,128},{384,256},{1,385},{129,1},{257,129},{385... | collective-permute-start | bytes 1966088 | tf_op jit(solution)/shard_map/ppermute | solution.py:189
  37.7 6.6 %collective-permute-start = (s32[128]{0:T(128)S(1)}, s32[128]{0:T(128)S(1)}, u32[]{:S(2)}, u32[]{:S(2)}) collective-permute-start(s32[128]{0:T(128)S(1)} %pad.4), channel_id=1, source_target_pairs={{0,1},{1,0},{2,3},{3,2},{4,5},{5,4},{6,7},{7,6},{8,9},{9,8},{10,11... | collective-permute-start | bytes 1544 | tf_op jit(solution)/shard_map/ppermute | solution.py:184
  40.4 24.1 %collective-permute-start.3 = (bf16[256,1280]{1,0:T(8,128)(2,1)}, bf16[256,1280]{1,0:T(8,128)(2,1)}, u32[]{:S(2)}, u32[]{:S(2)}) collective-permute-start(bf16[256,1280]{1,0:T(8,128)(2,1)} %pad_maximum_fusion.q_ref), channel_id=1, source_target_pairs={{0,256},{128,384},{256,0},{384,128},{1,257},{129,385},{257,1},{385... | collective-permute-start | bytes 1966088 | tf_op jit(solution)/shard_map/ppermute | solution.py:189
  46.7 0.7 copy-start.1

commit v5 on v4

v5 whole, which is shorter than its diff:
```python
import functools
import math

import jax
import jax.numpy as jnp
from jax import lax
from jax.experimental import pallas as pl
from jax.experimental.pallas import tpu as pltpu
from jax.sharding import Mesh
from jax.sharding import PartitionSpec as P

TILE = 128
BLK = ("x", "zh")
SHARD = ("yq", "yp", "zl", "c")
QUARTERS = 4
HALF = 2
CHUNK = 256
UNROLL = 4


def pair_weight(scores, rows, cols, row_count, col_count):
    valid = (rows < row_count) & (cols < col_count)
    masked = jnp.where(valid, scores, -1e30)
    row_max = jnp.max(masked, axis=1, keepdims=True)
    row_lse = row_max + jnp.log(jnp.sum(jnp.exp(masked - row_max), axis=1, keepdims=True))
    col_max = jnp.max(masked, axis=0, keepdims=True)
    col_lse = col_max + jnp.log(jnp.sum(jnp.exp(masked - col_max), axis=0, keepdims=True))
    weight = jnp.where(valid, jnp.exp(scores - 0.5 * (row_lse + col_lse)), 0.0)
    return weight.astype(jnp.bfloat16)


def spread_kernel(place, own_ref, first_ref, second_ref, out_ref):
    rows = own_ref.shape[0]
    near = place[0] == 0
    tiles = jnp.where(near, own_ref[...], first_ref[...]), jnp.where(near, first_ref[...], second_ref[...])
    for peer in range(out_ref.shape[0]):
        for index, tile in enumerate(tiles):
            out_ref[peer, index * rows : (index + 1) * rows, :] = tile


def spread(place, own, first, second, peers):
    rows, width = own.shape
    vmem = pl.BlockSpec(memory_space=pltpu.VMEM)
    return pl.pallas_call(
        spread_kernel,
        in_specs=[pl.BlockSpec(memory_space=pltpu.SMEM)] + [vmem] * 3,
        out_specs=vmem,
        out_shape=jax.ShapeDtypeStruct((peers, HALF * rows, width), jnp.bfloat16),
        name="spread",
    )(place, own, first, second)


def plan_kernel(tiles, slots, place, meta, lists):
    stride = meta.shape[0] // 2
    core, deep = place[0], place[1]
    lists[0] = 0
    for side in range(2):
        base = side * stride

        def look(slot, carry, base=base, side=side):
            query_tile = meta[base + 2 * slot]
            near = (query_tile & 3) ^ deep

            @pl.when((near >> 1) == core)
            def _():
                count = lists[0] + 1
                lists[0] = count
                lists[count] = (
                    (near & 1)
                    + 2 * (query_tile >> 2)
                    + 16 * (meta[base + 2 * slot + 1] + side * tiles)
                    + 256 * meta[base + 2 * slots + 2 * slot]
                    + 65536 * meta[base + 2 * slots + 2 * slot + 1]
                )

            return carry

        lax.fori_loop(0, meta[base + 4 * slots], look, 0)
    for extra in range(1, UNROLL):
        lists[lists[0] + extra] = 0


def plan(place, meta, tiles, slots):
    smem = pl.BlockSpec(memory_space=pltpu.SMEM)
    return pl.pallas_call(
        functools.partial(plan_kernel, tiles, slots),
        in_specs=[smem, smem],
        out_specs=smem,
        out_shape=jax.ShapeDtypeStruct((2 * slots + 1 + UNROLL,), jnp.int32),
        name="plan",
    )(place, meta)


def align_kernel(scale, place, lists, q_ref, own_ref, other_ref, out_ref, scores, weights):
    deep = place[1]
    total, _ = q_ref.shape
    width = own_ref.shape[0]
    group = HALF * TILE
    piece = TILE // QUARTERS

    across = (((1,), (1,)), ((), ()))
    for first in range(0, total, group):
        weights[first : first + group, :] = jnp.zeros((group, 2 * width), weights.dtype)
        query = q_ref[first : first + group, :]
        for side, ref in enumerate((own_ref, other_ref)):
            for at in range(0, width, CHUNK):
                scores[first : first + group, side * width + at : side * width + at + CHUNK] = (
                    lax.dot_general(
                        query, ref[at : at + CHUNK, :], across, preferred_element_type=jnp.float32
                    )
                    * scale
                )

    place_in_tile = lax.broadcasted_iota(jnp.int32, (TILE, TILE), 0)
    rows = ((place_in_tile >> 3) & 3) * 32 + (place_in_tile >> 5) * 8 + (place_in_tile & 7)
    cols = lax.broadcasted_iota(jnp.int32, (TILE, TILE), 1)

    def batch(index, carry):
        made = []
        for k in range(UNROLL):
            slot = lists[1 + index * UNROLL + k]
            first = ((slot >> 1) & 7) * group + (slot & 1) * piece
            at_rows = [
                pl.ds(pl.multiple_of(first + quarter * HALF * piece, piece), piece)
                for quarter in range(QUARTERS)
            ]
            at_col = pl.ds(pl.multiple_of(((slot >> 4) & 15) * TILE, TILE), TILE)
            score = jnp.concatenate([scores[at_row, at_col] for at_row in at_rows])
            weight = pair_weight(score, rows, cols, (slot >> 8) & 255, slot >> 16)
            made.append((at_rows, at_col, weight))
        for at_rows, at_col, weight in made:
            for quarter, at_row in enumerate(at_rows):
                weights[at_row, at_col] += weight[
                    quarter * piece : (quarter + 1) * piece
                ].astype(jnp.float32)
        return carry

    lax.fori_loop(0, (lists[0] + UNROLL - 1) // UNROLL, batch, 0)

    to = lax.broadcasted_iota(jnp.int32, (group, group), 0)
    row = lax.broadcasted_iota(jnp.int32, (group, group), 1)
    tile = ((to >> 4) & 1) ^ (deep & 1)
    wanted = (to >> 6) * 64 + tile * 32 + ((to >> 2) & 3) * 8 + ((to >> 5) & 1) * 4 + (to & 3)
    sort = (row == wanted).astype(jnp.bfloat16)
    for first in range(0, total, group):
        weight = jnp.dot(
            sort,
            weights[first : first + group, :].astype(jnp.bfloat16),
            preferred_element_type=jnp.float32,
        ).astype(jnp.bfloat16)
        out_ref[first : first + group, :] = (
            jnp.dot(weight[:, :width], own_ref[...], preferred_element_type=jnp.float32)
            + jnp.dot(weight[:, width:], other_ref[...], preferred_element_type=jnp.float32)
        ).astype(out_ref.dtype)


def align(place, lists, queries, own, other):
    rows, width = queries.shape
    columns = 2 * own.shape[0]
    smem = pl.BlockSpec(memory_space=pltpu.SMEM)
    vmem = pl.BlockSpec(memory_space=pltpu.VMEM)
    return pl.pallas_call(
        functools.partial(align_kernel, width ** (-0.5)),
        in_specs=[smem, smem, vmem, vmem, vmem],
        out_specs=vmem,
        scratch_shapes=[
            pltpu.VMEM((rows, columns), jnp.float32),
            pltpu.VMEM((rows, columns), jnp.float32),
        ],
        out_shape=jax.ShapeDtypeStruct((rows, width), jnp.bfloat16),
        compiler_params=pltpu.CompilerParams(vmem_limit_bytes=24 * 1024 * 1024),
        cost_estimate=pl.CostEstimate(
            flops=4 * rows * columns * width, bytes_accessed=0, transcendentals=0
        ),
        name="align",
    )(place, lists, queries, own, other)


def combine_kernel(cores, place, parts_ref, out_ref):
    peers, rows, _ = parts_ref.shape
    deep = place[1]
    for core in range(cores):
        total = sum(
            parts_ref[peer].astype(jnp.float32) for peer in range(core, peers, cores)
        ).astype(out_ref.dtype)
        out_ref[pl.ds(pl.multiple_of((core ^ (deep >> 1)) * rows, rows), rows), :] = total


def combine(place, parts, cores):
    peers, rows, width = parts.shape
    vmem = pl.BlockSpec(memory_space=pltpu.VMEM)
    return pl.pallas_call(
        functools.partial(combine_kernel, cores),
        in_specs=[pl.BlockSpec(memory_space=pltpu.SMEM), vmem],
        out_specs=vmem,
        out_shape=jax.ShapeDtypeStruct((cores * rows, width), jnp.bfloat16),
        compiler_params=pltpu.CompilerParams(vmem_limit_bytes=24 * 1024 * 1024),
        cost_estimate=pl.CostEstimate(
            flops=peers * rows * width, bytes_accessed=0, transcendentals=0
        ),
        name="combine",
    )(place, parts)


def sibling(value):
    return lax.ppermute(value, "c", [(0, 1), (1, 0)])


def on_device(queries, database, pair_tiles, pair_lengths, live_pairs):
    tile, width = queries.shape
    slots = pair_tiles.shape[1]
    core = lax.axis_index("c").astype(jnp.int32)
    deep = lax.axis_index("zh").astype(jnp.int32)
    place = jnp.stack([core, deep])
    places = lax.axis_size("zh")

    quarter = queries.reshape(lax.axis_size("yq"), 2, 2, 8, width)
    quarter = lax.dynamic_index_in_dim(quarter, lax.axis_index("yp"), 1, keepdims=False)
    quarter = lax.dynamic_index_in_dim(quarter, lax.axis_index("zl"), 1, keepdims=False)
    quarter = quarter.reshape(tile // QUARTERS, width)
    near = [(2 * z + c, 2 * (z ^ (1 + c)) + c) for z in range(places) for c in range(2)]
    far = [(2 * z + 1, 2 * (z ^ 3) + 1) for z in range(places)]
    first = lax.ppermute(quarter, ("zh", "c"), near)
    second = lax.ppermute(quarter, ("zh", "c"), far)

    own_meta = jnp.concatenate([pair_tiles.reshape(-1), pair_lengths.reshape(-1), live_pairs])
    own_meta = jnp.pad(own_meta, (0, 128 - own_meta.shape[0]))
    meta = jnp.concatenate([own_meta, sibling(own_meta)])
    lists = plan(place, meta, database.shape[0] // tile, slots)

    around = ("x", "yp", "zl")
    peers = math.prod(lax.axis_size(axis) for axis in around)
    panel = spread(place, quarter, first, second, peers)
    panel, database = lax.optimization_barrier((panel, database))
    other = sibling(database)
    panels = lax.all_to_all(panel, around, 0, 0, tiled=True).reshape(-1, width)

    terms = align(place, lists, panels, database, other)

    around = ("x", "yp", "zl", "c")
    peers = math.prod(lax.axis_size(axis) for axis in around)
    parts = lax.all_to_all(terms.reshape(peers, -1, width), around, 0, 0, tiled=True)
    column = combine(place, parts, lax.axis_size("c"))
    pieces = lax.all_to_all(column.reshape(-1, 4, width), ("zh", "yq"), 0, 0, tiled=True)
    return jnp.sum(pieces.astype(jnp.float32), axis=0).astype(jnp.bfloat16)


def solution(mesh):
    fine = Mesh(mesh.devices.reshape(4, 4, 4, 2, 2, 2), BLK + SHARD)
    both = BLK + SHARD
    in_specs = (P(BLK, None), P(both, None), P(both, None, None), P(both, None, None), P(both))
    return jax.shard_map(
        on_device, mesh=fine, in_specs=in_specs, out_specs=P(both, None), check_vma=False
    )
```

time: 142 us -> 140 us (0.986)
  waiting for transfers between devices: 12.7 us -> 26.5 us
  starting transfers between devices: 31.5 us -> 23.9 us
  blocking collectives: 70 us -> 63.9 us
  Pallas kernels: 22.8 us -> 18.7 us
  local copies, waits for them, and re-layouts: 1.19 us -> 4.2 us
    all_to_all x0 -> x1, waiting for transfers between devices: none -> 18.3 us  [on_device(): panels = lax.all_to_all(panel, around, 0, 0, tiled=True).reshape(-1, width)]
    ppermute x5 -> x2, starting transfers between devices: 24.7 us -> 13.4 us  [the longest x1 11.5 us: on_device(): second = lax.ppermute(quarter, ('zh', 'c'), far)]
    all_to_all x1, blocking collectives: 46.3 us -> 39.6 us  [on_device(): lax.all_to_all(terms.reshape(peers, -1, width), around, 0, 0, tiled=True)]
    all_to_all x0 -> x1, starting transfers between devices: none -> 6.21 us  [on_device(): panels = lax.all_to_all(panel, around, 0, 0, tiled=True).reshape(-1, width)]
    ppermute x5 -> x2, waiting for transfers between devices: 12.7 us -> 7.42 us  [the longest x1 7.41 us: on_device(): first = lax.ppermute(quarter, ('zh', 'c'), near)]
    pallas_call x4 -> x2, Pallas kernels: 20.1 us -> 16 us  [the longest x1 13.3 us: align(): pl.pallas_call(functools.partial(align_kernel, width ** (-0.5)), in_specs...]
    unnamed x10 -> x20, local copies, waits for them, and re-layouts: 0.86 us -> 3.95 us
    ppermute x2, starting transfers between devices: 6.8 us -> 4.32 us  [sibling(): return lax.ppermute(value, 'c', [(0, 1), (1, 0)])]
  transfers between devices with their start and end apart: 7 -> 5, of which waited for: 3 -> 3; matrix products, arithmetic and copies ran while one was open for 1% -> 1% of each run, Pallas kernels for 12% -> 1%
where the time goes in v5:
time: 140 us
  blocking collectives  63.9 us (46%)
  waiting for transfers between devices  26.5 us (19%)
  starting transfers between devices  23.9 us (17%)
  Pallas kernels  18.7 us (13%)
  local copies, waits for them, and re-layouts  4.2 us (3%)
  other arithmetic  1.92 us (1%)
    all_to_all x1, blocking collectives, on_device(): lax.all_to_all(terms.reshape(peers, -1, width), around, 0, 0, tiled=True)  39.6 us
    all_to_all x1, blocking collectives, on_device(): lax.all_to_all(column.reshape(-1, 4, width), ('zh', 'yq'), 0, 0, tiled=True)  24.3 us
    all_to_all x1, waiting for transfers between devices, on_device(): panels = lax.all_to_all(panel, around, 0, 0, tiled=True).reshape(-1, width)  18.3 us
    pallas_call x1, Pallas kernels, align(): pl.pallas_call(functools.partial(align_kernel, width ** (-0.5)), in_specs...  13.3 us
    ppermute x1, starting transfers between devices, on_device(): second = lax.ppermute(quarter, ('zh', 'c'), far)  11.5 us
    ppermute x1, waiting for transfers between devices, on_device(): first = lax.ppermute(quarter, ('zh', 'c'), near)  7.41 us
    all_to_all x1, starting transfers between devices, on_device(): panels = lax.all_to_all(panel, around, 0, 0, tiled=True).reshape(-1, width)  6.21 us
    ppermute x2, starting transfers between devices, sibling(): return lax.ppermute(value, 'c', [(0, 1), (1, 0)])  4.32 us
  transfers between devices with their start and end apart: 5, of which 3 were waited for; matrix products, arithmetic and copies ran while one was open for 1% of the time, Pallas kernels for 1%

profile of v5, /device:TPU:1, one launch (start us, length us, event | category | flops | bytes accessed | tf_op | source)
XLA Modules:
  0.0 139.9 jit_solution(13111799178431470852)
XLA Ops:
  0.0 0.0 copy-start
  0.0 1.0 copy-done
  1.0 0.0 copy-start.4
  1.0 11.5 %collective-permute-start.2 = (bf16[32,1280]{1,0:T(8,128)(2,1)S(1)}, bf16[32,1280]{1,0:T(8,128)(2,1)S(1)}, u32[]{:S(2)}, u32[]{:S(2)}) collective-permute-start(bf16[32,1280]{1,0:T(8,128)(2,1)S(1)} %dynamic-slice_bitcast_fusion.own_ref), channel_id=1, source_target_pairs={{1,97},{33,65},{65,33},{97,1},{3,99},{35,67},{67,35},{99,3},{5,101... | collective-permute-start | bytes 245768 | tf_op jit(solution)/shard_map/ppermute | solution.py:224
  12.5 1.9 %collective-permute-start.1 = (bf16[32,1280]{1,0:T(8,128)(2,1)S(1)}, bf16[32,1280]{1,0:T(8,128)(2,1)S(1)}, u32[]{:S(2)}, u32[]{:S(2)}) collective-permute-start(bf16[32,1280]{1,0:T(8,128)(2,1)S(1)} %dynamic-slice_bitcast_fusion.own_ref), channel_id=1, source_target_pairs={{0,32},{1,65},{32,0},{33,97},{64,96},{65,1},{96,64},{97,33},{2,34}... | collective-permute-start | bytes 245768 | tf_op jit(solution)/shard_map/ppermute | solution.py:223
  14.4 0.6 pad_add_fusion.1.place
  15.0 0.0 collective-permute-done.2.second_ref
  15.0 0.0 copy-start.5
  15.0 7.4 %collective-permute-done.1.first_ref = bf16[32,1280]{1,0:T(8,128)(2,1)S(1)} collective-permute-done((bf16[32,1280]{1,0:T(8,128)(2,1)S(1)}, bf16[32,1280]{1,0:T(8,128)(2,1)S(1)}, u32[]{:S(2)}, u32[]{:S(2)}) %collective-permute-start.1) | collective-permute-done | bytes 81952 | tf_op jit(solution)/shard_map/ppermute | solution.py:223
  22.4 0.0 copy-done.4
  22.4 0.0 copy-done.5
  22.4 0.0 copy-start.6
  22.4 0.6 copy-done.6
  23.1 2.7 %spread.1 = bf16[16,64,1280]{2,1,0:T(8,128)(2,1)} custom-call(s32[2]{0:T(128)} %pad_add_fusion.1.place, bf16[32,1280]{1,0:T(8,128)(2,1)} %copy-done.4, bf16[32,1280]{1,0:T(8,128)(2,1)} %copy-done.6, bf16[32,1280]{1,0:T(8,128)(2,1)} %copy-done.5), custom_call_target="tpu_custom_call" | custom-call | tf_op jit(solution)/shard_map/spread/pallas_call | solution.py:44
  25.8 0.0 copy-start.7
  25.8 0.0 copy-start.8
  25.8 0.0 copy-start.1
  25.8 6.2 %all-to-all-start = ((bf16[16,64,1280]{2,1,0:T(8,128)(2,1)}), bf16[16,64,1280]{2,1,0:T(8,128)(2,1)S(1)}, u32[]{:S(2)}, u32[]{:S(2)}) async-start(bf16[16,64,1280]{2,1,0:T(8,128)(2,1)} %spread.1), calls=%async_computation | async-start | bytes 5242880 | tf_op jit(solution)/shard_map/all_to_all | solution.py:236
  32.0 1.9 %collective-permute-start.3 = (bf16[768,1280]{1,0:T(8,128)(2,1)}, bf16[768,1280]{1,0:T(8,128)(2,1)}, u32[]{:S(2)}, u32[]{:S(2)}) collective-permute-start(bf16[768,1280]{1,0:T(8,128)(2,1)} %own_ref), channel_id=1, source_target_pairs={{0,1},{1,0},{2,3},{3,2},{4,5},{5,4},{6,7},{7,6},{8,9},{9,8},{10,11... | collective-permute-start | bytes 5898248 | tf_op jit(solution)/shard_map/ppermute | solution.py:206
  34.6 0.0 copy-done.7
  34.6 0.1 copy.9
  34.7 0.1 reshape.24
  34.8 0.0 copy-done.8
  34.8 0.1 copy.10
  34.9 0.1 reshape.25
  35.0 0.1 pad_add_fusion.2
  35.1 2.4 %collective-permute-start = (s32[128]{0:T(128)S(1)}, s32[128]{0:T(128)S(1)}, u32[]{:S(2)}, u32[]{:S(2)}) collective-permute-start(s32[128]{0:T(128)S(1)} %pad.4), channel_id=1, source_target_pairs={{0,1},{1,0},{2,3},{3,2},{4,5},{5,4},{6,7},{7,6},{8,9},{9,8},{10,11... | collective-permute-start | bytes 1544 | tf_op jit(solution)/shard_map/ppermute | solution.py:206
  37.5 0.8 collective-permute-done
  38.3 0.6 pad_add_fusion.meta
  38.9 1.8 %plan.1.lists = s32[53]{0:T(128)} custom-call(s32[2]{0:T(128)} %pad_add_fusion.1.place, s32[256]{0:T(256)} %pad_add_fusion.meta), custom_call_target="tpu_custom_call" | custom-call | tf_op jit(solution)/shard_map/plan/pallas_call | solution.py:85
  40.6 0.0 collective-permute-done.3.other_ref
  40.6 18.3 %all-to-all-done = bf16[16,64,1280]{2,1,0:T(8,128)(2,1)S(1)} async-done(((bf16[16,64,1280]{2,1,0:T(8,128)(2,1)}), bf16[16,64,1280]{2,1,0:T(8,128)(2,1)S(1)}, u32[]{:S(2)}, u32[]{:S(2)}) %all-to-all-start) | async-done | bytes 2621472 | tf_op jit(solution)/shard_map/all_to_all | solution.py:236
  58.9 0.0 copy-done.1
  58.9 0.0 copy-start.2
  58.9 0.6 copy-done.2
  59.5 0.0 copy-start.3
  59.6 1.5 %copy-done.3 = bf16[768,1280]{1,0:T(8,128)(2,1)S(1)} copy-done((bf16[768,1280]{1,0:T(8,128)(2,1)S(1)}, bf16[768,1280]{1,0:T(8,128)(2,1)}, u32[]{:S(2)}) %copy-start.3) | copy-done | bytes 1966104
  61.1 13.3 %align.1 = bf16[1024,1280]{1,0:T(8,128)(2,1)S(1)} custom-call(s32[2]{0:T(128)S(1)} %copy-done.1, s32[53]{0:T(128)S(1)} %copy-done.2, bf16[1024,1280]{1,0:T(8,128)(2,1)S(1)} %bitcast.10, bf16[768,1280]{1,0:T(8,128)(2,1)S(1)} %copy-done.3, bf16[768,1280]{1,0:T(8,128)(2,1)} %collective-permute-done.3.other_ref), custom_call_target="tpu_custom_call" | custom-call | flops 8053063680 | tf_op jit(solution)/shard_map/align/pallas_call | solution.py:162
  74.4 39.6 %all_to_all.15.parts_ref = bf16[32,32,1280]{2,1,0:T(8,128)(2,1)S(1)} all-to-all(bf16[32,32,1280]{2,1,0:T(8,128)(2,1)S(1)} %bitcast.11), channel_id=1, replica_groups=mesh['x'=4,'zh'=4,'yq'=4,'yp'=2,'zl'=2,'c'=2] {'x','yp','zl','c'}, dimensions={0} | all-to-all | bytes 5242880 | tf_op jit(solution)/shard_map/all_to_all | solution.py:242
  114.0 0.9 combine.1
  114.9 24.3 %all_to_all.16 = bf16[16,4,1280]{2,1,0:T(4,128)(2,1)S(1)} all-to-all(bf16[16,4,1280]{2,1,0:T(4,128)(2,1)S(1)} %reshape.30), channel_id=1, replica_groups=mesh['x'=4,'zh'=4,'yq'=4,'yp'=2,'zl'=2,'c'=2] {'zh','yq'}, dimensions={0} | all-to-all | bytes 327680 | tf_op jit(solution)/shard_map/all_to_all | solution.py:244
  139.2 0.7 reduce_sum.12
  (3 shorter events, 0.1 us)
Async XLA Ops:
  0.0 1.0 copy-start
  1.0 21.5 %copy-start.4 = (bf16[32,1280]{1,0:T(8,128)(2,1)}, bf16[32,1280]{1,0:T(8,128)(2,1)S(1)}, u32[]{:S(2)}) copy-start(bf16[32,1280]{1,0:T(8,128)(2,1)S(1)} %dynamic-slice_bitcast_fusion.own_ref) | copy-start | bytes 245764
  1.0 14.0 %collective-permute-start.2 = (bf16[32,1280]{1,0:T(8,128)(2,1)S(1)}, bf16[32,1280]{1,0:T(8,128)(2,1)S(1)}, u32[]{:S(2)}, u32[]{:S(2)}) collective-permute-start(bf16[32,1280]{1,0:T(8,128)(2,1)S(1)} %dynamic-slice_bitcast_fusion.own_ref), channel_id=1, source_target_pairs={{1,97},{33,65},{65,33},{97,1},{3,99},{35,67},{67,35},{99,3},{5,101... | collective-permute-start | bytes 245768 | tf_op jit(solution)/shard_map/ppermute | solution.py:224
  12.5 9.9 %collective-permute-start.1 = (bf16[32,1280]{1,0:T(8,128)(2,1)S(1)}, bf16[32,1280]{1,0:T(8,128)(2,1)S(1)}, u32[]{:S(2)}, u32[]{:S(2)}) collective-permute-start(bf16[32,1280]{1,0:T(8,128)(2,1)S(1)} %dynamic-slice_bitcast_fusion.own_ref), channel_id=1, source_target_pairs={{0,32},{1,65},{32,0},{33,97},{64,96},{65,1},{96,64},{97,33},{2,34}... | collective-permute-start | bytes 245768 | tf_op jit(solution)/shard_map/ppermute | solution.py:223
  15.0 7.4 %copy-start.5 = (bf16[32,1280]{1,0:T(8,128)(2,1)}, bf16[32,1280]{1,0:T(8,128)(2,1)S(1)}, u32[]{:S(2)}) copy-start(bf16[32,1280]{1,0:T(8,128)(2,1)S(1)} %collective-permute-done.2.second_ref) | copy-start | bytes 245764
  22.4 0.6 copy-start.6
  25.8 8.8 %copy-start.7 = (s32[1,24,2]{1,2,0:T(2,128)S(1)}, s32[1,24,2]{1,2,0:T(2,128)}, u32[]{:S(2)}) copy-start(s32[1,24,2]{1,2,0:T(2,128)} %param.7) | copy-start | bytes 580
  25.8 9.0 %copy-start.8 = (s32[1,24,2]{1,2,0:T(2,128)S(1)}, s32[1,24,2]{1,2,0:T(2,128)}, u32[]{:S(2)}) copy-start(s32[1,24,2]{1,2,0:T(2,128)} %param.8) | copy-start | bytes 580
  25.8 33.1 %copy-start.1 = (s32[2]{0:T(128)S(1)}, s32[2]{0:T(128)}, u32[]{:S(2)}) copy-start(s32[2]{0:T(128)} %pad_add_fusion.1.place) | copy-start | bytes 28
  25.8 33.1 %all-to-all-start = ((bf16[16,64,1280]{2,1,0:T(8,128)(2,1)}), bf16[16,64,1280]{2,1,0:T(8,128)(2,1)S(1)}, u32[]{:S(2)}, u32[]{:S(2)}) async-start(bf16[16,64,1280]{2,1,0:T(8,128)(2,1)} %spread.1), calls=%async_computation | async-start | bytes 5242880 | tf_op jit(solution)/shard_map/all_to_all | solution.py:236
  32.0 8.6 %collective-permute-start.3 = (bf16[768,1280]{1,0:T(8,128)(2,1)}, bf16[768,1280]{1,0:T(8,128)(2,1)}, u32[]{:S(2)}, u32[]{:S(2)}) collective-permute-start(bf16[768,1280]{1,0:T(8,128)(2,1)} %own_ref), channel_id=1, source_target_pairs={{0,1},{1,0},{2,3},{3,2},{4,5},{5,4},{6,7},{7,6},{8,9},{9,8},{10,11... | collective-permute-start | bytes 5898248 | tf_op jit(solution)/shard_map/ppermute | solution.py:206
  35.1 3.2 %collective-permute-start = (s32[128]{0:T(128)S(1)}, s32[128]{0:T(128)S(1)}, u32[]{:S(2)}, u32[]{:S(2)}) collective-permute-start(s32[128]{0:T(128)S(1)} %pad.4), channel_id=1, source_target_pairs={{0,1},{1,0},{2,3},{3,2},{4,5},{5,4},{6,7},{7,6},{8,9},{9,8},{10,11... | collective-permute-start | bytes 1544 | tf_op jit(solution)/shard_map/ppermute | solution.py:206
  58.9 0.6 copy-start.2
  59.5 1.5 %copy-start.3 = (bf16[768,1280]{1,0:T(8,128)(2,1)S(1)}, bf16[768,1280]{1,0:T(8,128)(2,1)}, u32[]{:S(2)}) copy-start(bf16[768,1280]{1,0:T(8,128)(2,1)} %own_ref) | copy-start | bytes 5898244

commit v6 on v5

--- a/solution.py
+++ b/solution.py
@@ -29,13 +29,30 @@
     return weight.astype(jnp.bfloat16)
 
 
-def spread_kernel(place, own_ref, first_ref, second_ref, out_ref):
-    rows = own_ref.shape[0]
-    near = place[0] == 0
-    tiles = jnp.where(near, own_ref[...], first_ref[...]), jnp.where(near, first_ref[...], second_ref[...])
-    for peer in range(out_ref.shape[0]):
-        for index, tile in enumerate(tiles):
-            out_ref[peer, index * rows : (index + 1) * rows, :] = tile
+def spread_kernel(place, own_ref, first_ref, second_ref, out_ref, held, sent):
+    near, odd = place[0] == 0, place[1] & 1
+    both = jnp.concatenate(
+        [
+            jnp.where(near, own_ref[...], first_ref[...]),
+            jnp.where(near, first_ref[...], second_ref[...]),
+        ]
+    )
+    count = both.shape[0]
+    to = lax.broadcasted_iota(jnp.int32, (count, count), 0)
+    row = lax.broadcasted_iota(jnp.int32, (count, count), 1)
+    wanted = (((to >> 4) & 1) ^ odd) * 32 + ((to >> 2) & 3) * 8 + (to >> 5) * 4 + (to & 3)
+    both = jnp.dot(
+        (row == wanted).astype(both.dtype), both, preferred_element_type=jnp.float32
+    ).astype(both.dtype)
+    held[...] = both
+    copies = [
+        pltpu.make_async_copy(held, out_ref.at[peer], sent.at[peer])
+        for peer in range(out_ref.shape[0])
+    ]
+    for copy in copies:
+        copy.start()
+    for copy in copies:
+        copy.wait()
 
 
 def spread(place, own, first, second, peers):
@@ -44,8 +61,13 @@
     return pl.pallas_call(
         spread_kernel,
         in_specs=[pl.BlockSpec(memory_space=pltpu.SMEM)] + [vmem] * 3,
-        out_specs=vmem,
+        out_specs=pl.BlockSpec(memory_space=pl.ANY),
+        scratch_shapes=[
+            pltpu.VMEM((HALF * rows, width), jnp.bfloat16),
+            pltpu.SemaphoreType.DMA((peers,)),
+        ],
         out_shape=jax.ShapeDtypeStruct((peers, HALF * rows, width), jnp.bfloat16),
+        compiler_params=pltpu.CompilerParams(vmem_limit_bytes=8 * 1024 * 1024),
         name="spread",
     )(place, own, first, second)
 
@@ -66,7 +88,7 @@
                 count = lists[0] + 1
                 lists[0] = count
                 lists[count] = (
-                    (near & 1)
+                    (query_tile & 1)
                     + 2 * (query_tile >> 2)
                     + 16 * (meta[base + 2 * slot + 1] + side * tiles)
                     + 256 * meta[base + 2 * slots + 2 * slot]
@@ -87,16 +109,17 @@
         in_specs=[smem, smem],
         out_specs=smem,
         out_shape=jax.ShapeDtypeStruct((2 * slots + 1 + UNROLL,), jnp.int32),
+        compiler_params=pltpu.CompilerParams(vmem_limit_bytes=1024 * 1024),
         name="plan",
     )(place, meta)
 
 
-def align_kernel(scale, place, lists, q_ref, own_ref, other_ref, out_ref, scores, weights):
-    deep = place[1]
+def align_kernel(scale, lists, q_ref, own_ref, other_ref, out_ref, scores, weights):
     total, _ = q_ref.shape
     width = own_ref.shape[0]
     group = HALF * TILE
-    piece = TILE // QUARTERS
+    pieces = 2 * QUARTERS
+    piece = TILE // pieces
 
     across = (((1,), (1,)), ((), ()))
     for first in range(0, total, group):
@@ -112,7 +135,12 @@
                 )
 
     place_in_tile = lax.broadcasted_iota(jnp.int32, (TILE, TILE), 0)
-    rows = ((place_in_tile >> 3) & 3) * 32 + (place_in_tile >> 5) * 8 + (place_in_tile & 7)
+    rows = (
+        ((place_in_tile >> 2) & 3) * 32
+        + (place_in_tile >> 5) * 8
+        + ((place_in_tile >> 4) & 1) * 4
+        + (place_in_tile & 3)
+    )
     cols = lax.broadcasted_iota(jnp.int32, (TILE, TILE), 1)
 
     def batch(index, carry):
@@ -121,51 +149,42 @@
             slot = lists[1 + index * UNROLL + k]
             first = ((slot >> 1) & 7) * group + (slot & 1) * piece
             at_rows = [
-                pl.ds(pl.multiple_of(first + quarter * HALF * piece, piece), piece)
-                for quarter in range(QUARTERS)
+                pl.ds(pl.multiple_of(first + step * HALF * piece, piece), piece)
+                for step in range(pieces)
             ]
             at_col = pl.ds(pl.multiple_of(((slot >> 4) & 15) * TILE, TILE), TILE)
             score = jnp.concatenate([scores[at_row, at_col] for at_row in at_rows])
             weight = pair_weight(score, rows, cols, (slot >> 8) & 255, slot >> 16)
             made.append((at_rows, at_col, weight))
         for at_rows, at_col, weight in made:
-            for quarter, at_row in enumerate(at_rows):
-                weights[at_row, at_col] += weight[
-                    quarter * piece : (quarter + 1) * piece
-                ].astype(jnp.float32)
+            for step, at_row in enumerate(at_rows):
+                weights[at_row, at_col] += weight[step * piece : (step + 1) * piece].astype(
+                    weights.dtype
+                )
         return carry
 
     lax.fori_loop(0, (lists[0] + UNROLL - 1) // UNROLL, batch, 0)
 
-    to = lax.broadcasted_iota(jnp.int32, (group, group), 0)
-    row = lax.broadcasted_iota(jnp.int32, (group, group), 1)
-    tile = ((to >> 4) & 1) ^ (deep & 1)
-    wanted = (to >> 6) * 64 + tile * 32 + ((to >> 2) & 3) * 8 + ((to >> 5) & 1) * 4 + (to & 3)
-    sort = (row == wanted).astype(jnp.bfloat16)
     for first in range(0, total, group):
-        weight = jnp.dot(
-            sort,
-            weights[first : first + group, :].astype(jnp.bfloat16),
-            preferred_element_type=jnp.float32,
-        ).astype(jnp.bfloat16)
+        weight = weights[first : first + group, :].astype(jnp.bfloat16)
         out_ref[first : first + group, :] = (
             jnp.dot(weight[:, :width], own_ref[...], preferred_element_type=jnp.float32)
             + jnp.dot(weight[:, width:], other_ref[...], preferred_element_type=jnp.float32)
         ).astype(out_ref.dtype)
 
 
-def align(place, lists, queries, own, other):
+def align(lists, queries, own, other):
     rows, width = queries.shape
     columns = 2 * own.shape[0]
     smem = pl.BlockSpec(memory_space=pltpu.SMEM)
     vmem = pl.BlockSpec(memory_space=pltpu.VMEM)
     return pl.pallas_call(
         functools.partial(align_kernel, width ** (-0.5)),
-        in_specs=[smem, smem, vmem, vmem, vmem],
+        in_specs=[smem, vmem, vmem, vmem],
         out_specs=vmem,
         scratch_shapes=[
             pltpu.VMEM((rows, columns), jnp.float32),
-            pltpu.VMEM((rows, columns), jnp.float32),
+            pltpu.VMEM((rows, columns), jnp.bfloat16),
         ],
         out_shape=jax.ShapeDtypeStruct((rows, width), jnp.bfloat16),
         compiler_params=pltpu.CompilerParams(vmem_limit_bytes=24 * 1024 * 1024),
@@ -173,7 +192,7 @@
             flops=4 * rows * columns * width, bytes_accessed=0, transcendentals=0
         ),
         name="align",
-    )(place, lists, queries, own, other)
+    )(lists, queries, own, other)
 
 
 def combine_kernel(cores, place, parts_ref, out_ref):
@@ -220,6 +239,7 @@
     quarter = quarter.reshape(tile // QUARTERS, width)
     near = [(2 * z + c, 2 * (z ^ (1 + c)) + c) for z in range(places) for c in range(2)]
     far = [(2 * z + 1, 2 * (z ^ 3) + 1) for z in range(places)]
+    quarter, database = lax.optimization_barrier((quarter, database))
     first = lax.ppermute(quarter, ("zh", "c"), near)
     second = lax.ppermute(quarter, ("zh", "c"), far)
 
@@ -227,15 +247,15 @@
     own_meta = jnp.pad(own_meta, (0, 128 - own_meta.shape[0]))
     meta = jnp.concatenate([own_meta, sibling(own_meta)])
     lists = plan(place, meta, database.shape[0] // tile, slots)
+    other = sibling(database)
 
     around = ("x", "yp", "zl")
     peers = math.prod(lax.axis_size(axis) for axis in around)
     panel = spread(place, quarter, first, second, peers)
-    panel, database = lax.optimization_barrier((panel, database))
-    other = sibling(database)
+    panel, other = lax.optimization_barrier((panel, other))
     panels = lax.all_to_all(panel, around, 0, 0, tiled=True).reshape(-1, width)
 
-    terms = align(place, lists, panels, database, other)
+    terms = align(lists, panels, database, other)
 
     around = ("x", "yp", "zl", "c")
     peers = math.prod(lax.axis_size(axis) for axis in around)

time: 140 us -> 140 us (level)
  Pallas kernels: 18.7 us -> 16.4 us
  waiting for transfers between devices: 26.5 us -> 28.1 us
  local copies, waits for them, and re-layouts: 4.2 us -> 5.77 us
    ppermute x1, starting transfers between devices: 11.5 us -> 1.94 us  [on_device(): second = lax.ppermute(quarter, ('zh', 'c'), far)]
    ppermute x2, starting transfers between devices: 4.32 us -> 10.7 us  [sibling(): return lax.ppermute(value, 'c', [(0, 1), (1, 0)])]
    ppermute x1, waiting for transfers between devices: 7.41 us -> 2.25 us  [on_device(): first = lax.ppermute(quarter, ('zh', 'c'), near)]
    all_to_all x1, waiting for transfers between devices: 18.3 us -> 21.6 us  [on_device(): panels = lax.all_to_all(panel, around, 0, 0, tiled=True).reshape(-1, width)]
    ppermute x1, starting transfers between devices: 1.92 us -> 5.26 us  [on_device(): first = lax.ppermute(quarter, ('zh', 'c'), near)]
    ppermute x1, waiting for transfers between devices: 0.01 us -> 3.11 us  [on_device(): second = lax.ppermute(quarter, ('zh', 'c'), far)]
    pallas_call x1, Pallas kernels: 13.3 us -> 11.5 us  [align(): pl.pallas_call(functools.partial(align_kernel, width ** (-0.5)), in_specs...]
    unnamed x20 -> x14, local copies, waits for them, and re-layouts: 3.95 us -> 5.52 us
  transfers between devices with their start and end apart: 5 -> 5, of which waited for: 3 -> 4; matrix products, arithmetic and copies ran while one was open for 1% -> 0% of each run, Pallas kernels for 1% -> 3%
where the time goes in v6:
time: 140 us; the launch traced here: 139 us
  blocking collectives  62.7 us (45%)
  waiting for transfers between devices  28.1 us (20%)
  starting transfers between devices  24.7 us (18%)
  Pallas kernels  16.4 us (12%)
  local copies, waits for them, and re-layouts  5.77 us (4%)
    all_to_all x1, blocking collectives, on_device(): lax.all_to_all(terms.reshape(peers, -1, width), around, 0, 0, tiled=True)  38.2 us
    all_to_all x1, blocking collectives, on_device(): lax.all_to_all(column.reshape(-1, 4, width), ('zh', 'yq'), 0, 0, tiled=True)  24.5 us
    all_to_all x1, waiting for transfers between devices, on_device(): panels = lax.all_to_all(panel, around, 0, 0, tiled=True).reshape(-1, width)  21.6 us
    pallas_call x1, Pallas kernels, align(): pl.pallas_call(functools.partial(align_kernel, width ** (-0.5)), in_specs...  11.5 us
    ppermute x2, starting transfers between devices, sibling(): return lax.ppermute(value, 'c', [(0, 1), (1, 0)])  10.7 us
    all_to_all x1, starting transfers between devices, on_device(): panels = lax.all_to_all(panel, around, 0, 0, tiled=True).reshape(-1, width)  6.82 us
    unnamed x14, local copies, waits for them, and re-layouts  5.52 us
    ppermute x1, starting transfers between devices, on_device(): first = lax.ppermute(quarter, ('zh', 'c'), near)  5.26 us
  transfers between devices with their start and end apart: 5, of which 4 were waited for; matrix products, arithmetic and copies ran while one was open for 0% of the time, Pallas kernels for 3%

profile of v6, /device:TPU:1, one launch (start us, length us, event | category | flops | bytes accessed | tf_op | source)
XLA Modules:
  0.0 139.3 jit_solution(7889909728867604965)
XLA Ops:
  0.0 0.0 copy-start
  0.0 1.0 copy-done
  1.0 8.8 %collective-permute-start.3 = (bf16[768,1280]{1,0:T(8,128)(2,1)}, bf16[768,1280]{1,0:T(8,128)(2,1)S(1)}, u32[]{:S(2)}, u32[]{:S(2)}) collective-permute-start(bf16[768,1280]{1,0:T(8,128)(2,1)} %own_ref), channel_id=1, source_target_pairs={{0,1},{1,0},{2,3},{3,2},{4,5},{5,4},{6,7},{7,6},{8,9},{9,8},{10,11... | collective-permute-start | bytes 5898248 | tf_op jit(solution)/shard_map/ppermute | solution.py:225
  9.8 5.3 %collective-permute-start.1 = (bf16[32,1280]{1,0:T(8,128)(2,1)S(1)}, bf16[32,1280]{1,0:T(8,128)(2,1)S(1)}, u32[]{:S(2)}, u32[]{:S(2)}) collective-permute-start(bf16[32,1280]{1,0:T(8,128)(2,1)S(1)} %dynamic-slice_bitcast_fusion.own_ref), channel_id=1, source_target_pairs={{0,32},{1,65},{32,0},{33,97},{64,96},{65,1},{96,64},{97,33},{2,34}... | collective-permute-start | bytes 245768 | tf_op jit(solution)/shard_map/ppermute | solution.py:243
  15.0 1.9 %collective-permute-start.2 = (bf16[32,1280]{1,0:T(8,128)(2,1)S(1)}, bf16[32,1280]{1,0:T(8,128)(2,1)S(1)}, u32[]{:S(2)}, u32[]{:S(2)}) collective-permute-start(bf16[32,1280]{1,0:T(8,128)(2,1)S(1)} %dynamic-slice_bitcast_fusion.own_ref), channel_id=1, source_target_pairs={{1,97},{33,65},{65,33},{97,1},{3,99},{35,67},{67,35},{99,3},{5,101... | collective-permute-start | bytes 245768 | tf_op jit(solution)/shard_map/ppermute | solution.py:244
  17.0 0.1 pad_add_fusion.1.place
  17.1 2.2 %collective-permute-done.1.first_ref = bf16[32,1280]{1,0:T(8,128)(2,1)S(1)} collective-permute-done((bf16[32,1280]{1,0:T(8,128)(2,1)S(1)}, bf16[32,1280]{1,0:T(8,128)(2,1)S(1)}, u32[]{:S(2)}, u32[]{:S(2)}) %collective-permute-start.1) | collective-permute-done | bytes 81952 | tf_op jit(solution)/shard_map/ppermute | solution.py:243
  19.3 3.1 %collective-permute-done.2.second_ref = bf16[32,1280]{1,0:T(8,128)(2,1)S(1)} collective-permute-done((bf16[32,1280]{1,0:T(8,128)(2,1)S(1)}, bf16[32,1280]{1,0:T(8,128)(2,1)S(1)}, u32[]{:S(2)}, u32[]{:S(2)}) %collective-permute-start.2) | collective-permute-done | bytes 81952 | tf_op jit(solution)/shard_map/ppermute | solution.py:244
  22.4 2.4 %spread.1 = bf16[16,64,1280]{2,1,0:T(8,128)(2,1)} custom-call(s32[2]{0:T(128)S(1)} %pad_add_fusion.1.place, bf16[32,1280]{1,0:T(8,128)(2,1)S(1)} %dynamic-slice_bitcast_fusion.own_ref, bf16[32,1280]{1,0:T(8,128)(2,1)S(1)} %collective-permute-done.1.first_ref, bf16[32,1280]{1,0:T(8,128)(2,1)S(1)} %collective-permute-done.2.second_ref), custom_call_target="tpu_custom_call" | custom-call | tf_op jit(solution)/shard_map/spread/pallas_call | solution.py:61
  24.8 0.0 copy-start.4
  24.8 0.0 copy-start.5
  24.8 0.0 collective-permute-done.3.other_ref
  24.8 0.0 copy-start.2
  24.9 1.3 copy-done.2
  26.1 6.8 %all-to-all-start = ((bf16[16,64,1280]{2,1,0:T(8,128)(2,1)}), bf16[16,64,1280]{2,1,0:T(8,128)(2,1)S(1)}, u32[]{:S(2)}, u32[]{:S(2)}) async-start(bf16[16,64,1280]{2,1,0:T(8,128)(2,1)} %spread.1), calls=%async_computation | async-start | bytes 5242880 | tf_op jit(solution)/shard_map/all_to_all | solution.py:256
  33.0 0.0 copy-done.4
  33.0 0.1 copy.9
  33.0 0.1 reshape.24
  33.1 0.0 copy-done.5
  33.2 0.1 copy.10
  33.2 0.1 reshape.25
  34.0 0.1 pad_add_fusion.2
  34.1 1.9 %collective-permute-start = (s32[128]{0:T(128)S(1)}, s32[128]{0:T(128)S(1)}, u32[]{:S(2)}, u32[]{:S(2)}) collective-permute-start(s32[128]{0:T(128)S(1)} %pad.4), channel_id=1, source_target_pairs={{0,1},{1,0},{2,3},{3,2},{4,5},{5,4},{6,7},{7,6},{8,9},{9,8},{10,11... | collective-permute-start | bytes 1544 | tf_op jit(solution)/shard_map/ppermute | solution.py:225
  36.0 1.1 collective-permute-done
  37.1 1.7 %plan.1.lists = s32[53]{0:T(128)S(1)} custom-call(s32[2]{0:T(128)S(1)} %pad_add_fusion.1.place, s32[256]{0:T(256)S(1)} %pad_add_fusion.meta), custom_call_target="tpu_custom_call" | custom-call | tf_op jit(solution)/shard_map/plan/pallas_call | solution.py:107
  38.8 21.6 %all-to-all-done = bf16[16,64,1280]{2,1,0:T(8,128)(2,1)S(1)} async-done(((bf16[16,64,1280]{2,1,0:T(8,128)(2,1)}), bf16[16,64,1280]{2,1,0:T(8,128)(2,1)S(1)}, u32[]{:S(2)}, u32[]{:S(2)}) %all-to-all-start) | async-done | bytes 2621472 | tf_op jit(solution)/shard_map/all_to_all | solution.py:256
  60.4 0.0 copy-start.1
  60.4 1.5 %copy-done.1 = bf16[768,1280]{1,0:T(8,128)(2,1)S(1)} copy-done((bf16[768,1280]{1,0:T(8,128)(2,1)S(1)}, bf16[768,1280]{1,0:T(8,128)(2,1)}, u32[]{:S(2)}) %copy-start.1) | copy-done | bytes 1966104
  62.0 0.0 copy-start.3
  62.0 1.5 %copy-done.3 = bf16[768,1280]{1,0:T(8,128)(2,1)S(1)} copy-done((bf16[768,1280]{1,0:T(8,128)(2,1)S(1)}, bf16[768,1280]{1,0:T(8,128)(2,1)}, u32[]{:S(2)}) %copy-start.3) | copy-done | bytes 1966104
  63.5 11.5 %align.1 = bf16[1024,1280]{1,0:T(8,128)(2,1)S(1)} custom-call(s32[53]{0:T(128)S(1)} %plan.1.lists, bf16[1024,1280]{1,0:T(8,128)(2,1)S(1)} %bitcast.10, bf16[768,1280]{1,0:T(8,128)(2,1)S(1)} %copy-done.1, bf16[768,1280]{1,0:T(8,128)(2,1)S(1)} %copy-done.3), custom_call_target="tpu_custom_call" | custom-call | flops 8053063680 | tf_op jit(solution)/shard_map/align/pallas_call | solution.py:181
  75.0 38.2 %all_to_all.15.parts_ref = bf16[32,32,1280]{2,1,0:T(8,128)(2,1)S(1)} all-to-all(bf16[32,32,1280]{2,1,0:T(8,128)(2,1)S(1)} %bitcast.11), channel_id=1, replica_groups=mesh['x'=4,'zh'=4,'yq'=4,'yp'=2,'zl'=2,'c'=2] {'x','yp','zl','c'}, dimensions={0} | all-to-all | bytes 5242880 | tf_op jit(solution)/shard_map/all_to_all | solution.py:262
  113.2 0.9 combine.1
  114.1 24.5 %all_to_all.16 = bf16[16,4,1280]{2,1,0:T(4,128)(2,1)S(1)} all-to-all(bf16[16,4,1280]{2,1,0:T(4,128)(2,1)S(1)} %reshape.30), channel_id=1, replica_groups=mesh['x'=4,'zh'=4,'yq'=4,'yp'=2,'zl'=2,'c'=2] {'zh','yq'}, dimensions={0} | all-to-all | bytes 327680 | tf_op jit(solution)/shard_map/all_to_all | solution.py:264
  138.6 0.7 reduce_sum.12
  (4 shorter events, 0.1 us)
Async XLA Ops:
  0.0 1.0 copy-start
  1.0 23.9 %collective-permute-start.3 = (bf16[768,1280]{1,0:T(8,128)(2,1)}, bf16[768,1280]{1,0:T(8,128)(2,1)S(1)}, u32[]{:S(2)}, u32[]{:S(2)}) collective-permute-start(bf16[768,1280]{1,0:T(8,128)(2,1)} %own_ref), channel_id=1, source_target_pairs={{0,1},{1,0},{2,3},{3,2},{4,5},{5,4},{6,7},{7,6},{8,9},{9,8},{10,11... | collective-permute-start | bytes 5898248 | tf_op jit(solution)/shard_map/ppermute | solution.py:225
  9.8 9.5 %collective-permute-start.1 = (bf16[32,1280]{1,0:T(8,128)(2,1)S(1)}, bf16[32,1280]{1,0:T(8,128)(2,1)S(1)}, u32[]{:S(2)}, u32[]{:S(2)}) collective-permute-start(bf16[32,1280]{1,0:T(8,128)(2,1)S(1)} %dynamic-slice_bitcast_fusion.own_ref), channel_id=1, source_target_pairs={{0,32},{1,65},{32,0},{33,97},{64,96},{65,1},{96,64},{97,33},{2,34}... | collective-permute-start | bytes 245768 | tf_op jit(solution)/shard_map/ppermute | solution.py:243
  15.0 7.4 %collective-permute-start.2 = (bf16[32,1280]{1,0:T(8,128)(2,1)S(1)}, bf16[32,1280]{1,0:T(8,128)(2,1)S(1)}, u32[]{:S(2)}, u32[]{:S(2)}) collective-permute-start(bf16[32,1280]{1,0:T(8,128)(2,1)S(1)} %dynamic-slice_bitcast_fusion.own_ref), channel_id=1, source_target_pairs={{1,97},{33,65},{65,33},{97,1},{3,99},{35,67},{67,35},{99,3},{5,101... | collective-permute-start | bytes 245768 | tf_op jit(solution)/shard_map/ppermute | solution.py:244
  24.8 8.1 %copy-start.4 = (s32[1,24,2]{1,2,0:T(2,128)S(1)}, s32[1,24,2]{1,2,0:T(2,128)}, u32[]{:S(2)}) copy-start(s32[1,24,2]{1,2,0:T(2,128)} %param.7) | copy-start | bytes 580
  24.8 8.3 %copy-start.5 = (s32[1,24,2]{1,2,0:T(2,128)S(1)}, s32[1,24,2]{1,2,0:T(2,128)}, u32[]{:S(2)}) copy-start(s32[1,24,2]{1,2,0:T(2,128)} %param.8) | copy-start | bytes 580
  24.8 1.3 copy-start.2
  26.1 34.3 %all-to-all-start = ((bf16[16,64,1280]{2,1,0:T(8,128)(2,1)}), bf16[16,64,1280]{2,1,0:T(8,128)(2,1)S(1)}, u32[]{:S(2)}, u32[]{:S(2)}) async-start(bf16[16,64,1280]{2,1,0:T(8,128)(2,1)} %spread.1), calls=%async_computation | async-start | bytes 5242880 | tf_op jit(solution)/shard_map/all_to_all | solution.py:256
  34.1 3.0 %collective-permute-start = (s32[128]{0:T(128)S(1)}, s32[128]{0:T(128)S(1)}, u32[]{:S(2)}, u32[]{:S(2)}) collective-permute-start(s32[128]{0:T(128)S(1)} %pad.4), channel_id=1, source_target_pairs={{0,1},{1,0},{2,3},{3,2},{4,5},{5,4},{6,7},{7,6},{8,9},{9,8},{10,11... | collective-permute-start | bytes 1544 | tf_op jit(solution)/shard_map/ppermute | solution.py:225
  60.4 1.5 %copy-start.1 = (bf16[768,1280]{1,0:T(8,128)(2,1)S(1)}, bf16[768,1280]{1,0:T(8,128)(2,1)}, u32[]{:S(2)}) copy-start(bf16[768,1280]{1,0:T(8,128)(2,1)} %own_ref) | copy-start | bytes 5898244
  62.0 1.5 %copy-start.3 = (bf16[768,1280]{1,0:T(8,128)(2,1)S(1)}, bf16[768,1280]{1,0:T(8,128)(2,1)}, u32[]{:S(2)}) copy-start(bf16[768,1280]{1,0:T(8,128)(2,1)} %copy-done.2) | copy-start | bytes 5898244

commit v7 on v6

--- a/solution.py
+++ b/solution.py
@@ -239,7 +239,6 @@
     quarter = quarter.reshape(tile // QUARTERS, width)
     near = [(2 * z + c, 2 * (z ^ (1 + c)) + c) for z in range(places) for c in range(2)]
     far = [(2 * z + 1, 2 * (z ^ 3) + 1) for z in range(places)]
-    quarter, database = lax.optimization_barrier((quarter, database))
     first = lax.ppermute(quarter, ("zh", "c"), near)
     second = lax.ppermute(quarter, ("zh", "c"), far)
 
@@ -247,12 +246,12 @@
     own_meta = jnp.pad(own_meta, (0, 128 - own_meta.shape[0]))
     meta = jnp.concatenate([own_meta, sibling(own_meta)])
     lists = plan(place, meta, database.shape[0] // tile, slots)
-    other = sibling(database)
 
     around = ("x", "yp", "zl")
     peers = math.prod(lax.axis_size(axis) for axis in around)
     panel = spread(place, quarter, first, second, peers)
-    panel, other = lax.optimization_barrier((panel, other))
+    panel, database = lax.optimization_barrier((panel, database))
+    other = sibling(database)
     panels = lax.all_to_all(panel, around, 0, 0, tiled=True).reshape(-1, width)
 
     terms = align(lists, panels, database, other)

time: 140 us -> 138 us (0.986)
  local copies, waits for them, and re-layouts: 5.77 us -> 2.95 us
  Pallas kernels: 16.4 us -> 18.1 us
    ppermute x1, starting transfers between devices: 1.94 us -> 11.5 us  [on_device(): second = lax.ppermute(quarter, ('zh', 'c'), far)]
    ppermute x2, starting transfers between devices: 10.7 us -> 4.32 us  [sibling(): return lax.ppermute(value, 'c', [(0, 1), (1, 0)])]
    ppermute x1, waiting for transfers between devices: 2.25 us -> 7.94 us  [on_device(): first = lax.ppermute(quarter, ('zh', 'c'), near)]
    ppermute x1, starting transfers between devices: 5.26 us -> 1.92 us  [on_device(): first = lax.ppermute(quarter, ('zh', 'c'), near)]
    ppermute x1, waiting for transfers between devices: 3.11 us -> 0.01 us  [on_device(): second = lax.ppermute(quarter, ('zh', 'c'), far)]
    all_to_all x1, waiting for transfers between devices: 21.6 us -> 18.8 us  [on_device(): panels = lax.all_to_all(panel, around, 0, 0, tiled=True).reshape(-1, width)]
    unnamed x14 -> x10, local copies, waits for them, and re-layouts: 5.52 us -> 2.7 us
    pallas_call x1, Pallas kernels: 11.5 us -> 13 us  [align(): pl.pallas_call(functools.partial(align_kernel, width ** (-0.5)), in_specs...]
  transfers between devices with their start and end apart: 5 -> 5, of which waited for: 4 -> 3; matrix products, arithmetic and copies ran while one was open for 0% -> 0% of each run, Pallas kernels for 3% -> 1%
where the time goes in v7:
time: 138 us
  blocking collectives  63.7 us (46%)
  waiting for transfers between devices  27.5 us (20%)
  starting transfers between devices  23.8 us (17%)
  Pallas kernels  18.1 us (13%)
  local copies, waits for them, and re-layouts  2.95 us (2%)
    all_to_all x1, blocking collectives, on_device(): lax.all_to_all(terms.reshape(peers, -1, width), around, 0, 0, tiled=True)  38.8 us
    all_to_all x1, blocking collectives, on_device(): lax.all_to_all(column.reshape(-1, 4, width), ('zh', 'yq'), 0, 0, tiled=True)  24.9 us
    all_to_all x1, waiting for transfers between devices, on_device(): panels = lax.all_to_all(panel, around, 0, 0, tiled=True).reshape(-1, width)  18.8 us
    pallas_call x1, Pallas kernels, align(): pl.pallas_call(functools.partial(align_kernel, width ** (-0.5)), in_specs...  13 us
    ppermute x1, starting transfers between devices, on_device(): second = lax.ppermute(quarter, ('zh', 'c'), far)  11.5 us
    ppermute x1, waiting for transfers between devices, on_device(): first = lax.ppermute(quarter, ('zh', 'c'), near)  7.94 us
    all_to_all x1, starting transfers between devices, on_device(): panels = lax.all_to_all(panel, around, 0, 0, tiled=True).reshape(-1, width)  6.08 us
    ppermute x2, starting transfers between devices, sibling(): return lax.ppermute(value, 'c', [(0, 1), (1, 0)])  4.32 us
  transfers between devices with their start and end apart: 5, of which 3 were waited for; matrix products, arithmetic and copies ran while one was open for 0% of the time, Pallas kernels for 1%

profile of v7, /device:TPU:1, one launch (start us, length us, event | category | flops | bytes accessed | tf_op | source)
XLA Modules:
  0.0 137.6 jit_solution(1932072686315759933)
XLA Ops:
  0.0 0.0 copy-start
  0.0 1.0 copy-done
  1.0 11.5 %collective-permute-start.2 = (bf16[32,1280]{1,0:T(8,128)(2,1)S(1)}, bf16[32,1280]{1,0:T(8,128)(2,1)S(1)}, u32[]{:S(2)}, u32[]{:S(2)}) collective-permute-start(bf16[32,1280]{1,0:T(8,128)(2,1)S(1)} %dynamic-slice_bitcast_fusion.own_ref), channel_id=1, source_target_pairs={{1,97},{33,65},{65,33},{97,1},{3,99},{35,67},{67,35},{99,3},{5,101... | collective-permute-start | bytes 245768 | tf_op jit(solution)/shard_map/ppermute | solution.py:243
  12.5 1.9 %collective-permute-start.1 = (bf16[32,1280]{1,0:T(8,128)(2,1)S(1)}, bf16[32,1280]{1,0:T(8,128)(2,1)S(1)}, u32[]{:S(2)}, u32[]{:S(2)}) collective-permute-start(bf16[32,1280]{1,0:T(8,128)(2,1)S(1)} %dynamic-slice_bitcast_fusion.own_ref), channel_id=1, source_target_pairs={{0,32},{1,65},{32,0},{33,97},{64,96},{65,1},{96,64},{97,33},{2,34}... | collective-permute-start | bytes 245768 | tf_op jit(solution)/shard_map/ppermute | solution.py:242
  14.4 0.1 pad_add_fusion.1.place
  14.5 0.0 collective-permute-done.2.second_ref
  14.5 7.9 %collective-permute-done.1.first_ref = bf16[32,1280]{1,0:T(8,128)(2,1)S(1)} collective-permute-done((bf16[32,1280]{1,0:T(8,128)(2,1)S(1)}, bf16[32,1280]{1,0:T(8,128)(2,1)S(1)}, u32[]{:S(2)}, u32[]{:S(2)}) %collective-permute-start.1) | collective-permute-done | bytes 81952 | tf_op jit(solution)/shard_map/ppermute | solution.py:242
  22.4 2.4 %spread.1 = bf16[16,64,1280]{2,1,0:T(8,128)(2,1)} custom-call(s32[2]{0:T(128)S(1)} %pad_add_fusion.1.place, bf16[32,1280]{1,0:T(8,128)(2,1)S(1)} %dynamic-slice_bitcast_fusion.own_ref, bf16[32,1280]{1,0:T(8,128)(2,1)S(1)} %collective-permute-done.1.first_ref, bf16[32,1280]{1,0:T(8,128)(2,1)S(1)} %collective-permute-done.2.second_ref), custom_call_target="tpu_custom_call" | custom-call | tf_op jit(solution)/shard_map/spread/pallas_call | solution.py:61
  24.8 0.0 copy-start.2
  24.8 0.0 copy-start.3
  24.8 6.1 %all-to-all-start = ((bf16[16,64,1280]{2,1,0:T(8,128)(2,1)}), bf16[16,64,1280]{2,1,0:T(8,128)(2,1)S(1)}, u32[]{:S(2)}, u32[]{:S(2)}) async-start(bf16[16,64,1280]{2,1,0:T(8,128)(2,1)} %spread.1), calls=%async_computation | async-start | bytes 5242880 | tf_op jit(solution)/shard_map/all_to_all | solution.py:255
  30.9 1.9 %collective-permute-start.3 = (bf16[768,1280]{1,0:T(8,128)(2,1)}, bf16[768,1280]{1,0:T(8,128)(2,1)}, u32[]{:S(2)}, u32[]{:S(2)}) collective-permute-start(bf16[768,1280]{1,0:T(8,128)(2,1)} %own_ref), channel_id=1, source_target_pairs={{0,1},{1,0},{2,3},{3,2},{4,5},{5,4},{6,7},{7,6},{8,9},{9,8},{10,11... | collective-permute-start | bytes 5898248 | tf_op jit(solution)/shard_map/ppermute | solution.py:225
  33.5 0.0 copy-done.2
  33.5 0.1 copy.9
  33.6 0.1 reshape.24
  33.7 0.0 copy-done.3
  33.7 0.1 copy.10
  33.8 0.1 reshape.25
  33.9 0.1 pad_add_fusion.2
  34.0 2.4 %collective-permute-start = (s32[128]{0:T(128)S(1)}, s32[128]{0:T(128)S(1)}, u32[]{:S(2)}, u32[]{:S(2)}) collective-permute-start(s32[128]{0:T(128)S(1)} %pad.4), channel_id=1, source_target_pairs={{0,1},{1,0},{2,3},{3,2},{4,5},{5,4},{6,7},{7,6},{8,9},{9,8},{10,11... | collective-permute-start | bytes 1544 | tf_op jit(solution)/shard_map/ppermute | solution.py:225
  36.4 0.8 collective-permute-done
  37.2 1.9 %plan.1.lists = s32[53]{0:T(128)S(1)} custom-call(s32[2]{0:T(128)S(1)} %pad_add_fusion.1.place, s32[256]{0:T(256)S(1)} %pad_add_fusion.meta), custom_call_target="tpu_custom_call" | custom-call | tf_op jit(solution)/shard_map/plan/pallas_call | solution.py:107
  39.1 0.0 collective-permute-done.3.other_ref
  39.1 18.8 %all-to-all-done = bf16[16,64,1280]{2,1,0:T(8,128)(2,1)S(1)} async-done(((bf16[16,64,1280]{2,1,0:T(8,128)(2,1)}), bf16[16,64,1280]{2,1,0:T(8,128)(2,1)S(1)}, u32[]{:S(2)}, u32[]{:S(2)}) %all-to-all-start) | async-done | bytes 2621472 | tf_op jit(solution)/shard_map/all_to_all | solution.py:255
  57.8 0.0 copy-start.1
  57.8 1.5 %copy-done.1 = bf16[768,1280]{1,0:T(8,128)(2,1)S(1)} copy-done((bf16[768,1280]{1,0:T(8,128)(2,1)S(1)}, bf16[768,1280]{1,0:T(8,128)(2,1)}, u32[]{:S(2)}) %copy-start.1) | copy-done | bytes 1966104
  59.4 13.0 %align.1 = bf16[1024,1280]{1,0:T(8,128)(2,1)S(1)} custom-call(s32[53]{0:T(128)S(1)} %plan.1.lists, bf16[1024,1280]{1,0:T(8,128)(2,1)S(1)} %bitcast.10, bf16[768,1280]{1,0:T(8,128)(2,1)S(1)} %copy-done.1, bf16[768,1280]{1,0:T(8,128)(2,1)} %collective-permute-done.3.other_ref), custom_call_target="tpu_custom_call" | custom-call | flops 8053063680 | tf_op jit(solution)/shard_map/align/pallas_call | solution.py:181
  72.3 38.8 %all_to_all.15.parts_ref = bf16[32,32,1280]{2,1,0:T(8,128)(2,1)S(1)} all-to-all(bf16[32,32,1280]{2,1,0:T(8,128)(2,1)S(1)} %bitcast.11), channel_id=1, replica_groups=mesh['x'=4,'zh'=4,'yq'=4,'yp'=2,'zl'=2,'c'=2] {'x','yp','zl','c'}, dimensions={0} | all-to-all | bytes 5242880 | tf_op jit(solution)/shard_map/all_to_all | solution.py:261
  111.1 0.9 combine.1
  112.1 24.9 %all_to_all.16 = bf16[16,4,1280]{2,1,0:T(4,128)(2,1)S(1)} all-to-all(bf16[16,4,1280]{2,1,0:T(4,128)(2,1)S(1)} %reshape.30), channel_id=1, replica_groups=mesh['x'=4,'zh'=4,'yq'=4,'yp'=2,'zl'=2,'c'=2] {'zh','yq'}, dimensions={0} | all-to-all | bytes 327680 | tf_op jit(solution)/shard_map/all_to_all | solution.py:263
  136.9 0.7 reduce_sum.12
  (4 shorter events, 0.1 us)
Async XLA Ops:
  0.0 1.0 copy-start
  1.0 13.5 %collective-permute-start.2 = (bf16[32,1280]{1,0:T(8,128)(2,1)S(1)}, bf16[32,1280]{1,0:T(8,128)(2,1)S(1)}, u32[]{:S(2)}, u32[]{:S(2)}) collective-permute-start(bf16[32,1280]{1,0:T(8,128)(2,1)S(1)} %dynamic-slice_bitcast_fusion.own_ref), channel_id=1, source_target_pairs={{1,97},{33,65},{65,33},{97,1},{3,99},{35,67},{67,35},{99,3},{5,101... | collective-permute-start | bytes 245768 | tf_op jit(solution)/shard_map/ppermute | solution.py:243
  12.5 9.9 %collective-permute-start.1 = (bf16[32,1280]{1,0:T(8,128)(2,1)S(1)}, bf16[32,1280]{1,0:T(8,128)(2,1)S(1)}, u32[]{:S(2)}, u32[]{:S(2)}) collective-permute-start(bf16[32,1280]{1,0:T(8,128)(2,1)S(1)} %dynamic-slice_bitcast_fusion.own_ref), channel_id=1, source_target_pairs={{0,32},{1,65},{32,0},{33,97},{64,96},{65,1},{96,64},{97,33},{2,34}... | collective-permute-start | bytes 245768 | tf_op jit(solution)/shard_map/ppermute | solution.py:242
  24.8 8.7 %copy-start.2 = (s32[1,24,2]{1,2,0:T(2,128)S(1)}, s32[1,24,2]{1,2,0:T(2,128)}, u32[]{:S(2)}) copy-start(s32[1,24,2]{1,2,0:T(2,128)} %param.7) | copy-start | bytes 580
  24.8 8.9 %copy-start.3 = (s32[1,24,2]{1,2,0:T(2,128)S(1)}, s32[1,24,2]{1,2,0:T(2,128)}, u32[]{:S(2)}) copy-start(s32[1,24,2]{1,2,0:T(2,128)} %param.8) | copy-start | bytes 580
  24.8 33.0 %all-to-all-start = ((bf16[16,64,1280]{2,1,0:T(8,128)(2,1)}), bf16[16,64,1280]{2,1,0:T(8,128)(2,1)S(1)}, u32[]{:S(2)}, u32[]{:S(2)}) async-start(bf16[16,64,1280]{2,1,0:T(8,128)(2,1)} %spread.1), calls=%async_computation | async-start | bytes 5242880 | tf_op jit(solution)/shard_map/all_to_all | solution.py:255
  30.9 8.1 %collective-permute-start.3 = (bf16[768,1280]{1,0:T(8,128)(2,1)}, bf16[768,1280]{1,0:T(8,128)(2,1)}, u32[]{:S(2)}, u32[]{:S(2)}) collective-permute-start(bf16[768,1280]{1,0:T(8,128)(2,1)} %own_ref), channel_id=1, source_target_pairs={{0,1},{1,0},{2,3},{3,2},{4,5},{5,4},{6,7},{7,6},{8,9},{9,8},{10,11... | collective-permute-start | bytes 5898248 | tf_op jit(solution)/shard_map/ppermute | solution.py:225
  34.0 3.2 %collective-permute-start = (s32[128]{0:T(128)S(1)}, s32[128]{0:T(128)S(1)}, u32[]{:S(2)}, u32[]{:S(2)}) collective-permute-start(s32[128]{0:T(128)S(1)} %pad.4), channel_id=1, source_target_pairs={{0,1},{1,0},{2,3},{3,2},{4,5},{5,4},{6,7},{7,6},{8,9},{9,8},{10,11... | collective-permute-start | bytes 1544 | tf_op jit(solution)/shard_map/ppermute | solution.py:225
  57.8 1.5 %copy-start.1 = (bf16[768,1280]{1,0:T(8,128)(2,1)S(1)}, bf16[768,1280]{1,0:T(8,128)(2,1)}, u32[]{:S(2)}) copy-start(bf16[768,1280]{1,0:T(8,128)(2,1)} %own_ref) | copy-start | bytes 5898244

commit v8 on v7

--- a/solution.py
+++ b/solution.py
@@ -29,21 +29,14 @@
     return weight.astype(jnp.bfloat16)
 
 
-def spread_kernel(place, own_ref, first_ref, second_ref, out_ref, held, sent):
-    near, odd = place[0] == 0, place[1] & 1
-    both = jnp.concatenate(
-        [
-            jnp.where(near, own_ref[...], first_ref[...]),
-            jnp.where(near, first_ref[...], second_ref[...]),
-        ]
-    )
-    count = both.shape[0]
+def spread_kernel(rows_ref, out_ref, held, sent):
+    count = rows_ref.shape[0]
     to = lax.broadcasted_iota(jnp.int32, (count, count), 0)
     row = lax.broadcasted_iota(jnp.int32, (count, count), 1)
-    wanted = (((to >> 4) & 1) ^ odd) * 32 + ((to >> 2) & 3) * 8 + (to >> 5) * 4 + (to & 3)
+    wanted = ((to >> 2) & 3) * 16 + (to >> 4) * 4 + (to & 3)
     both = jnp.dot(
-        (row == wanted).astype(both.dtype), both, preferred_element_type=jnp.float32
-    ).astype(both.dtype)
+        (row == wanted).astype(rows_ref.dtype), rows_ref[...], preferred_element_type=jnp.float32
+    ).astype(rows_ref.dtype)
     held[...] = both
     copies = [
         pltpu.make_async_copy(held, out_ref.at[peer], sent.at[peer])
@@ -55,21 +48,19 @@
         copy.wait()
 
 
-def spread(place, own, first, second, peers):
-    rows, width = own.shape
-    vmem = pl.BlockSpec(memory_space=pltpu.VMEM)
+def spread(rows, peers):
     return pl.pallas_call(
         spread_kernel,
-        in_specs=[pl.BlockSpec(memory_space=pltpu.SMEM)] + [vmem] * 3,
+        in_specs=[pl.BlockSpec(memory_space=pltpu.VMEM)],
         out_specs=pl.BlockSpec(memory_space=pl.ANY),
         scratch_shapes=[
-            pltpu.VMEM((HALF * rows, width), jnp.bfloat16),
+            pltpu.VMEM(rows.shape, jnp.bfloat16),
             pltpu.SemaphoreType.DMA((peers,)),
         ],
-        out_shape=jax.ShapeDtypeStruct((peers, HALF * rows, width), jnp.bfloat16),
+        out_shape=jax.ShapeDtypeStruct((peers, *rows.shape), jnp.bfloat16),
         compiler_params=pltpu.CompilerParams(vmem_limit_bytes=8 * 1024 * 1024),
         name="spread",
-    )(place, own, first, second)
+    )(rows)
 
 
 def plan_kernel(tiles, slots, place, meta, lists):
@@ -93,6 +84,7 @@
                     + 16 * (meta[base + 2 * slot + 1] + side * tiles)
                     + 256 * meta[base + 2 * slots + 2 * slot]
                     + 65536 * meta[base + 2 * slots + 2 * slot + 1]
+                    + 16777216 * (near & 1)
                 )
 
             return carry
@@ -147,14 +139,19 @@
         made = []
         for k in range(UNROLL):
             slot = lists[1 + index * UNROLL + k]
-            first = ((slot >> 1) & 7) * group + (slot & 1) * piece
+            start = ((slot >> 1) & 7) * group
+            scored = [
+                pl.ds(pl.multiple_of(start + pair * TILE + (slot >> 24) * 64, 64), 64)
+                for pair in range(2)
+            ]
+            first = start + (slot & 1) * piece
             at_rows = [
                 pl.ds(pl.multiple_of(first + step * HALF * piece, piece), piece)
                 for step in range(pieces)
             ]
             at_col = pl.ds(pl.multiple_of(((slot >> 4) & 15) * TILE, TILE), TILE)
-            score = jnp.concatenate([scores[at_row, at_col] for at_row in at_rows])
-            weight = pair_weight(score, rows, cols, (slot >> 8) & 255, slot >> 16)
+            score = jnp.concatenate([scores[at_row, at_col] for at_row in scored])
+            weight = pair_weight(score, rows, cols, (slot >> 8) & 255, (slot >> 16) & 255)
             made.append((at_rows, at_col, weight))
         for at_rows, at_col, weight in made:
             for step, at_row in enumerate(at_rows):
@@ -231,16 +228,17 @@
     core = lax.axis_index("c").astype(jnp.int32)
     deep = lax.axis_index("zh").astype(jnp.int32)
     place = jnp.stack([core, deep])
-    places = lax.axis_size("zh")
-
-    quarter = queries.reshape(lax.axis_size("yq"), 2, 2, 8, width)
-    quarter = lax.dynamic_index_in_dim(quarter, lax.axis_index("yp"), 1, keepdims=False)
-    quarter = lax.dynamic_index_in_dim(quarter, lax.axis_index("zl"), 1, keepdims=False)
-    quarter = quarter.reshape(tile // QUARTERS, width)
-    near = [(2 * z + c, 2 * (z ^ (1 + c)) + c) for z in range(places) for c in range(2)]
-    far = [(2 * z + 1, 2 * (z ^ 3) + 1) for z in range(places)]
-    first = lax.ppermute(quarter, ("zh", "c"), near)
-    second = lax.ppermute(quarter, ("zh", "c"), far)
+
+    half = queries.reshape(lax.axis_size("yq"), 2, 16, width)
+    half = lax.dynamic_index_in_dim(half, lax.axis_index("yp"), 1, keepdims=False)
+    half = half.reshape(tile // 2, width)
+    route = [
+        ((4 * (z ^ (2 * c + low)) + 2 * low + c), 4 * z + 2 * low + c)
+        for z in range(lax.axis_size("zh"))
+        for low in range(2)
+        for c in range(2)
+    ]
+    fetched = lax.ppermute(half, ("zh", "zl", "c"), route)
 
     own_meta = jnp.concatenate([pair_tiles.reshape(-1), pair_lengths.reshape(-1), live_pairs])
     own_meta = jnp.pad(own_meta, (0, 128 - own_meta.shape[0]))
@@ -249,7 +247,7 @@
 
     around = ("x", "yp", "zl")
     peers = math.prod(lax.axis_size(axis) for axis in around)
-    panel = spread(place, quarter, first, second, peers)
+    panel = spread(fetched, peers)
     panel, database = lax.optimization_barrier((panel, database))
     other = sibling(database)
     panels = lax.all_to_all(panel, around, 0, 0, tiled=True).reshape(-1, width)

time: 138 us -> 137 us (level)
  waiting for transfers between devices: 27.5 us -> 24 us
  blocking collectives: 63.7 us -> 66.2 us
    ppermute x2 -> x1, waiting for transfers between devices: 7.94 us -> 2.89 us  [on_device(): fetched = lax.ppermute(half, ('zh', 'zl', 'c'), route)]
    all_to_all x1, starting transfers between devices: 6.08 us -> 9.25 us  [on_device(): panels = lax.all_to_all(panel, around, 0, 0, tiled=True).reshape(-1, width)]
    all_to_all x1, blocking collectives: 24.9 us -> 27.6 us  [on_device(): lax.all_to_all(column.reshape(-1, 4, width), ('zh', 'yq'), 0, 0, tiled=True)]
    ppermute x2 -> x1, starting transfers between devices: 13.4 us -> 11.5 us  [on_device(): fetched = lax.ppermute(half, ('zh', 'zl', 'c'), route)]
    all_to_all x1, waiting for transfers between devices: 18.8 us -> 20.4 us  [on_device(): panels = lax.all_to_all(panel, around, 0, 0, tiled=True).reshape(-1, width)]
  transfers between devices with their start and end apart: 5 -> 4, of which waited for: 3 -> 3; matrix products, arithmetic and copies ran while one was open for 0% -> 0% of each run, Pallas kernels for 1% -> 1%
where the time goes in v8:
time: 137 us
  blocking collectives  66.2 us (48%)
  starting transfers between devices  25 us (18%)
  waiting for transfers between devices  24 us (18%)
  Pallas kernels  16.9 us (12%)
  local copies, waits for them, and re-layouts  2.95 us (2%)
    all_to_all x1, blocking collectives, on_device(): lax.all_to_all(terms.reshape(peers, -1, width), around, 0, 0, tiled=True)  38.6 us
    all_to_all x1, blocking collectives, on_device(): lax.all_to_all(column.reshape(-1, 4, width), ('zh', 'yq'), 0, 0, tiled=True)  27.6 us
    all_to_all x1, waiting for transfers between devices, on_device(): panels = lax.all_to_all(panel, around, 0, 0, tiled=True).reshape(-1, width)  20.4 us
    pallas_call x1, Pallas kernels, align(): pl.pallas_call(functools.partial(align_kernel, width ** (-0.5)), in_specs...  12.5 us
    ppermute x1, starting transfers between devices, on_device(): fetched = lax.ppermute(half, ('zh', 'zl', 'c'), route)  11.5 us
    all_to_all x1, starting transfers between devices, on_device(): panels = lax.all_to_all(panel, around, 0, 0, tiled=True).reshape(-1, width)  9.25 us
    ppermute x2, starting transfers between devices, sibling(): return lax.ppermute(value, 'c', [(0, 1), (1, 0)])  4.32 us
    ppermute x1, waiting for transfers between devices, on_device(): fetched = lax.ppermute(half, ('zh', 'zl', 'c'), route)  2.89 us
  transfers between devices with their start and end apart: 4, of which 3 were waited for; matrix products, arithmetic and copies ran while one was open for 0% of the time, Pallas kernels for 1%

profile of v8, /device:TPU:1, one launch (start us, length us, event | category | flops | bytes accessed | tf_op | source)
XLA Modules:
  0.0 136.7 jit_solution(16958258876720121830)
XLA Ops:
  0.0 0.0 copy-start
  0.0 1.0 copy-done
  1.0 11.5 %collective-permute-start.1 = (bf16[64,1280]{1,0:T(8,128)(2,1)S(1)}, bf16[64,1280]{1,0:T(8,128)(2,1)S(1)}, u32[]{:S(2)}, u32[]{:S(2)}) collective-permute-start(bf16[64,1280]{1,0:T(8,128)(2,1)S(1)} %bitcast.11), channel_id=1, source_target_pairs={{0,0},{65,1},{34,2},{99,3},{32,32},{97,33},{2,34},{67,35},{64,64},... | collective-permute-start | bytes 491528 | tf_op jit(solution)/shard_map/ppermute | solution.py:241
  12.5 2.9 %collective-permute-done.1.rows_ref = bf16[64,1280]{1,0:T(8,128)(2,1)S(1)} collective-permute-done((bf16[64,1280]{1,0:T(8,128)(2,1)S(1)}, bf16[64,1280]{1,0:T(8,128)(2,1)S(1)}, u32[]{:S(2)}, u32[]{:S(2)}) %collective-permute-start.1) | collective-permute-done | bytes 163872 | tf_op jit(solution)/shard_map/ppermute | solution.py:241
  15.4 1.9 %spread.1 = bf16[16,64,1280]{2,1,0:T(8,128)(2,1)} custom-call(bf16[64,1280]{1,0:T(8,128)(2,1)S(1)} %collective-permute-done.1.rows_ref), custom_call_target="tpu_custom_call" | custom-call | tf_op jit(solution)/shard_map/spread/pallas_call | solution.py:52
  17.2 0.0 copy-start.2
  17.2 0.0 copy-start.3
  17.2 9.2 %all-to-all-start = ((bf16[16,64,1280]{2,1,0:T(8,128)(2,1)}), bf16[16,64,1280]{2,1,0:T(8,128)(2,1)S(1)}, u32[]{:S(2)}, u32[]{:S(2)}) async-start(bf16[16,64,1280]{2,1,0:T(8,128)(2,1)} %spread.1), calls=%async_computation | async-start | bytes 5242880 | tf_op jit(solution)/shard_map/all_to_all | solution.py:253
  26.5 1.9 %collective-permute-start.2 = (bf16[768,1280]{1,0:T(8,128)(2,1)}, bf16[768,1280]{1,0:T(8,128)(2,1)}, u32[]{:S(2)}, u32[]{:S(2)}) collective-permute-start(bf16[768,1280]{1,0:T(8,128)(2,1)} %own_ref), channel_id=1, source_target_pairs={{0,1},{1,0},{2,3},{3,2},{4,5},{5,4},{6,7},{7,6},{8,9},{9,8},{10,11... | collective-permute-start | bytes 5898248 | tf_op jit(solution)/shard_map/ppermute | solution.py:222
  29.1 0.0 copy-done.2
  29.1 0.1 copy.9
  29.2 0.1 reshape.22
  29.3 0.0 copy-done.3
  29.3 0.1 copy.10
  29.4 0.1 reshape.23
  29.5 0.1 pad_add_fusion.2
  29.5 2.4 %collective-permute-start = (s32[128]{0:T(128)S(1)}, s32[128]{0:T(128)S(1)}, u32[]{:S(2)}, u32[]{:S(2)}) collective-permute-start(s32[128]{0:T(128)S(1)} %pad.4), channel_id=1, source_target_pairs={{0,1},{1,0},{2,3},{3,2},{4,5},{5,4},{6,7},{7,6},{8,9},{9,8},{10,11... | collective-permute-start | bytes 1544 | tf_op jit(solution)/shard_map/ppermute | solution.py:222
  32.0 0.1 pad_add_fusion.1.place
  32.0 0.7 collective-permute-done
  32.8 1.7 %plan.1.lists = s32[53]{0:T(128)S(1)} custom-call(s32[2]{0:T(128)S(1)} %pad_add_fusion.1.place, s32[256]{0:T(256)S(1)} %pad_add_fusion.meta), custom_call_target="tpu_custom_call" | custom-call | tf_op jit(solution)/shard_map/plan/pallas_call | solution.py:99
  34.5 0.0 collective-permute-done.2.other_ref
  34.5 20.4 %all-to-all-done = bf16[16,64,1280]{2,1,0:T(8,128)(2,1)S(1)} async-done(((bf16[16,64,1280]{2,1,0:T(8,128)(2,1)}), bf16[16,64,1280]{2,1,0:T(8,128)(2,1)S(1)}, u32[]{:S(2)}, u32[]{:S(2)}) %all-to-all-start) | async-done | bytes 2621472 | tf_op jit(solution)/shard_map/all_to_all | solution.py:253
  54.9 0.0 copy-start.1
  54.9 1.5 %copy-done.1 = bf16[768,1280]{1,0:T(8,128)(2,1)S(1)} copy-done((bf16[768,1280]{1,0:T(8,128)(2,1)S(1)}, bf16[768,1280]{1,0:T(8,128)(2,1)}, u32[]{:S(2)}) %copy-start.1) | copy-done | bytes 1966104
  56.4 12.5 %align.1 = bf16[1024,1280]{1,0:T(8,128)(2,1)S(1)} custom-call(s32[53]{0:T(128)S(1)} %plan.1.lists, bf16[1024,1280]{1,0:T(8,128)(2,1)S(1)} %bitcast.9, bf16[768,1280]{1,0:T(8,128)(2,1)S(1)} %copy-done.1, bf16[768,1280]{1,0:T(8,128)(2,1)} %collective-permute-done.2.other_ref), custom_call_target="tpu_custom_call" | custom-call | flops 8053063680 | tf_op jit(solution)/shard_map/align/pallas_call | solution.py:178
  68.9 38.6 %all_to_all.15.parts_ref = bf16[32,32,1280]{2,1,0:T(8,128)(2,1)S(1)} all-to-all(bf16[32,32,1280]{2,1,0:T(8,128)(2,1)S(1)} %bitcast.10), channel_id=1, replica_groups=mesh['x'=4,'zh'=4,'yq'=4,'yp'=2,'zl'=2,'c'=2] {'x','yp','zl','c'}, dimensions={0} | all-to-all | bytes 5242880 | tf_op jit(solution)/shard_map/all_to_all | solution.py:259
  107.5 0.9 combine.1
  108.5 27.6 %all_to_all.16 = bf16[16,4,1280]{2,1,0:T(4,128)(2,1)S(1)} all-to-all(bf16[16,4,1280]{2,1,0:T(4,128)(2,1)S(1)} %reshape.28), channel_id=1, replica_groups=mesh['x'=4,'zh'=4,'yq'=4,'yp'=2,'zl'=2,'c'=2] {'zh','yq'}, dimensions={0} | all-to-all | bytes 327680 | tf_op jit(solution)/shard_map/all_to_all | solution.py:261
  136.0 0.7 reduce_sum.12
  (4 shorter events, 0.1 us)
Async XLA Ops:
  0.0 1.0 copy-start
  1.0 14.4 %collective-permute-start.1 = (bf16[64,1280]{1,0:T(8,128)(2,1)S(1)}, bf16[64,1280]{1,0:T(8,128)(2,1)S(1)}, u32[]{:S(2)}, u32[]{:S(2)}) collective-permute-start(bf16[64,1280]{1,0:T(8,128)(2,1)S(1)} %bitcast.11), channel_id=1, source_target_pairs={{0,0},{65,1},{34,2},{99,3},{32,32},{97,33},{2,34},{67,35},{64,64},... | collective-permute-start | bytes 491528 | tf_op jit(solution)/shard_map/ppermute | solution.py:241
  17.2 11.9 %copy-start.2 = (s32[1,24,2]{1,2,0:T(2,128)S(1)}, s32[1,24,2]{1,2,0:T(2,128)}, u32[]{:S(2)}) copy-start(s32[1,24,2]{1,2,0:T(2,128)} %param.7) | copy-start | bytes 580
  17.2 12.0 %copy-start.3 = (s32[1,24,2]{1,2,0:T(2,128)S(1)}, s32[1,24,2]{1,2,0:T(2,128)}, u32[]{:S(2)}) copy-start(s32[1,24,2]{1,2,0:T(2,128)} %param.8) | copy-start | bytes 580
  17.2 37.6 %all-to-all-start = ((bf16[16,64,1280]{2,1,0:T(8,128)(2,1)}), bf16[16,64,1280]{2,1,0:T(8,128)(2,1)S(1)}, u32[]{:S(2)}, u32[]{:S(2)}) async-start(bf16[16,64,1280]{2,1,0:T(8,128)(2,1)} %spread.1), calls=%async_computation | async-start | bytes 5242880 | tf_op jit(solution)/shard_map/all_to_all | solution.py:253
  26.5 8.0 %collective-permute-start.2 = (bf16[768,1280]{1,0:T(8,128)(2,1)}, bf16[768,1280]{1,0:T(8,128)(2,1)}, u32[]{:S(2)}, u32[]{:S(2)}) collective-permute-start(bf16[768,1280]{1,0:T(8,128)(2,1)} %own_ref), channel_id=1, source_target_pairs={{0,1},{1,0},{2,3},{3,2},{4,5},{5,4},{6,7},{7,6},{8,9},{9,8},{10,11... | collective-permute-start | bytes 5898248 | tf_op jit(solution)/shard_map/ppermute | solution.py:222
  29.5 3.2 %collective-permute-start = (s32[128]{0:T(128)S(1)}, s32[128]{0:T(128)S(1)}, u32[]{:S(2)}, u32[]{:S(2)}) collective-permute-start(s32[128]{0:T(128)S(1)} %pad.4), channel_id=1, source_target_pairs={{0,1},{1,0},{2,3},{3,2},{4,5},{5,4},{6,7},{7,6},{8,9},{9,8},{10,11... | collective-permute-start | bytes 1544 | tf_op jit(solution)/shard_map/ppermute | solution.py:222
  54.9 1.5 %copy-start.1 = (bf16[768,1280]{1,0:T(8,128)(2,1)S(1)}, bf16[768,1280]{1,0:T(8,128)(2,1)}, u32[]{:S(2)}) copy-start(bf16[768,1280]{1,0:T(8,128)(2,1)} %own_ref) | copy-start | bytes 5898244

commit v9 on v8

--- a/solution.py
+++ b/solution.py
@@ -116,7 +116,12 @@
     across = (((1,), (1,)), ((), ()))
     for first in range(0, total, group):
         weights[first : first + group, :] = jnp.zeros((group, 2 * width), weights.dtype)
-        query = q_ref[first : first + group, :]
+        query = jnp.concatenate(
+            [
+                q_ref[block * 64 : (block + 1) * 64, :]
+                for block in range(first // group, total // 64, total // group)
+            ]
+        )
         for side, ref in enumerate((own_ref, other_ref)):
             for at in range(0, width, CHUNK):
                 scores[first : first + group, side * width + at : side * width + at + CHUNK] = (
@@ -162,12 +167,24 @@
 
     lax.fori_loop(0, (lists[0] + UNROLL - 1) // UNROLL, batch, 0)
 
-    for first in range(0, total, group):
-        weight = weights[first : first + group, :].astype(jnp.bfloat16)
-        out_ref[first : first + group, :] = (
-            jnp.dot(weight[:, :width], own_ref[...], preferred_element_type=jnp.float32)
-            + jnp.dot(weight[:, width:], other_ref[...], preferred_element_type=jnp.float32)
+    groups = total // group
+    sent = 2 * piece
+    for index in range(groups):
+        terms = (
+            jnp.dot(
+                weights[index * group : (index + 1) * group, :width],
+                own_ref[...],
+                preferred_element_type=jnp.float32,
+            )
+            + jnp.dot(
+                weights[index * group : (index + 1) * group, width:],
+                other_ref[...],
+                preferred_element_type=jnp.float32,
+            )
         ).astype(out_ref.dtype)
+        for peer in range(group // sent):
+            at = (peer * groups + index) * sent
+            out_ref[at : at + sent, :] = terms[peer * sent : (peer + 1) * sent]
 
 
 def align(lists, queries, own, other):
@@ -192,21 +209,23 @@
     )(lists, queries, own, other)
 
 
-def combine_kernel(cores, place, parts_ref, out_ref):
+def combine_kernel(cores, groups, place, parts_ref, out_ref):
     peers, rows, _ = parts_ref.shape
     deep = place[1]
     for core in range(cores):
         total = sum(
-            parts_ref[peer].astype(jnp.float32) for peer in range(core, peers, cores)
+            parts_ref[peer].astype(jnp.float32)
+            for peer in range(peers)
+            if peer // groups % cores == core
         ).astype(out_ref.dtype)
         out_ref[pl.ds(pl.multiple_of((core ^ (deep >> 1)) * rows, rows), rows), :] = total
 
 
-def combine(place, parts, cores):
+def combine(place, parts, cores, groups):
     peers, rows, width = parts.shape
     vmem = pl.BlockSpec(memory_space=pltpu.VMEM)
     return pl.pallas_call(
-        functools.partial(combine_kernel, cores),
+        functools.partial(combine_kernel, cores, groups),
         in_specs=[pl.BlockSpec(memory_space=pltpu.SMEM), vmem],
         out_specs=vmem,
         out_shape=jax.ShapeDtypeStruct((cores * rows, width), jnp.bfloat16),
@@ -245,7 +264,7 @@
     meta = jnp.concatenate([own_meta, sibling(own_meta)])
     lists = plan(place, meta, database.shape[0] // tile, slots)
 
-    around = ("x", "yp", "zl")
+    around = ("yp", "zl", "x")
     peers = math.prod(lax.axis_size(axis) for axis in around)
     panel = spread(fetched, peers)
     panel, database = lax.optimization_barrier((panel, database))
@@ -254,10 +273,10 @@
 
     terms = align(lists, panels, database, other)
 
-    around = ("x", "yp", "zl", "c")
+    around = ("yp", "zl", "c", "x")
     peers = math.prod(lax.axis_size(axis) for axis in around)
     parts = lax.all_to_all(terms.reshape(peers, -1, width), around, 0, 0, tiled=True)
-    column = combine(place, parts, lax.axis_size("c"))
+    column = combine(place, parts, lax.axis_size("c"), lax.axis_size("x"))
     pieces = lax.all_to_all(column.reshape(-1, 4, width), ("zh", "yq"), 0, 0, tiled=True)
     return jnp.sum(pieces.astype(jnp.float32), axis=0).astype(jnp.bfloat16)
 

time: 137 us -> 136 us (level)
  blocking collectives: 66.2 us -> 62.4 us
  Pallas kernels: 16.9 us -> 18.5 us
    all_to_all x1, blocking collectives: 27.6 us -> 24.4 us  [on_device(): lax.all_to_all(column.reshape(-1, 4, width), ('zh', 'yq'), 0, 0, tiled=True)]
    pallas_call x1, Pallas kernels: 12.5 us -> 13.9 us  [align(): pl.pallas_call(functools.partial(align_kernel, width ** (-0.5)), in_specs...]
where the time goes in v9:
time: 136 us; the launch traced here: 135 us
  blocking collectives  62.4 us (46%)
  starting transfers between devices  25 us (18%)
  waiting for transfers between devices  24.9 us (18%)
  Pallas kernels  18.5 us (14%)
  local copies, waits for them, and re-layouts  2.95 us (2%)
    all_to_all x1, blocking collectives, on_device(): lax.all_to_all(terms.reshape(peers, -1, width), around, 0, 0, tiled=True)  38 us
    all_to_all x1, blocking collectives, on_device(): lax.all_to_all(column.reshape(-1, 4, width), ('zh', 'yq'), 0, 0, tiled=True)  24.4 us
    all_to_all x1, waiting for transfers between devices, on_device(): panels = lax.all_to_all(panel, around, 0, 0, tiled=True).reshape(-1, width)  21.3 us
    pallas_call x1, Pallas kernels, align(): pl.pallas_call(functools.partial(align_kernel, width ** (-0.5)), in_specs...  13.9 us
    ppermute x1, starting transfers between devices, on_device(): fetched = lax.ppermute(half, ('zh', 'zl', 'c'), route)  11.5 us
    all_to_all x1, starting transfers between devices, on_device(): panels = lax.all_to_all(panel, around, 0, 0, tiled=True).reshape(-1, width)  9.25 us
    ppermute x2, starting transfers between devices, sibling(): return lax.ppermute(value, 'c', [(0, 1), (1, 0)])  4.32 us
    ppermute x1, waiting for transfers between devices, on_device(): fetched = lax.ppermute(half, ('zh', 'zl', 'c'), route)  2.89 us
  transfers between devices with their start and end apart: 4, of which 3 were waited for; matrix products, arithmetic and copies ran while one was open for 0% of the time, Pallas kernels for 1%

profile of v9, /device:TPU:1, one launch (start us, length us, event | category | flops | bytes accessed | tf_op | source)
XLA Modules:
  0.0 135.3 jit_solution(6870183743338081331)
XLA Ops:
  0.0 0.0 copy-start
  0.0 1.0 copy-done
  1.0 11.5 %collective-permute-start.1 = (bf16[64,1280]{1,0:T(8,128)(2,1)S(1)}, bf16[64,1280]{1,0:T(8,128)(2,1)S(1)}, u32[]{:S(2)}, u32[]{:S(2)}) collective-permute-start(bf16[64,1280]{1,0:T(8,128)(2,1)S(1)} %bitcast.11), channel_id=1, source_target_pairs={{0,0},{65,1},{34,2},{99,3},{32,32},{97,33},{2,34},{67,35},{64,64},... | collective-permute-start | bytes 491528 | tf_op jit(solution)/shard_map/ppermute | solution.py:260
  12.5 2.9 %collective-permute-done.1.rows_ref = bf16[64,1280]{1,0:T(8,128)(2,1)S(1)} collective-permute-done((bf16[64,1280]{1,0:T(8,128)(2,1)S(1)}, bf16[64,1280]{1,0:T(8,128)(2,1)S(1)}, u32[]{:S(2)}, u32[]{:S(2)}) %collective-permute-start.1) | collective-permute-done | bytes 163872 | tf_op jit(solution)/shard_map/ppermute | solution.py:260
  15.4 1.9 %spread.1 = bf16[16,64,1280]{2,1,0:T(8,128)(2,1)} custom-call(bf16[64,1280]{1,0:T(8,128)(2,1)S(1)} %collective-permute-done.1.rows_ref), custom_call_target="tpu_custom_call" | custom-call | tf_op jit(solution)/shard_map/spread/pallas_call | solution.py:52
  17.2 0.0 copy-start.2
  17.2 0.0 copy-start.3
  17.2 9.2 %all-to-all-start = ((bf16[16,64,1280]{2,1,0:T(8,128)(2,1)}), bf16[16,64,1280]{2,1,0:T(8,128)(2,1)S(1)}, u32[]{:S(2)}, u32[]{:S(2)}) async-start(bf16[16,64,1280]{2,1,0:T(8,128)(2,1)} %spread.1), calls=%async_computation | async-start | bytes 5242880 | tf_op jit(solution)/shard_map/all_to_all | solution.py:272
  26.5 1.9 %collective-permute-start.2 = (bf16[768,1280]{1,0:T(8,128)(2,1)}, bf16[768,1280]{1,0:T(8,128)(2,1)}, u32[]{:S(2)}, u32[]{:S(2)}) collective-permute-start(bf16[768,1280]{1,0:T(8,128)(2,1)} %own_ref), channel_id=1, source_target_pairs={{0,1},{1,0},{2,3},{3,2},{4,5},{5,4},{6,7},{7,6},{8,9},{9,8},{10,11... | collective-permute-start | bytes 5898248 | tf_op jit(solution)/shard_map/ppermute | solution.py:241
  29.1 0.0 copy-done.2
  29.1 0.1 copy.9
  29.2 0.1 reshape.22
  29.3 0.0 copy-done.3
  29.3 0.1 copy.10
  29.4 0.1 reshape.23
  29.5 0.1 pad_add_fusion.2
  29.5 2.4 %collective-permute-start = (s32[128]{0:T(128)S(1)}, s32[128]{0:T(128)S(1)}, u32[]{:S(2)}, u32[]{:S(2)}) collective-permute-start(s32[128]{0:T(128)S(1)} %pad.4), channel_id=1, source_target_pairs={{0,1},{1,0},{2,3},{3,2},{4,5},{5,4},{6,7},{7,6},{8,9},{9,8},{10,11... | collective-permute-start | bytes 1544 | tf_op jit(solution)/shard_map/ppermute | solution.py:241
  32.0 0.1 pad_add_fusion.1.place
  32.0 0.7 collective-permute-done
  32.8 1.9 %plan.1.lists = s32[53]{0:T(128)S(1)} custom-call(s32[2]{0:T(128)S(1)} %pad_add_fusion.1.place, s32[256]{0:T(256)S(1)} %pad_add_fusion.meta), custom_call_target="tpu_custom_call" | custom-call | tf_op jit(solution)/shard_map/plan/pallas_call | solution.py:99
  34.7 0.0 collective-permute-done.2.other_ref
  34.7 21.3 %all-to-all-done = bf16[16,64,1280]{2,1,0:T(8,128)(2,1)S(1)} async-done(((bf16[16,64,1280]{2,1,0:T(8,128)(2,1)}), bf16[16,64,1280]{2,1,0:T(8,128)(2,1)S(1)}, u32[]{:S(2)}, u32[]{:S(2)}) %all-to-all-start) | async-done | bytes 2621472 | tf_op jit(solution)/shard_map/all_to_all | solution.py:272
  55.9 0.0 copy-start.1
  55.9 1.5 %copy-done.1 = bf16[768,1280]{1,0:T(8,128)(2,1)S(1)} copy-done((bf16[768,1280]{1,0:T(8,128)(2,1)S(1)}, bf16[768,1280]{1,0:T(8,128)(2,1)}, u32[]{:S(2)}) %copy-start.1) | copy-done | bytes 1966104
  57.5 13.9 %align.1 = bf16[1024,1280]{1,0:T(8,128)(2,1)S(1)} custom-call(s32[53]{0:T(128)S(1)} %plan.1.lists, bf16[1024,1280]{1,0:T(8,128)(2,1)S(1)} %bitcast.9, bf16[768,1280]{1,0:T(8,128)(2,1)S(1)} %copy-done.1, bf16[768,1280]{1,0:T(8,128)(2,1)} %collective-permute-done.2.other_ref), custom_call_target="tpu_custom_call" | custom-call | flops 8053063680 | tf_op jit(solution)/shard_map/align/pallas_call | solution.py:195
  71.4 38.0 %all_to_all.15.parts_ref = bf16[32,32,1280]{2,1,0:T(8,128)(2,1)S(1)} all-to-all(bf16[32,32,1280]{2,1,0:T(8,128)(2,1)S(1)} %bitcast.10), channel_id=1, replica_groups=mesh['x'=4,'zh'=4,'yq'=4,'yp'=2,'zl'=2,'c'=2] {'yp','zl','c','x'}, dimensions={0} | all-to-all | bytes 5242880 | tf_op jit(solution)/shard_map/all_to_all | solution.py:278
  109.3 0.9 combine.1
  110.3 24.4 %all_to_all.16 = bf16[16,4,1280]{2,1,0:T(4,128)(2,1)S(1)} all-to-all(bf16[16,4,1280]{2,1,0:T(4,128)(2,1)S(1)} %reshape.28), channel_id=1, replica_groups=mesh['x'=4,'zh'=4,'yq'=4,'yp'=2,'zl'=2,'c'=2] {'zh','yq'}, dimensions={0} | all-to-all | bytes 327680 | tf_op jit(solution)/shard_map/all_to_all | solution.py:280
  134.7 0.7 reduce_sum.12
  (4 shorter events, 0.1 us)
Async XLA Ops:
  0.0 1.0 copy-start
  1.0 14.4 %collective-permute-start.1 = (bf16[64,1280]{1,0:T(8,128)(2,1)S(1)}, bf16[64,1280]{1,0:T(8,128)(2,1)S(1)}, u32[]{:S(2)}, u32[]{:S(2)}) collective-permute-start(bf16[64,1280]{1,0:T(8,128)(2,1)S(1)} %bitcast.11), channel_id=1, source_target_pairs={{0,0},{65,1},{34,2},{99,3},{32,32},{97,33},{2,34},{67,35},{64,64},... | collective-permute-start | bytes 491528 | tf_op jit(solution)/shard_map/ppermute | solution.py:260
  17.2 11.9 %copy-start.2 = (s32[1,24,2]{1,2,0:T(2,128)S(1)}, s32[1,24,2]{1,2,0:T(2,128)}, u32[]{:S(2)}) copy-start(s32[1,24,2]{1,2,0:T(2,128)} %param.7) | copy-start | bytes 580
  17.2 12.0 %copy-start.3 = (s32[1,24,2]{1,2,0:T(2,128)S(1)}, s32[1,24,2]{1,2,0:T(2,128)}, u32[]{:S(2)}) copy-start(s32[1,24,2]{1,2,0:T(2,128)} %param.8) | copy-start | bytes 580
  17.2 38.7 %all-to-all-start = ((bf16[16,64,1280]{2,1,0:T(8,128)(2,1)}), bf16[16,64,1280]{2,1,0:T(8,128)(2,1)S(1)}, u32[]{:S(2)}, u32[]{:S(2)}) async-start(bf16[16,64,1280]{2,1,0:T(8,128)(2,1)} %spread.1), calls=%async_computation | async-start | bytes 5242880 | tf_op jit(solution)/shard_map/all_to_all | solution.py:272
  26.5 8.2 %collective-permute-start.2 = (bf16[768,1280]{1,0:T(8,128)(2,1)}, bf16[768,1280]{1,0:T(8,128)(2,1)}, u32[]{:S(2)}, u32[]{:S(2)}) collective-permute-start(bf16[768,1280]{1,0:T(8,128)(2,1)} %own_ref), channel_id=1, source_target_pairs={{0,1},{1,0},{2,3},{3,2},{4,5},{5,4},{6,7},{7,6},{8,9},{9,8},{10,11... | collective-permute-start | bytes 5898248 | tf_op jit(solution)/shard_map/ppermute | solution.py:241
  29.5 3.2 %collective-permute-start = (s32[128]{0:T(128)S(1)}, s32[128]{0:T(128)S(1)}, u32[]{:S(2)}, u32[]{:S(2)}) collective-permute-start(s32[128]{0:T(128)S(1)} %pad.4), channel_id=1, source_target_pairs={{0,1},{1,0},{2,3},{3,2},{4,5},{5,4},{6,7},{7,6},{8,9},{9,8},{10,11... | collective-permute-start | bytes 1544 | tf_op jit(solution)/shard_map/ppermute | solution.py:241
  55.9 1.5 %copy-start.1 = (bf16[768,1280]{1,0:T(8,128)(2,1)S(1)}, bf16[768,1280]{1,0:T(8,128)(2,1)}, u32[]{:S(2)}) copy-start(bf16[768,1280]{1,0:T(8,128)(2,1)} %own_ref) | copy-start | bytes 5898244

commit v10 on v8

--- a/solution.py
+++ b/solution.py
@@ -66,7 +66,9 @@
 def plan_kernel(tiles, slots, place, meta, lists):
     stride = meta.shape[0] // 2
     core, deep = place[0], place[1]
+    last = lists.shape[0] - 1
     lists[0] = 0
+    lists[last] = 0
     for side in range(2):
         base = side * stride
 
@@ -78,6 +80,9 @@
             def _():
                 count = lists[0] + 1
                 lists[0] = count
+                column = meta[base + 2 * slot + 1] + side * tiles
+                block = (query_tile >> 2) * tiles + (column >> 1)
+                lists[last] = lists[last] | jnp.left_shift(jnp.int32(1), block)
                 lists[count] = (
                     (query_tile & 1)
                     + 2 * (query_tile >> 2)
@@ -100,7 +105,7 @@
         functools.partial(plan_kernel, tiles, slots),
         in_specs=[smem, smem],
         out_specs=smem,
-        out_shape=jax.ShapeDtypeStruct((2 * slots + 1 + UNROLL,), jnp.int32),
+        out_shape=jax.ShapeDtypeStruct((2 * slots + 2 + UNROLL,), jnp.int32),
         compiler_params=pltpu.CompilerParams(vmem_limit_bytes=1024 * 1024),
         name="plan",
     )(place, meta)
@@ -114,14 +119,21 @@
     piece = TILE // pieces
 
     across = (((1,), (1,)), ((), ()))
-    for first in range(0, total, group):
-        weights[first : first + group, :] = jnp.zeros((group, 2 * width), weights.dtype)
-        query = q_ref[first : first + group, :]
-        for side, ref in enumerate((own_ref, other_ref)):
-            for at in range(0, width, CHUNK):
-                scores[first : first + group, side * width + at : side * width + at + CHUNK] = (
+    weights[...] = jnp.zeros_like(weights)
+    used = lists[lists.shape[0] - 1]
+    chunks = 2 * width // CHUNK
+    for index in range(total // group):
+        part = slice(index * group, (index + 1) * group)
+        for chunk in range(chunks):
+            ref = own_ref if chunk < chunks // 2 else other_ref
+            at = chunk % (chunks // 2) * CHUNK
+
+            @pl.when(((used >> (index * chunks + chunk)) & 1) == 1)
+            def _(part=part, chunk=chunk, ref=ref, at=at):
+                scores[part, chunk * CHUNK : (chunk + 1) * CHUNK] = (
                     lax.dot_general(
-                        query, ref[at : at + CHUNK, :], across, preferred_element_type=jnp.float32
+                        q_ref[part, :], ref[at : at + CHUNK, :], across,
+                        preferred_element_type=jnp.float32,
                     )
                     * scale
                 )

time: 137 us -> 138 us (level)
    all_to_all x1, blocking collectives: 38.6 us -> 41.7 us  [on_device(): lax.all_to_all(terms.reshape(peers, -1, width), around, 0, 0, tiled=True)]
    all_to_all x1, blocking collectives: 27.6 us -> 25.4 us  [on_device(): lax.all_to_all(column.reshape(-1, 4, width), ('zh', 'yq'), 0, 0, tiled=True)]
where the time goes in v10:
time: 138 us; the launch traced here: 137 us
  blocking collectives  67.1 us (49%)
  starting transfers between devices  25 us (18%)
  waiting for transfers between devices  23.9 us (17%)
  Pallas kernels  16.2 us (12%)
  local copies, waits for them, and re-layouts  2.95 us (2%)
    all_to_all x1, blocking collectives, on_device(): lax.all_to_all(terms.reshape(peers, -1, width), around, 0, 0, tiled=True)  41.7 us
    all_to_all x1, blocking collectives, on_device(): lax.all_to_all(column.reshape(-1, 4, width), ('zh', 'yq'), 0, 0, tiled=True)  25.4 us
    all_to_all x1, waiting for transfers between devices, on_device(): panels = lax.all_to_all(panel, around, 0, 0, tiled=True).reshape(-1, width)  20.3 us
    pallas_call x1, Pallas kernels, align(): pl.pallas_call(functools.partial(align_kernel, width ** (-0.5)), in_specs...  11.8 us
    ppermute x1, starting transfers between devices, on_device(): fetched = lax.ppermute(half, ('zh', 'zl', 'c'), route)  11.5 us
    all_to_all x1, starting transfers between devices, on_device(): panels = lax.all_to_all(panel, around, 0, 0, tiled=True).reshape(-1, width)  9.25 us
    ppermute x2, starting transfers between devices, sibling(): return lax.ppermute(value, 'c', [(0, 1), (1, 0)])  4.32 us
    ppermute x1, waiting for transfers between devices, on_device(): fetched = lax.ppermute(half, ('zh', 'zl', 'c'), route)  2.89 us
  transfers between devices with their start and end apart: 4, of which 3 were waited for; matrix products, arithmetic and copies ran while one was open for 0% of the time, Pallas kernels for 1%

profile of v10, /device:TPU:1, one launch (start us, length us, event | category | flops | bytes accessed | tf_op | source)
XLA Modules:
  0.0 136.8 jit_solution(741134017874019919)
XLA Ops:
  0.0 0.0 copy-start
  0.0 1.0 copy-done
  1.0 11.5 %collective-permute-start.1 = (bf16[64,1280]{1,0:T(8,128)(2,1)S(1)}, bf16[64,1280]{1,0:T(8,128)(2,1)S(1)}, u32[]{:S(2)}, u32[]{:S(2)}) collective-permute-start(bf16[64,1280]{1,0:T(8,128)(2,1)S(1)} %bitcast.11), channel_id=1, source_target_pairs={{0,0},{65,1},{34,2},{99,3},{32,32},{97,33},{2,34},{67,35},{64,64},... | collective-permute-start | bytes 491528 | tf_op jit(solution)/shard_map/ppermute | solution.py:253
  12.5 2.9 %collective-permute-done.1.rows_ref = bf16[64,1280]{1,0:T(8,128)(2,1)S(1)} collective-permute-done((bf16[64,1280]{1,0:T(8,128)(2,1)S(1)}, bf16[64,1280]{1,0:T(8,128)(2,1)S(1)}, u32[]{:S(2)}, u32[]{:S(2)}) %collective-permute-start.1) | collective-permute-done | bytes 163872 | tf_op jit(solution)/shard_map/ppermute | solution.py:253
  15.4 1.9 %spread.1 = bf16[16,64,1280]{2,1,0:T(8,128)(2,1)} custom-call(bf16[64,1280]{1,0:T(8,128)(2,1)S(1)} %collective-permute-done.1.rows_ref), custom_call_target="tpu_custom_call" | custom-call | tf_op jit(solution)/shard_map/spread/pallas_call | solution.py:52
  17.2 0.0 copy-start.2
  17.2 0.0 copy-start.3
  17.2 9.2 %all-to-all-start = ((bf16[16,64,1280]{2,1,0:T(8,128)(2,1)}), bf16[16,64,1280]{2,1,0:T(8,128)(2,1)S(1)}, u32[]{:S(2)}, u32[]{:S(2)}) async-start(bf16[16,64,1280]{2,1,0:T(8,128)(2,1)} %spread.1), calls=%async_computation | async-start | bytes 5242880 | tf_op jit(solution)/shard_map/all_to_all | solution.py:265
  26.5 1.9 %collective-permute-start.2 = (bf16[768,1280]{1,0:T(8,128)(2,1)}, bf16[768,1280]{1,0:T(8,128)(2,1)}, u32[]{:S(2)}, u32[]{:S(2)}) collective-permute-start(bf16[768,1280]{1,0:T(8,128)(2,1)} %own_ref), channel_id=1, source_target_pairs={{0,1},{1,0},{2,3},{3,2},{4,5},{5,4},{6,7},{7,6},{8,9},{9,8},{10,11... | collective-permute-start | bytes 5898248 | tf_op jit(solution)/shard_map/ppermute | solution.py:234
  29.1 0.0 copy-done.2
  29.1 0.1 copy.9
  29.2 0.1 reshape.22
  29.3 0.0 copy-done.3
  29.3 0.1 copy.10
  29.4 0.1 reshape.23
  29.5 0.1 pad_add_fusion.2
  29.5 2.4 %collective-permute-start = (s32[128]{0:T(128)S(1)}, s32[128]{0:T(128)S(1)}, u32[]{:S(2)}, u32[]{:S(2)}) collective-permute-start(s32[128]{0:T(128)S(1)} %pad.4), channel_id=1, source_target_pairs={{0,1},{1,0},{2,3},{3,2},{4,5},{5,4},{6,7},{7,6},{8,9},{9,8},{10,11... | collective-permute-start | bytes 1544 | tf_op jit(solution)/shard_map/ppermute | solution.py:234
  32.0 0.1 pad_add_fusion.1.place
  32.0 0.7 collective-permute-done
  32.8 1.7 %plan.1.lists = s32[54]{0:T(128)S(1)} custom-call(s32[2]{0:T(128)S(1)} %pad_add_fusion.1.place, s32[256]{0:T(256)S(1)} %pad_add_fusion.meta), custom_call_target="tpu_custom_call" | custom-call | tf_op jit(solution)/shard_map/plan/pallas_call | solution.py:104
  34.5 0.0 collective-permute-done.2.other_ref
  34.5 20.3 %all-to-all-done = bf16[16,64,1280]{2,1,0:T(8,128)(2,1)S(1)} async-done(((bf16[16,64,1280]{2,1,0:T(8,128)(2,1)}), bf16[16,64,1280]{2,1,0:T(8,128)(2,1)S(1)}, u32[]{:S(2)}, u32[]{:S(2)}) %all-to-all-start) | async-done | bytes 2621472 | tf_op jit(solution)/shard_map/all_to_all | solution.py:265
  54.9 0.0 copy-start.1
  54.9 1.5 %copy-done.1 = bf16[768,1280]{1,0:T(8,128)(2,1)S(1)} copy-done((bf16[768,1280]{1,0:T(8,128)(2,1)S(1)}, bf16[768,1280]{1,0:T(8,128)(2,1)}, u32[]{:S(2)}) %copy-start.1) | copy-done | bytes 1966104
  56.4 11.8 %align.1 = bf16[1024,1280]{1,0:T(8,128)(2,1)S(1)} custom-call(s32[54]{0:T(128)S(1)} %plan.1.lists, bf16[1024,1280]{1,0:T(8,128)(2,1)S(1)} %bitcast.9, bf16[768,1280]{1,0:T(8,128)(2,1)S(1)} %copy-done.1, bf16[768,1280]{1,0:T(8,128)(2,1)} %collective-permute-done.2.other_ref), custom_call_target="tpu_custom_call" | custom-call | flops 8053063680 | tf_op jit(solution)/shard_map/align/pallas_call | solution.py:190
  68.2 41.7 %all_to_all.15.parts_ref = bf16[32,32,1280]{2,1,0:T(8,128)(2,1)S(1)} all-to-all(bf16[32,32,1280]{2,1,0:T(8,128)(2,1)S(1)} %bitcast.10), channel_id=1, replica_groups=mesh['x'=4,'zh'=4,'yq'=4,'yp'=2,'zl'=2,'c'=2] {'x','yp','zl','c'}, dimensions={0} | all-to-all | bytes 5242880 | tf_op jit(solution)/shard_map/all_to_all | solution.py:271
  109.8 0.9 combine.1
  110.7 25.4 %all_to_all.16 = bf16[16,4,1280]{2,1,0:T(4,128)(2,1)S(1)} all-to-all(bf16[16,4,1280]{2,1,0:T(4,128)(2,1)S(1)} %reshape.28), channel_id=1, replica_groups=mesh['x'=4,'zh'=4,'yq'=4,'yp'=2,'zl'=2,'c'=2] {'zh','yq'}, dimensions={0} | all-to-all | bytes 327680 | tf_op jit(solution)/shard_map/all_to_all | solution.py:273
  136.1 0.7 reduce_sum.12
  (4 shorter events, 0.1 us)
Async XLA Ops:
  0.0 1.0 copy-start
  1.0 14.4 %collective-permute-start.1 = (bf16[64,1280]{1,0:T(8,128)(2,1)S(1)}, bf16[64,1280]{1,0:T(8,128)(2,1)S(1)}, u32[]{:S(2)}, u32[]{:S(2)}) collective-permute-start(bf16[64,1280]{1,0:T(8,128)(2,1)S(1)} %bitcast.11), channel_id=1, source_target_pairs={{0,0},{65,1},{34,2},{99,3},{32,32},{97,33},{2,34},{67,35},{64,64},... | collective-permute-start | bytes 491528 | tf_op jit(solution)/shard_map/ppermute | solution.py:253
  17.2 11.9 %copy-start.2 = (s32[1,24,2]{1,2,0:T(2,128)S(1)}, s32[1,24,2]{1,2,0:T(2,128)}, u32[]{:S(2)}) copy-start(s32[1,24,2]{1,2,0:T(2,128)} %param.7) | copy-start | bytes 580
  17.2 12.0 %copy-start.3 = (s32[1,24,2]{1,2,0:T(2,128)S(1)}, s32[1,24,2]{1,2,0:T(2,128)}, u32[]{:S(2)}) copy-start(s32[1,24,2]{1,2,0:T(2,128)} %param.8) | copy-start | bytes 580
  17.2 37.6 %all-to-all-start = ((bf16[16,64,1280]{2,1,0:T(8,128)(2,1)}), bf16[16,64,1280]{2,1,0:T(8,128)(2,1)S(1)}, u32[]{:S(2)}, u32[]{:S(2)}) async-start(bf16[16,64,1280]{2,1,0:T(8,128)(2,1)} %spread.1), calls=%async_computation | async-start | bytes 5242880 | tf_op jit(solution)/shard_map/all_to_all | solution.py:265
  26.5 8.0 %collective-permute-start.2 = (bf16[768,1280]{1,0:T(8,128)(2,1)}, bf16[768,1280]{1,0:T(8,128)(2,1)}, u32[]{:S(2)}, u32[]{:S(2)}) collective-permute-start(bf16[768,1280]{1,0:T(8,128)(2,1)} %own_ref), channel_id=1, source_target_pairs={{0,1},{1,0},{2,3},{3,2},{4,5},{5,4},{6,7},{7,6},{8,9},{9,8},{10,11... | collective-permute-start | bytes 5898248 | tf_op jit(solution)/shard_map/ppermute | solution.py:234
  29.5 3.2 %collective-permute-start = (s32[128]{0:T(128)S(1)}, s32[128]{0:T(128)S(1)}, u32[]{:S(2)}, u32[]{:S(2)}) collective-permute-start(s32[128]{0:T(128)S(1)} %pad.4), channel_id=1, source_target_pairs={{0,1},{1,0},{2,3},{3,2},{4,5},{5,4},{6,7},{7,6},{8,9},{9,8},{10,11... | collective-permute-start | bytes 1544 | tf_op jit(solution)/shard_map/ppermute | solution.py:234
  54.9 1.5 %copy-start.1 = (bf16[768,1280]{1,0:T(8,128)(2,1)S(1)}, bf16[768,1280]{1,0:T(8,128)(2,1)}, u32[]{:S(2)}) copy-start(bf16[768,1280]{1,0:T(8,128)(2,1)} %own_ref) | copy-start | bytes 5898244
